TPU v7x, 256 devices: a whole 4x4x8 slice. The times are simulated.
256 devices in a mesh: sec: 2 (over x_hi), dp: 16 (over z, core), vocab: 8 (over y, x_lo).
Axes of the slice: x: 4 (x_hi: 2, x_lo: 2; x = x_hi * 2 + x_lo), y: 4, z: 8, core: 2. Of those that a mesh axis runs over, the one named last changes fastest.
Arguments:
- hidden: bfloat16 [768, 5120], P('dp', ('sec', 'vocab')), may hold values from -12 to 12
- head: bfloat16 [5120, 147456], P('sec', ('dp', 'vocab')), may hold values from -1 to 1
- teacher_logits: bfloat16 [768, 147456], P(('sec', 'dp'), 'vocab'), may hold values from -16 to 300
- loss_mask: int32 [768], replicated, may hold values 0 or 1
- token_ids: int32 [768], replicated, may hold values from 0 to 147455
- row_order: int32 [768], replicated, may hold values from 0 to 767, each once
Outputs:
- head_grad: bfloat16 [5120, 147456], P('sec', ('dp', 'vocab'))
- hidden_grad: float32 [768, 5120], P('dp', ('sec', 'vocab'))
- token_kl: float32 [768], P(('sec', 'dp'))
- sampled_gap: float32 [768], P(('sec', 'dp'))
Inputs may be any that keep to these rules, and one draw needn't show every extreme that they name: `row_order`: a permutation of 0 to 767.
All inputs are finite; a program needn't handle non-finite values.
Results may differ from a plain program's by a relative error of at most 0.012.
Values may be sent and summed in bfloat16 or wider, within the bound.
No kernel may reach another device: no remote copies, remote signals or barrier semaphores. Data moves between devices by JAX's collectives and lax.ppermute only.
A program may use at most 128 MiB of HBM per device.

v0:
```python
import jax
import jax.numpy as jnp
from jax import lax
from jax.sharding import PartitionSpec as P


def on_device(hidden, head, teacher_logits, loss_mask, token_ids, row_order):
    dp_size = lax.axis_size("dp")
    vocab_size = lax.axis_size("vocab")
    sec_size = lax.axis_size("sec")
    block_width = head.shape[1]
    teacher_rows = teacher_logits.shape[0]
    tiles = teacher_logits.reshape(teacher_rows, dp_size // vocab_size, vocab_size, block_width)
    ordered = lax.all_to_all(
        lax.all_to_all(tiles, "vocab", split_axis=2, concat_axis=1, tiled=True),
        "dp",
        split_axis=1,
        concat_axis=0,
        tiled=True,
    )
    ordered = ordered.reshape(dp_size * teacher_rows, block_width)
    arrived = lax.all_gather(ordered, "sec", axis=0, tiled=True)
    inverse = jnp.argsort(row_order)
    teacher_full = jnp.take(arrived, inverse, axis=0)
    features = lax.all_gather(hidden, "vocab", axis=1, tiled=True)
    all_rows = lax.all_gather(features, "dp", axis=0, tiled=True)
    partial_value = jnp.dot(all_rows, head, preferred_element_type=jnp.float32)
    total_rows = all_rows.shape[0]
    logits = lax.psum(partial_value, "sec")
    teacher_block = teacher_full.astype(jnp.float32)
    offset = (lax.axis_index("dp") * vocab_size + lax.axis_index("vocab")) * block_width
    columns = offset + jnp.arange(block_width, dtype=jnp.int32)
    sampled_hit = columns[None, :] == token_ids[:, None]
    student_pick = jnp.sum(jnp.where(sampled_hit, logits, 0.0), axis=1)
    teacher_pick = jnp.sum(jnp.where(sampled_hit, teacher_block, 0.0), axis=1)
    local_student = jnp.max(logits, axis=1)
    local_teacher = jnp.max(teacher_block, axis=1)
    max_student, max_teacher = lax.pmax((local_student, local_teacher), ("dp", "vocab"))
    student_exp = jnp.exp(logits - max_student[:, None])
    teacher_exp = jnp.exp(teacher_block - max_teacher[:, None])
    sum_student, sum_teacher, cross_sum, student_pick, teacher_pick = lax.psum(
        (
            jnp.sum(student_exp, axis=1),
            jnp.sum(teacher_exp, axis=1),
            jnp.sum(student_exp * (logits - teacher_block), axis=1),
            student_pick,
            teacher_pick,
        ),
        ("dp", "vocab"),
    )
    student_lse = max_student + jnp.log(sum_student)
    teacher_lse = max_teacher + jnp.log(sum_teacher)
    token_kl = cross_sum / sum_student - student_lse + teacher_lse
    sampled_gap = student_pick - student_lse - (teacher_pick - teacher_lse)
    weights = loss_mask.astype(jnp.float32)
    log_student = logits - student_lse[:, None]
    log_teacher = teacher_block - teacher_lse[:, None]
    probs = jnp.exp(log_student)
    logit_grad = (
        weights[:, None] * probs * (log_student - log_teacher - token_kl[:, None])
    ).astype(jnp.bfloat16)
    head_grad = lax.dot_general(
        all_rows, logit_grad, (((0,), (0,)), ((), ())), preferred_element_type=jnp.float32
    ).astype(jnp.bfloat16)
    own_rows = lax.psum_scatter(
        lax.dot_general(
            logit_grad, head, (((1,), (1,)), ((), ())), preferred_element_type=jnp.float32
        ),
        "dp",
        scatter_dimension=0,
        tiled=True,
    )
    hidden_grad = lax.psum_scatter(own_rows, "vocab", scatter_dimension=1, tiled=True)
    row_share = total_rows // (sec_size * dp_size)
    owner = lax.axis_index("sec") * dp_size + lax.axis_index("dp")
    local_first = owner * row_share
    kl_rows = lax.dynamic_slice_in_dim(token_kl, local_first, row_share, 0)
    gap_rows = lax.dynamic_slice_in_dim(sampled_gap, local_first, row_share, 0)
    return (head_grad, hidden_grad, kl_rows, gap_rows)


def solution(mesh):
    in_specs = (
        P("dp", ("sec", "vocab")),
        P("sec", ("dp", "vocab")),
        P(("sec", "dp"), "vocab"),
        P(),
        P(),
        P(),
    )
    out_specs = (
        P("sec", ("dp", "vocab")),
        P("dp", ("sec", "vocab")),
        P(("sec", "dp")),
        P(("sec", "dp")),
    )
    return jax.shard_map(
        on_device, mesh=mesh, in_specs=in_specs, out_specs=out_specs, check_vma=False
    )
```

profile of v0, /device:TPU:10, one launch (start us, length us, event | category | flops | bytes accessed | tf_op | source)
XLA Modules:
  0.0 1214.4 jit_solution(7398706442351885761)
XLA Ops:
  7.2 27.3 %all-gather = bf16[8,320,48]{1,2,0:T(8,128)(2,1)S(1)} all-gather(bf16[1,320,48]{1,2,0:T(8,128)(2,1)} %bitcast.36), channel_id=1, replica_groups=mesh['sec'=2,'dp'=16,'vocab'=8] {'vocab'}, dimensions={0}, use_global_device_ids=true | all-gather | bytes 276480 | tf_op jit(solution)/shard_map/all_gather | solution.py:25
  34.5 0.1 copy.17
  34.6 0.9 reshape.43
  35.5 0.0 all-gather.6.cloned.1.call-start
  35.6 1.3 copy.24
  36.8 0.7 copy.18
  37.5 16.0 %all_to_all.33 = bf16[24,2,8,1152]{3,1,0,2:T(2,128)(2,1)S(1)} all-to-all(bf16[24,2,8,1152]{3,1,0,2:T(2,128)(2,1)S(1)} %copy.18), channel_id=1, replica_groups=mesh['sec'=2,'dp'=16,'vocab'=8] {'vocab'}, dimensions={2} | all-to-all | bytes 1769472 | tf_op jit(solution)/shard_map/all_to_all | solution.py:15
  53.5 0.1 copy.19
  53.6 41.0 %all_to_all.34 = bf16[24,16,1,1152]{3,0,2,1:T(8,128)(2,1)} all-to-all(bf16[24,16,1,1152]{3,0,2,1:T(8,128)(2,1)S(1)} %bitcast.31), channel_id=1, replica_groups=mesh['sec'=2,'dp'=16,'vocab'=8] {'dp'}, dimensions={1} | all-to-all | bytes 1769472 | tf_op jit(solution)/shard_map/all_to_all | solution.py:14
  94.6 1.8 all-gather.4.cloned.1.call-done
  96.4 9.9 fusion.16
  106.3 0.0 reduce-scatter.5.cloned.1.call-start
  106.4 0.6 copy-done
  107.0 4.4 sort.17
  111.4 23.0 %all-gather.6.cloned.1.call-done = bf16[768,1152]{1,0:T(8,128)(2,1)} async-done(((bf16[384,1152]{1,0:T(8,128)(2,1)}), bf16[768,1152]{1,0:T(8,128)(2,1)}) %all-gather.6.cloned.1.call-update) | async-done | bytes 1769488 | tf_op jit(solution)/shard_map/all_gather | solution.py:22
  134.5 5.9 gather_fusion
  140.4 0.6 fusion.12
  141.0 103.8 %all-reduce.4.cloned.1.call-done = f32[768,1152]{1,0:T(8,128)} async-done(((f32[768,1152]{1,0:T(8,128)}), f32[768,1152]{1,0:T(8,128)}) %all-reduce.4.cloned.1.call-update) | async-done | bytes 3538960 | tf_op jit(solution)/shard_map/psum | solution.py:29
  244.7 2.2 reduce_max.23
  247.0 278.9 %all-reduce.1 = (f32[768]{0:T(1024)S(1)}, f32[768]{0:T(1024)S(1)}) all-reduce(bf16[768]{0:T(1024)(128)(2,1)S(1)} %fusion.12, f32[768]{0:T(1024)S(1)} %reduce_max.23), channel_id=1, replica_groups=mesh['sec'=2,'dp'=16,'vocab'=8] {'dp','vocab'}, use_global_device_ids=true, to_apply=%region_7.8 | all-reduce | flops 1536 | bytes 10752 | tf_op jit(solution)/shard_map/pmax | solution.py:38
  525.9 4.5 fusion.9
  530.4 550.4 %all-reduce = (f32[768]{0:T(1024)S(1)}, f32[768]{0:T(1024)S(1)}, f32[768]{0:T(1024)S(1)}, f32[768]{0:T(1024)S(1)}, f32[768]{0:T(1024)S(1)}) all-reduce(f32[768]{0:T(1024)S(1)} %get-tuple-element.26, f32[768]{0:T(1024)S(1)} %get-tuple-element.23, ...), channel_id=1, replica_groups=mesh['sec'=2,'dp'=16,'vocab'=8] {'dp','vocab'}, use_global_device_ids=true, to_apply=%region_9.10 | all-reduce | flops 3840 | bytes 30720 | tf_op jit(solution)/shard_map/psum | solution.py:41
  1080.9 11.8 fusion.13
  1092.7 0.2 reduce-scatter.7.cloned.1.call-start
  1092.9 71.0 %reduce-scatter.5.cloned.1.call-done = f32[48,2560]{1,0:T(8,128)} async-done(((f32[768,2560]{1,0:T(8,128)}), f32[48,2560]{1,0:T(8,128)}) %reduce-scatter.5.cloned.1.call-update) | async-done | bytes 491536 | tf_op jit(solution)/shard_map/reduce_scatter | solution.py:65
  1163.9 2.5 copy.22
  1166.5 11.2 fusion
  1177.7 8.8 copy.21
  1186.5 0.6 dynamic_slice.6
  1187.1 0.6 dynamic_slice.7
  1187.7 18.5 %reduce-scatter.7.cloned.1.call-done = f32[320,48]{1,0:T(8,128)} async-done(((f32[2560,48]{1,0:T(8,128)}), f32[320,48]{1,0:T(8,128)}) %reduce-scatter.7.cloned.1.call-update) | async-done | bytes 61456
  1206.2 1.7 copy.23
  (20 shorter events, 0.2 us)
Async XLA Ops:
  7.2 89.3 %all-gather.4.cloned.1.call-start = ((), (), s32[]{:S(2)}) async-start(), calls=%async_computation.4 | async-start | bytes 4177920 | tf_op jit(solution)/shard_map/all_gather | solution.py:26
  35.5 99.0 %all-gather.6.cloned.1.call-start = ((), (), s32[]{:S(2)}) async-start(), calls=%async_computation.6 | async-start | bytes 2654208 | tf_op jit(solution)/shard_map/all_gather | solution.py:22
  94.6 150.1 %all-reduce.4.cloned.1.call-start = ((), (), s32[]{:S(2)}) async-start(), calls=%async_computation.5 | async-start | bytes 7077888 | tf_op jit(solution)/shard_map/psum | solution.py:29
  106.3 0.7 copy-start
  106.3 0.7 copy-start.1
  106.3 1057.6 %reduce-scatter.5.cloned.1.call-start = ((), (), s32[]{:S(2)}) async-start(), calls=%async_computation.7 | async-start | bytes 8355840 | tf_op jit(solution)/shard_map/reduce_scatter | solution.py:65
  140.4 385.6 %copy-start.2 = (s32[768]{0:T(1024)S(1)}, s32[768]{0:T(1024)}, u32[]{:S(2)}) copy-start(s32[768]{0:T(1024)} %param.10) | copy-start | bytes 9220
  1092.7 113.5 %reduce-scatter.7.cloned.1.call-start = ((), (), s32[]{:S(2)}) async-start(), calls=%async_computation.8 | async-start | bytes 1474560
Sparse Core Ops, SparseCore 0:
  35.6 60.7 all-gather.3
  98.2 36.1 all-gather.5
  137.6 107.0 all-reduce.3
  1092.8 71.0 reduce-scatter.4
  1166.6 39.5 reduce-scatter.6
where the time goes:
time: 1220 us; the launch traced here: 1210 us
  blocking collectives  914 us (75%)
  waiting for transfers between devices  218 us (18%)
  matrix products  32.9 us (3%)
  local copies, waits for them, and re-layouts  23.7 us (2%)
  between operations  13.9 us (1%)
    psum x1, blocking collectives, on_device(): lax.psum((jnp.sum(student_exp, axis=1), jnp.sum(teacher_exp, axis=1), jnp...  550 us
    pmax x1, blocking collectives, on_device(): lax.pmax((local_student, local_teacher), ('dp', 'vocab'))  279 us
    psum x1, waiting for transfers between devices, on_device(): logits = lax.psum(partial_value, 'sec')  104 us
    reduce_scatter x1, waiting for transfers between devices, on_device(): lax.psum_scatter(lax.dot_general(logit_grad, head, (((1,), (1,)), ((), ()...  71 us
    all_to_all x1, blocking collectives, on_device(): lax.all_to_all(lax.all_to_all(tiles, 'vocab', split_axis=2, concat_axis=1...  41 us
    all_gather x1, blocking collectives, on_device(): features = lax.all_gather(hidden, 'vocab', axis=1, tiled=True)  27.3 us
  transfers between devices with their start and end apart: 5, of which 5 were waited for; matrix products, arithmetic and copies ran while one was open for 4% of the time, Pallas kernels for 0%

commit v1 on v0

v1 whole, which is shorter than its diff:
```python
import jax
import jax.numpy as jnp
from jax import lax
from jax.sharding import PartitionSpec as P

F32 = jnp.float32
BF16 = jnp.bfloat16
NT = (((1,), (1,)), ((), ()))


def merge_stats(table):
    max_s = jnp.max(table[:, 0], axis=0)
    max_t = jnp.max(table[:, 3], axis=0)
    scale_s = jnp.exp(table[:, 0] - max_s[None])
    scale_t = jnp.exp(table[:, 3] - max_t[None])
    return jnp.stack(
        [
            max_s,
            jnp.sum(table[:, 1] * scale_s, axis=0),
            jnp.sum(table[:, 2] * scale_s, axis=0),
            max_t,
            jnp.sum(table[:, 4] * scale_t, axis=0),
            jnp.sum(table[:, 5], axis=0),
            jnp.sum(table[:, 6], axis=0),
        ]
    )


def share(value, axis):
    count = lax.axis_size(axis)
    copies = jnp.broadcast_to(value[None], (count,) + value.shape)
    return lax.all_to_all(copies, axis, split_axis=0, concat_axis=0, tiled=True)


def on_device(hidden, head, teacher_logits, loss_mask, token_ids, row_order):
    dp_size = lax.axis_size("dp")
    vocab_size = lax.axis_size("vocab")
    z_size = dp_size // 2
    sec = lax.axis_index("sec")
    dp = lax.axis_index("dp")
    z, core = dp // 2, dp % 2
    block_width = head.shape[1]
    rows = hidden.shape[0]
    width = hidden.shape[1]
    total_rows = rows * dp_size
    half = total_rows // 2
    teacher_rows = teacher_logits.shape[0]
    swap_sec = [(0, 1), (1, 0)]
    swap_core = [(i, i ^ 1) for i in range(dp_size)]
    z_up = [(i, (i + 2) % dp_size) for i in range(dp_size)]
    z_down = [(i, (i - 2) % dp_size) for i in range(dp_size)]

    features = share(hidden, "vocab").transpose(1, 0, 2).reshape(rows, vocab_size * width)
    all_rows = lax.all_gather(features, "dp", axis=0, tiled=True)

    tiles = teacher_logits.reshape(teacher_rows, dp_size // vocab_size, vocab_size, block_width)
    ordered = lax.all_to_all(
        lax.all_to_all(tiles, "vocab", split_axis=2, concat_axis=1, tiled=True),
        "dp",
        split_axis=1,
        concat_axis=0,
        tiled=True,
    ).reshape(half, block_width)
    arrived = lax.ppermute(ordered, "sec", swap_sec)
    first = sec * half
    my_tokens = first + jnp.arange(half, dtype=jnp.int32)

    def aligned(part, owner):
        order = lax.dynamic_slice_in_dim(row_order, owner * half, half, 0)
        chosen = (order[None, :] == my_tokens[:, None]).astype(BF16)
        return jnp.dot(chosen, part, preferred_element_type=F32)

    teacher_block = aligned(ordered, sec) + aligned(arrived, 1 - sec)

    theirs = lax.dynamic_slice_in_dim(all_rows, (1 - sec) * half, half, 0)
    mine = lax.dynamic_slice_in_dim(all_rows, first, half, 0)
    quarter = half // 2
    sent = [
        lax.ppermute(
            jnp.dot(theirs[i * quarter : (i + 1) * quarter], head, preferred_element_type=F32),
            "sec",
            swap_sec,
        )
        for i in range(2)
    ]
    own = jnp.dot(mine, head, preferred_element_type=F32)
    logits = own + jnp.concatenate(sent, axis=0)

    ids = lax.dynamic_slice_in_dim(token_ids, first, half, 0)
    offset = (dp * vocab_size + lax.axis_index("vocab")) * block_width
    columns = offset + jnp.arange(block_width, dtype=jnp.int32)
    hit = columns[None, :] == ids[:, None]
    top_s = jnp.max(logits, axis=1)
    top_t = jnp.max(teacher_block, axis=1)
    exp_s = jnp.exp(logits - top_s[:, None])
    exp_t = jnp.exp(teacher_block - top_t[:, None])
    local = jnp.stack(
        [
            top_s,
            jnp.sum(exp_s, axis=1),
            jnp.sum(exp_s * (logits - teacher_block), axis=1),
            top_t,
            jnp.sum(exp_t, axis=1),
            jnp.sum(jnp.where(hit, logits, 0.0), axis=1),
            jnp.sum(jnp.where(hit, teacher_block, 0.0), axis=1),
        ]
    )
    stats = merge_stats(share(merge_stats(share(local, "dp")), "vocab"))
    student_lse = stats[0] + jnp.log(stats[1])
    teacher_lse = stats[3] + jnp.log(stats[4])
    token_kl = stats[2] / stats[1] - student_lse + teacher_lse
    sampled_gap = stats[5] - student_lse - (stats[6] - teacher_lse)

    weights = lax.dynamic_slice_in_dim(loss_mask, first, half, 0).astype(F32)
    log_student = logits - student_lse[:, None]
    log_teacher = teacher_block - teacher_lse[:, None]
    my_grad = (
        weights[:, None] * jnp.exp(log_student) * (log_student - log_teacher - token_kl[:, None])
    ).astype(BF16)
    their_grad = lax.ppermute(my_grad, "sec", swap_sec)
    logit_grad = lax.dynamic_update_slice_in_dim(
        jnp.concatenate([their_grad, their_grad], axis=0), my_grad, first, 0
    )

    around = (z + jnp.arange(z_size)) % z_size
    by_chip = jnp.take(logit_grad.reshape(z_size, 2, rows, block_width), around, axis=0)

    def hidden_terms(which):
        part = lax.dynamic_index_in_dim(by_chip, which, 1, keepdims=False)
        return lax.dot_general(
            part.reshape(half, block_width), head, NT, preferred_element_type=F32
        )

    other_core = lax.ppermute(hidden_terms(1 - core).astype(BF16), "dp", swap_core)
    terms = (hidden_terms(core) + other_core.astype(F32)).reshape(z_size, rows, -1)
    cut = rows // 2
    far = z_size // 2
    up = lax.ppermute(terms[far, :cut].astype(BF16), "dp", z_up)
    down = lax.ppermute(terms[far, cut:].astype(BF16), "dp", z_down)
    for step in range(far - 1, 0, -1):
        ahead, behind = terms[step], terms[z_size - step]
        if step == far - 1:
            ahead = jnp.concatenate([ahead[:cut] + up.astype(F32), ahead[cut:]], axis=0)
            behind = jnp.concatenate([behind[:cut], behind[cut:] + down.astype(F32)], axis=0)
        else:
            ahead = ahead + up.astype(F32)
            behind = behind + down.astype(F32)
        up = lax.ppermute(ahead.astype(BF16), "dp", z_up)
        down = lax.ppermute(behind.astype(BF16), "dp", z_down)
    row_terms = terms[0] + up.astype(F32) + down.astype(F32)
    parts = row_terms.reshape(rows, vocab_size, width).transpose(1, 0, 2).astype(BF16)
    parts = lax.all_to_all(parts, "vocab", split_axis=0, concat_axis=0, tiled=True)
    hidden_grad = jnp.sum(parts.astype(F32), axis=0)

    turned = lax.optimization_barrier(all_rows.T)
    head_grad = jnp.dot(turned, logit_grad, preferred_element_type=F32).astype(BF16)

    share_rows = half // dp_size
    kl_rows = lax.dynamic_slice_in_dim(token_kl, dp * share_rows, share_rows, 0)
    gap_rows = lax.dynamic_slice_in_dim(sampled_gap, dp * share_rows, share_rows, 0)
    return (head_grad, hidden_grad, kl_rows, gap_rows)


def solution(mesh):
    in_specs = (
        P("dp", ("sec", "vocab")),
        P("sec", ("dp", "vocab")),
        P(("sec", "dp"), "vocab"),
        P(),
        P(),
        P(),
    )
    out_specs = (
        P("sec", ("dp", "vocab")),
        P("dp", ("sec", "vocab")),
        P(("sec", "dp")),
        P(("sec", "dp")),
    )
    return jax.shard_map(
        on_device, mesh=mesh, in_specs=in_specs, out_specs=out_specs, check_vma=False
    )
```

time: 1220 us -> 288 us (0.24)
  blocking collectives: 914 us -> 41.2 us
  waiting for transfers between devices: 218 us -> 124 us
  starting transfers between devices: 0.39 us -> 37.8 us
    psum x1 -> x0, blocking collectives: 550 us -> none  [on_device(): lax.psum((jnp.sum(student_exp, axis=1), jnp.sum(teacher_exp, axis=1), jnp...]
    pmax x1 -> x0, blocking collectives: 279 us -> none  [on_device(): lax.pmax((local_student, local_teacher), ('dp', 'vocab'))]
    psum x1 -> x0, waiting for transfers between devices: 104 us -> none  [on_device(): logits = lax.psum(partial_value, 'sec')]
    ppermute x0 -> x13, waiting for transfers between devices: none -> 88.6 us  [the longest x2 36.8 us: on_device(): lax.ppermute(jnp.dot(theirs[i * quarter:(i + 1) * quarter], head, preferr...]
    reduce_scatter x1 -> x0, waiting for transfers between devices: 71 us -> none  [on_device(): lax.psum_scatter(lax.dot_general(logit_grad, head, (((1,), (1,)), ((), ()...]
    all_to_all x0 -> x3, waiting for transfers between devices: none -> 34.6 us  [the longest x1 30.9 us: on_device(): lax.all_to_all(lax.all_to_all(tiles, 'vocab', split_axis=2, concat_axis=1...]
    all_gather x1 -> x0, blocking collectives: 27.3 us -> none  [on_device(): features = lax.all_gather(hidden, 'vocab', axis=1, tiled=True)]
    all_gather x1 -> x0, waiting for transfers between devices: 23 us -> none  [on_device(): arrived = lax.all_gather(ordered, 'sec', axis=0, tiled=True)]
  transfers between devices with their start and end apart: 5 -> 17, of which waited for: 5 -> 15; matrix products, arithmetic and copies ran while one was open for 4% -> 12% of each run, Pallas kernels for 0% -> 0%
where the time goes in v1:
time: 288 us; the launch traced here: 286 us
  waiting for transfers between devices  124 us (43%)
  blocking collectives  41.2 us (14%)
  starting transfers between devices  37.8 us (13%)
  matrix products  35 us (12%)
  local copies, waits for them, and re-layouts  26.3 us (9%)
  between operations  14.3 us (5%)
  other arithmetic  7.77 us (3%)
    ppermute x2, waiting for transfers between devices, on_device(): lax.ppermute(jnp.dot(theirs[i * quarter:(i + 1) * quarter], head, preferr...  36.8 us
    all_to_all x1, waiting for transfers between devices, on_device(): lax.all_to_all(lax.all_to_all(tiles, 'vocab', split_axis=2, concat_axis=1...  30.9 us
    all_to_all x2, blocking collectives, share(): return lax.all_to_all(copies, axis, split_axis=0, concat_axis=0, tiled=True)  25.7 us
    ppermute x1, waiting for transfers between devices, on_device(): their_grad = lax.ppermute(my_grad, 'sec', swap_sec)  20.8 us
    all_to_all x1, blocking collectives, on_device(): lax.all_to_all(tiles, 'vocab', split_axis=2, concat_axis=1, tiled=True)  15.4 us
    ppermute x3, waiting for transfers between devices, on_device(): down = lax.ppermute(behind.astype(BF16), 'dp', z_down)  11.4 us
    dot_general x2, matrix products, on_device(): jnp.dot(theirs[i * quarter:(i + 1) * quarter], head, preferred_element_ty...  10.7 us
    unnamed x16, local copies, waits for them, and re-layouts  8.91 us
  transfers between devices with their start and end apart: 17, of which 15 were waited for; matrix products, arithmetic and copies ran while one was open for 12% of the time, Pallas kernels for 0%

profile of v1, /device:TPU:10, one launch (start us, length us, event | category | flops | bytes accessed | tf_op | source)
XLA Modules:
  0.0 286.4 jit_solution(13552494084344873807)
XLA Ops:
  8.1 11.2 %all_to_all.53 = bf16[8,48,320]{2,1,0:T(8,128)(2,1)S(1)} all-to-all(bf16[8,48,320]{2,1,0:T(8,128)(2,1)S(1)} %broadcast_in_dim.18), channel_id=1, replica_groups=mesh['sec'=2,'dp'=16,'vocab'=8] {'vocab'}, dimensions={0} | all-to-all | bytes 491520 | tf_op jit(solution)/shard_map/all_to_all | solution.py:32
  21.1 15.4 %all_to_all.54 = bf16[24,2,8,1152]{3,1,0,2:T(2,128)(2,1)S(1)} all-to-all(bf16[24,2,8,1152]{3,1,0,2:T(2,128)(2,1)S(1)} %copy.59), channel_id=1, replica_groups=mesh['sec'=2,'dp'=16,'vocab'=8] {'vocab'}, dimensions={2} | all-to-all | bytes 1769472 | tf_op jit(solution)/shard_map/all_to_all | solution.py:58
  37.5 8.6 %all-to-all-start.2 = ((bf16[24,16,1,1152]{3,0,2,1:T(8,128)(2,1)}), bf16[24,16,1,1152]{3,0,2,1:T(8,128)(2,1)S(1)}, u32[]{:S(2)}, u32[]{:S(2)}) async-start(bf16[24,16,1,1152]{3,0,2,1:T(8,128)(2,1)} %bitcast.4), calls=%async_computation.2 | async-start | bytes 1769472 | tf_op jit(solution)/shard_map/all_to_all | solution.py:57
  46.1 30.9 %all-to-all-done.2 = bf16[24,16,1,1152]{3,0,2,1:T(8,128)(2,1)S(1)} async-done(((bf16[24,16,1,1152]{3,0,2,1:T(8,128)(2,1)}), bf16[24,16,1,1152]{3,0,2,1:T(8,128)(2,1)S(1)}, u32[]{:S(2)}, u32[]{:S(2)}) %all-to-all-start.2) | async-done | bytes 884768 | tf_op jit(solution)/shard_map/all_to_all | solution.py:57
  77.2 2.3 collective-permute-start.2
  80.2 5.4 %fusion.6 = f32[192,1152]{1,0:T(8,128)} fusion(bf16[2560,1152]{1,0:T(8,128)(2,1)} %param.7, bf16[768,2560]{1,0:T(8,128)(2,1)} %all-gather.2.cloned.1.call-done, s32[]{:T(128)S(6)} %add.195), kind=kOutput, calls=%fused_computation.20 | convolution fusion | flops 1132462080 | bytes 7766020 | tf_op jit(solution)/shard_map/dot_general | solution.py:80
  85.6 2.1 collective-permute-start.1
  87.7 5.4 %fusion.8 = f32[192,1152]{1,0:T(8,128)} fusion(bf16[2560,1152]{1,0:T(8,128)(2,1)} %param.7, bf16[768,2560]{1,0:T(8,128)(2,1)} %all-gather.2.cloned.1.call-done, s32[]{:T(128)S(6)} %select_n.78), kind=kOutput, calls=%fused_computation.22 | convolution fusion | flops 1132462080 | bytes 7766020 | tf_op jit(solution)/shard_map/dot_general | solution.py:80
  95.3 5.9 %collective-permute-done.2 = bf16[384,1152]{1,0:T(8,128)(2,1)S(1)} collective-permute-done((bf16[384,1152]{1,0:T(8,128)(2,1)S(1)}, bf16[384,1152]{1,0:T(8,128)(2,1)S(1)}, u32[]{:S(2)}, u32[]{:S(2)}) %collective-permute-start.2) | collective-permute-done | bytes 884768 | tf_op jit(solution)/shard_map/ppermute | solution.py:64
  102.1 18.3 %collective-permute-done.1 = f32[192,1152]{1,0:T(8,128)} collective-permute-done((f32[192,1152]{1,0:T(8,128)}, f32[192,1152]{1,0:T(8,128)}, u32[]{:S(2)}, u32[]{:S(2)}) %collective-permute-start.1) | collective-permute-done | bytes 884768 | tf_op jit(solution)/shard_map/ppermute | solution.py:79
  120.3 18.5 %collective-permute-done = f32[192,1152]{1,0:T(8,128)} collective-permute-done((f32[192,1152]{1,0:T(8,128)}, f32[192,1152]{1,0:T(8,128)}, u32[]{:S(2)}, u32[]{:S(2)}) %collective-permute-start) | collective-permute-done | bytes 884768 | tf_op jit(solution)/shard_map/ppermute | solution.py:79
  138.9 5.9 %fusion.56 = (f32[384]{0:T(512)S(1)}, f32[384,1152]{1,0:T(8,128)S(1)}) fusion(f32[192,1152]{1,0:T(8,128)} %collective-permute-done.1, f32[192,1152]{1,0:T(8,128)} %collective-permute-done, bf16[2560,1152]{1,0:T(8,128)(2,1)} %param.7, bf16[768,2560]{1,0:T(8,128)(2,1)S(1)} %copy-done.4, s32[]{:T(128)S(6)} %select_n.77), kind=kOutput, calls=%fused_computation.118 | convolution fusion | flops 2266250752 | bytes 11404804 | tf_op jit(solution)/shard_map/dot_general | solution.py:86
  150.4 14.6 %all_to_all.55 = f32[16,7,384]{2,1,0:T(8,128)S(1)} all-to-all(f32[16,7,384]{2,1,0:T(8,128)S(1)} %broadcast_in_dim.20), channel_id=1, replica_groups=mesh['sec'=2,'dp'=16,'vocab'=8] {'dp'}, dimensions={0} | all-to-all | bytes 344064 | tf_op jit(solution)/shard_map/all_to_all | solution.py:32
  170.0 5.1 %all-to-all-start.4 = ((f32[8,7,384]{2,1,0:T(8,128)}), f32[8,7,384]{2,1,0:T(8,128)}, u32[]{:S(2)}, u32[]{:S(2)}) async-start(f32[8,7,384]{2,1,0:T(8,128)} %broadcast_in_dim.21), calls=%async_computation.4 | async-start | bytes 196608 | tf_op jit(solution)/shard_map/all_to_all | solution.py:32
  175.8 3.7 %all-to-all-done.4 = f32[8,7,384]{2,1,0:T(8,128)} async-done(((f32[8,7,384]{2,1,0:T(8,128)}), f32[8,7,384]{2,1,0:T(8,128)}, u32[]{:S(2)}, u32[]{:S(2)}) %all-to-all-start.4) | async-done | bytes 86048 | tf_op jit(solution)/shard_map/all_to_all | solution.py:32
  182.5 2.2 collective-permute-start.3
  184.8 20.8 %collective-permute-done.3 = bf16[384,1152]{1,0:T(8,128)(2,1)S(1)} collective-permute-done((bf16[384,1152]{1,0:T(8,128)(2,1)}, bf16[384,1152]{1,0:T(8,128)(2,1)S(1)}, u32[]{:S(2)}, u32[]{:S(2)}) %collective-permute-start.3) | collective-permute-done | bytes 884768 | tf_op jit(solution)/shard_map/ppermute | solution.py:120
  208.2 5.6 %convolution_convert_fusion.1 = bf16[384,2560]{1,0:T(8,128)(2,1)S(1)} fusion(bf16[384,1152]{1,0:T(8,128)(2,1)S(1)} %bitcast.116, bf16[2560,1152]{1,0:T(8,128)(2,1)} %param.7), kind=kOutput, calls=%fused_computation.3 | convolution fusion | flops 2265907200 | bytes 8749056 | tf_op jit(solution)/shard_map/dot_general | solution.py:130
  213.9 4.0 %collective-permute-done.4 = bf16[384,2560]{1,0:T(8,128)(2,1)S(1)} collective-permute-done((bf16[384,2560]{1,0:T(8,128)(2,1)S(1)}, bf16[384,2560]{1,0:T(8,128)(2,1)S(1)}, u32[]{:S(2)}, u32[]{:S(2)}) %collective-permute-start.4) | collective-permute-done | bytes 1966112 | tf_op jit(solution)/shard_map/ppermute | solution.py:134
  217.9 2.7 fusion.51
  220.8 3.2 %collective-permute-start.9 = (bf16[24,2560]{1,0:T(8,128)(2,1)S(1)}, bf16[24,2560]{1,0:T(8,128)(2,1)S(1)}, u32[]{:S(2)}, u32[]{:S(2)}) collective-permute-start(bf16[24,2560]{1,0:T(8,128)(2,1)S(1)} %get-tuple-element.59), channel_id=1, source_target_pairs={{0,112},{8,120},{16,0},{24,8},{32,16},{40,24},{48,32},{56,40},{64,... | collective-permute-start | bytes 368648 | tf_op jit(solution)/shard_map/ppermute | solution.py:139
  224.0 3.3 %collective-permute-done.5 = bf16[24,2560]{1,0:T(8,128)(2,1)S(1)} collective-permute-done((bf16[24,2560]{1,0:T(8,128)(2,1)S(1)}, bf16[24,2560]{1,0:T(8,128)(2,1)S(1)}, u32[]{:S(2)}, u32[]{:S(2)}) %collective-permute-start.5) | collective-permute-done | bytes 122912 | tf_op jit(solution)/shard_map/ppermute | solution.py:138
  227.4 3.0 %collective-permute-start.10 = (bf16[48,2560]{1,0:T(8,128)(2,1)S(1)}, bf16[48,2560]{1,0:T(8,128)(2,1)S(1)}, u32[]{:S(2)}, u32[]{:S(2)}) collective-permute-start(bf16[48,2560]{1,0:T(8,128)(2,1)S(1)} %pad_maximum_fusion.2), channel_id=1, source_target_pairs={{0,112},{8,120},{16,0},{24,8},{32,16},{40,24},{48,32},{56,40},{64,... | collective-permute-start | bytes 737288 | tf_op jit(solution)/shard_map/ppermute | solution.py:149
  230.5 4.3 %collective-permute-done.10 = bf16[48,2560]{1,0:T(8,128)(2,1)S(1)} collective-permute-done((bf16[48,2560]{1,0:T(8,128)(2,1)S(1)}, bf16[48,2560]{1,0:T(8,128)(2,1)S(1)}, u32[]{:S(2)}, u32[]{:S(2)}) %collective-permute-start.10) | collective-permute-done | bytes 245792 | tf_op jit(solution)/shard_map/ppermute | solution.py:149
  234.8 3.5 %collective-permute-done.6 = bf16[48,2560]{1,0:T(8,128)(2,1)S(1)} collective-permute-done((bf16[48,2560]{1,0:T(8,128)(2,1)S(1)}, bf16[48,2560]{1,0:T(8,128)(2,1)S(1)}, u32[]{:S(2)}, u32[]{:S(2)}) %collective-permute-start.6) | collective-permute-done | bytes 245792 | tf_op jit(solution)/shard_map/ppermute | solution.py:148
  238.7 1.8 collective-permute-start.7
  240.5 4.2 %collective-permute-done.11 = bf16[48,2560]{1,0:T(8,128)(2,1)S(1)} collective-permute-done((bf16[48,2560]{1,0:T(8,128)(2,1)S(1)}, bf16[48,2560]{1,0:T(8,128)(2,1)S(1)}, u32[]{:S(2)}, u32[]{:S(2)}) %collective-permute-start.11) | collective-permute-done | bytes 245792 | tf_op jit(solution)/shard_map/ppermute | solution.py:149
  246.3 2.0 collective-permute-start.8
  249.5 3.0 %collective-permute-done.12 = bf16[48,2560]{1,0:T(8,128)(2,1)S(1)} collective-permute-done((bf16[48,2560]{1,0:T(8,128)(2,1)S(1)}, bf16[48,2560]{1,0:T(8,128)(2,1)S(1)}, u32[]{:S(2)}, u32[]{:S(2)}) %collective-permute-start.12) | collective-permute-done | bytes 245792 | tf_op jit(solution)/shard_map/ppermute | solution.py:149
  256.1 5.4 %all-to-all-start.5 = ((bf16[8,48,320]{2,1,0:T(8,128)(2,1)}), bf16[8,48,320]{2,1,0:T(8,128)(2,1)S(1)}, u32[]{:S(2)}, u32[]{:S(2)}) async-start(bf16[8,48,320]{2,1,0:T(8,128)(2,1)} %bitcast.107), calls=%async_computation.5 | async-start | bytes 589824 | tf_op jit(solution)/shard_map/all_to_all | solution.py:152
  261.5 8.6 %fusion = bf16[2560,1152]{0,1:T(8,128)(2,1)} fusion(bf16[768,1152]{1,0:T(8,128)(2,1)S(1)} %constant_dynamic-update-slice_fusion, bf16[2560,768]{0,1:T(8,128)(2,1)} %bitcast.120), kind=kOutput, calls=%fused_computation.2 | convolution fusion | flops 4532797440 | bytes 11599872 | tf_op jit(solution)/shard_map/dot_general | solution.py:156
  270.1 8.8 %copy.75 = bf16[2560,1152]{1,0:T(8,128)(2,1)} copy(bf16[2560,1152]{0,1:T(8,128)(2,1)} %fusion) | data formatting | bytes 11796480
  (91 shorter events, 32.5 us)
Async XLA Ops:
  7.2 13.1 %copy-start.1 = (bf16[24,18432]{1,0:T(8,128)(2,1)S(1)}, bf16[24,18432]{1,0:T(8,128)(2,1)}, u32[]{:S(2)}) copy-start(bf16[24,18432]{1,0:T(8,128)(2,1)} %param.8) | copy-start | bytes 2654212
  7.2 73.1 %all-gather.2.cloned.1.call-start = ((), (), s32[]{:S(2)}) async-start(), calls=%async_computation.6 | async-start | bytes 4177920 | tf_op jit(solution)/shard_map/all_gather | solution.py:54
  37.5 39.5 %all-to-all-start.2 = ((bf16[24,16,1,1152]{3,0,2,1:T(8,128)(2,1)}), bf16[24,16,1,1152]{3,0,2,1:T(8,128)(2,1)S(1)}, u32[]{:S(2)}, u32[]{:S(2)}) async-start(bf16[24,16,1,1152]{3,0,2,1:T(8,128)(2,1)} %bitcast.4), calls=%async_computation.2 | async-start | bytes 1769472 | tf_op jit(solution)/shard_map/all_to_all | solution.py:57
  77.2 24.0 %collective-permute-start.2 = (bf16[384,1152]{1,0:T(8,128)(2,1)S(1)}, bf16[384,1152]{1,0:T(8,128)(2,1)S(1)}, u32[]{:S(2)}, u32[]{:S(2)}) collective-permute-start(bf16[384,1152]{1,0:T(8,128)(2,1)S(1)} %bitcast.111), channel_id=1, source_target_pairs={{0,128},{128,0},{1,129},{129,1},{2,130},{130,2},{3,131},{131,3},{4... | collective-permute-start | bytes 2654216 | tf_op jit(solution)/shard_map/ppermute | solution.py:64
  85.6 8.9 %copy-start.3 = (s32[768]{0:T(1024)S(1)}, s32[768]{0:T(1024)}, u32[]{:S(2)}) copy-start(s32[768]{0:T(1024)} %param.10) | copy-start | bytes 9220
  85.6 9.0 %copy-start.2 = (s32[768]{0:T(1024)S(1)}, s32[768]{0:T(1024)}, u32[]{:S(2)}) copy-start(s32[768]{0:T(1024)} %param.11) | copy-start | bytes 9220
  85.6 34.8 %collective-permute-start.1 = (f32[192,1152]{1,0:T(8,128)}, f32[192,1152]{1,0:T(8,128)}, u32[]{:S(2)}, u32[]{:S(2)}) collective-permute-start(f32[192,1152]{1,0:T(8,128)} %fusion.6), channel_id=1, source_target_pairs={{0,128},{128,0},{1,129},{129,1},{2,130},{130,2},{3,131},{131,3},{4... | collective-permute-start | bytes 2654216 | tf_op jit(solution)/shard_map/ppermute | solution.py:79
  93.1 45.8 %collective-permute-start = (f32[192,1152]{1,0:T(8,128)}, f32[192,1152]{1,0:T(8,128)}, u32[]{:S(2)}, u32[]{:S(2)}) collective-permute-start(f32[192,1152]{1,0:T(8,128)} %fusion.8), channel_id=1, source_target_pairs={{0,128},{128,0},{1,129},{129,1},{2,130},{130,2},{3,131},{131,3},{4... | collective-permute-start | bytes 2654216 | tf_op jit(solution)/shard_map/ppermute | solution.py:79
  101.3 37.6 %copy-start.4 = (bf16[768,2560]{1,0:T(8,128)(2,1)S(1)}, bf16[768,2560]{1,0:T(8,128)(2,1)}, u32[]{:S(2)}) copy-start(bf16[768,2560]{1,0:T(8,128)(2,1)} %all-gather.2.cloned.1.call-done) | copy-start | bytes 11796484
  170.0 9.6 %all-to-all-start.4 = ((f32[8,7,384]{2,1,0:T(8,128)}), f32[8,7,384]{2,1,0:T(8,128)}, u32[]{:S(2)}, u32[]{:S(2)}) async-start(f32[8,7,384]{2,1,0:T(8,128)} %broadcast_in_dim.21), calls=%async_computation.4 | async-start | bytes 196608 | tf_op jit(solution)/shard_map/all_to_all | solution.py:32
  182.5 23.0 %collective-permute-start.3 = (bf16[384,1152]{1,0:T(8,128)(2,1)}, bf16[384,1152]{1,0:T(8,128)(2,1)S(1)}, u32[]{:S(2)}, u32[]{:S(2)}) collective-permute-start(bf16[384,1152]{1,0:T(8,128)(2,1)} %multiply_convert_fusion), channel_id=1, source_target_pairs={{0,128},{128,0},{1,129},{129,1},{2,130},{130,2},{3,131},{131,3},{4... | collective-permute-start | bytes 2654216 | tf_op jit(solution)/shard_map/ppermute | solution.py:120
  208.1 9.8 %slice-start = ((s8[5898240]{0:T(1024)(128)(4,1)}), s8[4194304]{0:T(1024)(128)(4,1)S(1)}, s32[]{:S(2)}) async-start(s8[5898240]{0:T(1024)(128)(4,1)} %bitcast.118), calls=%async_computation.7 | async-start | bytes 8388608
  208.2 9.7 %slice-start.1 = ((s8[5898240]{0:T(1024)(128)(4,1)}), s8[1703936]{0:T(1024)(128)(4,1)S(1)}, s32[]{:S(2)}) async-start(s8[5898240]{0:T(1024)(128)(4,1)} %bitcast.118), calls=%async_computation.8 | async-start | bytes 3407872
  213.8 4.1 %collective-permute-start.4 = (bf16[384,2560]{1,0:T(8,128)(2,1)S(1)}, bf16[384,2560]{1,0:T(8,128)(2,1)S(1)}, u32[]{:S(2)}, u32[]{:S(2)}) collective-permute-start(bf16[384,2560]{1,0:T(8,128)(2,1)S(1)} %convolution_convert_fusion.1), channel_id=1, source_target_pairs={{0,8},{8,0},{16,24},{24,16},{32,40},{40,32},{48,56},{56,48},{64,72... | collective-permute-start | bytes 5898248 | tf_op jit(solution)/shard_map/ppermute | solution.py:134
  220.6 25.5 %copy-start = (f32[384,2560]{1,0:T(8,128)}, f32[384,2560]{1,0:T(8,128)S(1)}, u32[]{:S(2)}) copy-start(f32[384,2560]{1,0:T(8,128)S(1)} %get-tuple-element.51) | copy-start | bytes 11796484
  220.7 6.7 %collective-permute-start.5 = (bf16[24,2560]{1,0:T(8,128)(2,1)S(1)}, bf16[24,2560]{1,0:T(8,128)(2,1)S(1)}, u32[]{:S(2)}, u32[]{:S(2)}) collective-permute-start(bf16[24,2560]{1,0:T(8,128)(2,1)S(1)} %get-tuple-element.58), channel_id=1, source_target_pairs={{0,16},{8,24},{16,32},{24,40},{32,48},{40,56},{48,64},{56,72},{64,... | collective-permute-start | bytes 368648 | tf_op jit(solution)/shard_map/ppermute | solution.py:138
  220.8 6.6 %collective-permute-start.9 = (bf16[24,2560]{1,0:T(8,128)(2,1)S(1)}, bf16[24,2560]{1,0:T(8,128)(2,1)S(1)}, u32[]{:S(2)}, u32[]{:S(2)}) collective-permute-start(bf16[24,2560]{1,0:T(8,128)(2,1)S(1)} %get-tuple-element.59), channel_id=1, source_target_pairs={{0,112},{8,120},{16,0},{24,8},{32,16},{40,24},{48,32},{56,40},{64,... | collective-permute-start | bytes 368648 | tf_op jit(solution)/shard_map/ppermute | solution.py:139
  227.4 7.4 %collective-permute-start.10 = (bf16[48,2560]{1,0:T(8,128)(2,1)S(1)}, bf16[48,2560]{1,0:T(8,128)(2,1)S(1)}, u32[]{:S(2)}, u32[]{:S(2)}) collective-permute-start(bf16[48,2560]{1,0:T(8,128)(2,1)S(1)} %pad_maximum_fusion.2), channel_id=1, source_target_pairs={{0,112},{8,120},{16,0},{24,8},{32,16},{40,24},{48,32},{56,40},{64,... | collective-permute-start | bytes 737288 | tf_op jit(solution)/shard_map/ppermute | solution.py:149
  230.5 7.9 %collective-permute-start.6 = (bf16[48,2560]{1,0:T(8,128)(2,1)S(1)}, bf16[48,2560]{1,0:T(8,128)(2,1)S(1)}, u32[]{:S(2)}, u32[]{:S(2)}) collective-permute-start(bf16[48,2560]{1,0:T(8,128)(2,1)S(1)} %pad_maximum_fusion.1), channel_id=1, source_target_pairs={{0,16},{8,24},{16,32},{24,40},{32,48},{40,56},{48,64},{56,72},{64,... | collective-permute-start | bytes 737288 | tf_op jit(solution)/shard_map/ppermute | solution.py:148
  238.4 6.3 %collective-permute-start.11 = (bf16[48,2560]{1,0:T(8,128)(2,1)S(1)}, bf16[48,2560]{1,0:T(8,128)(2,1)S(1)}, u32[]{:S(2)}, u32[]{:S(2)}) collective-permute-start(bf16[48,2560]{1,0:T(8,128)(2,1)S(1)} %get-tuple-element.55), channel_id=1, source_target_pairs={{0,112},{8,120},{16,0},{24,8},{32,16},{40,24},{48,32},{56,40},{64,... | collective-permute-start | bytes 737288 | tf_op jit(solution)/shard_map/ppermute | solution.py:149
  238.7 7.4 %collective-permute-start.7 = (bf16[48,2560]{1,0:T(8,128)(2,1)S(1)}, bf16[48,2560]{1,0:T(8,128)(2,1)S(1)}, u32[]{:S(2)}, u32[]{:S(2)}) collective-permute-start(bf16[48,2560]{1,0:T(8,128)(2,1)S(1)} %get-tuple-element.54), channel_id=1, source_target_pairs={{0,16},{8,24},{16,32},{24,40},{32,48},{40,56},{48,64},{56,72},{64,... | collective-permute-start | bytes 737288 | tf_op jit(solution)/shard_map/ppermute | solution.py:148
  246.2 6.3 %collective-permute-start.12 = (bf16[48,2560]{1,0:T(8,128)(2,1)S(1)}, bf16[48,2560]{1,0:T(8,128)(2,1)S(1)}, u32[]{:S(2)}, u32[]{:S(2)}) collective-permute-start(bf16[48,2560]{1,0:T(8,128)(2,1)S(1)} %get-tuple-element.53), channel_id=1, source_target_pairs={{0,112},{8,120},{16,0},{24,8},{32,16},{40,24},{48,32},{56,40},{64,... | collective-permute-start | bytes 737288 | tf_op jit(solution)/shard_map/ppermute | solution.py:149
  246.3 7.7 %collective-permute-start.8 = (bf16[48,2560]{1,0:T(8,128)(2,1)S(1)}, bf16[48,2560]{1,0:T(8,128)(2,1)S(1)}, u32[]{:S(2)}, u32[]{:S(2)}) collective-permute-start(bf16[48,2560]{1,0:T(8,128)(2,1)S(1)} %get-tuple-element.52), channel_id=1, source_target_pairs={{0,16},{8,24},{16,32},{24,40},{32,48},{40,56},{48,64},{56,72},{64,... | collective-permute-start | bytes 737288 | tf_op jit(solution)/shard_map/ppermute | solution.py:148
  256.1 22.7 %all-to-all-start.5 = ((bf16[8,48,320]{2,1,0:T(8,128)(2,1)}), bf16[8,48,320]{2,1,0:T(8,128)(2,1)S(1)}, u32[]{:S(2)}, u32[]{:S(2)}) async-start(bf16[8,48,320]{2,1,0:T(8,128)(2,1)} %bitcast.107), calls=%async_computation.5 | async-start | bytes 589824 | tf_op jit(solution)/shard_map/all_to_all | solution.py:152
Sparse Core Ops, SparseCore 0:
  20.4 59.8 all-gather.1

commit v2 on v0

v2 whole, which is shorter than its diff:
```python
import functools

import jax
import jax.numpy as jnp
from jax import lax
from jax.experimental import pallas as pl
from jax.experimental.pallas import tpu as pltpu
from jax.sharding import PartitionSpec as P

F32 = jnp.float32
BF16 = jnp.bfloat16
NT = (((1,), (1,)), ((), ()))
TN = (((0,), (0,)), ((), ()))
INTERP = False
VMEM_LIMIT = 16 * 1024 * 1024


def call(kernel, flops, traffic, **spec):
    return pl.pallas_call(
        kernel,
        compiler_params=pltpu.CompilerParams(vmem_limit_bytes=VMEM_LIMIT),
        cost_estimate=pl.CostEstimate(flops=flops, bytes_accessed=traffic, transcendentals=0),
        interpret=INTERP,
        **spec,
    )


def whole(shape):
    return pl.BlockSpec(shape, lambda i: (0,) * len(shape))


BATCHES = ((0, 1, 7), (2, 6), (3, 4, 5))
PLACE = tuple(k for batch in BATCHES for k in batch)


def logits_kernel(parts, *refs):
    row_refs, (own_ref, partner_ref, mine_ref, theirs_ref) = refs[:-4], refs[-4:]
    blocks, at = [], 0
    for count in parts:
        blocks.append(jnp.concatenate([ref[...] for ref in row_refs[at : at + count]], axis=1))
        at += count
    rows = jnp.concatenate(blocks, axis=0)
    size = blocks[0].shape[0]
    cut = size // 2
    columns = own_ref.shape[1]
    for base, ref in ((0, own_ref), (columns, partner_ref)):
        for first in range(0, columns, 256):
            last = min(first + 256, columns)
            terms = jnp.dot(rows, ref[:, first:last], preferred_element_type=F32)
            for i in range(len(parts)):
                mine_ref[i, :, base + first : base + last] = terms[i * size : i * size + cut]
                theirs_ref[i, :, base + first : base + last] = terms[
                    i * size + cut : (i + 1) * size
                ]


def logits_of(blocks, own, partner):
    depth, columns = own.shape
    size = blocks[0][0].shape[0]
    flat = [piece for block in blocks for piece in block]
    count = len(blocks)
    out = jax.ShapeDtypeStruct((count, size // 2, 2 * columns), F32)
    return call(
        functools.partial(logits_kernel, tuple(len(block) for block in blocks)),
        4 * count * size * depth * columns,
        4 * depth * columns + 8 * count * size * columns,
        in_specs=in_vmem(len(flat) + 2),
        out_specs=in_vmem(2),
        out_shape=[out, out],
    )(*flat, own, partner)


def align_kernel(order_ref, token_ref, a_ref, b_ref, c_ref, d_ref, out_ref, choice_ref):
    lines = a_ref.shape[0]

    @pl.when(pl.program_id(0) == 0)
    def _():
        choice_ref[...] = jnp.where(order_ref[...] == token_ref[...], 1.0, 0.0).astype(BF16)

    total = None
    for i, ref in enumerate((a_ref, b_ref, c_ref, d_ref)):
        choice = choice_ref[:, i * lines : (i + 1) * lines]
        term = jnp.dot(choice, ref[...], preferred_element_type=F32)
        total = term if total is None else total + term
    out_ref[...] = total.astype(BF16)


def aligned(order, token, own, swapped):
    lines, columns = own[0].shape
    tiles = 6 if columns % 768 == 0 else 2
    tile = columns // tiles
    here = pl.BlockSpec((lines, tile), lambda i: (0, i))
    there = pl.BlockSpec((lines, tile), lambda i: (0, lax.rem(i + tiles // 2, tiles)))
    tokens = token.shape[0]
    return call(
        align_kernel,
        8 * tokens * lines * columns,
        12 * lines * columns,
        grid=(tiles,),
        in_specs=[whole(order.shape), whole(token.shape), here, here, there, there],
        out_specs=pl.BlockSpec((tokens, tile), lambda i: (0, i)),
        out_shape=jax.ShapeDtypeStruct((tokens, columns), BF16),
        scratch_shapes=[pltpu.VMEM((tokens, 4 * lines), BF16)],
    )(order, token, *own, *swapped)


def stats_kernel(z_ref, *refs):
    count = len(BATCHES)
    kept, received = refs[:count], refs[count : 2 * count]
    teacher_ref, target_ref, logits_ref, table_ref, columns_ref = refs[2 * count :]
    cut = kept[0].shape[1]
    lane = lax.broadcasted_iota(jnp.int32, (cut, 128), 1)

    def total(value):
        return jnp.sum(value, axis=1, keepdims=True)

    place = 0
    for b, batch in enumerate(BATCHES):
        for i, k in enumerate(batch):
            logits = kept[b][i] + received[b][i]
            logits_ref[place] = logits
            teacher = teacher_ref[place].astype(F32)[:cut]
            hit = lax.broadcasted_iota(jnp.int32, logits.shape, 1) == target_ref[place]
            top_s = jnp.max(logits, axis=1, keepdims=True)
            top_t = jnp.max(teacher, axis=1, keepdims=True)
            exp_s = jnp.exp(logits - top_s)
            columns = [
                top_s,
                total(exp_s),
                total(exp_s * (logits - teacher)),
                top_t,
                total(jnp.exp(teacher - top_t)),
                total(jnp.where(hit, logits, 0.0)),
                total(jnp.where(hit, teacher, 0.0)),
            ]
            table = jnp.zeros((cut, 128), F32)
            for j, column in enumerate(columns):
                table = jnp.where(lane == j, column, table)
            chip = lax.rem(z_ref[0] + k, len(PLACE))
            columns_ref[pl.ds(pl.multiple_of(chip * cut, 8), cut), :] = table
            place += 1
    lines = cut * len(PLACE)
    turned = columns_ref[...].T[:8, :lines]
    table_ref[...] = jnp.broadcast_to(turned[None], table_ref.shape)


def in_vmem(count):
    return [pl.BlockSpec(memory_space=pltpu.VMEM)] * count


def stats_of(z, kept, received, teacher, target, members):
    cut, columns = kept[0].shape[1:]
    chips = len(PLACE)
    lines = chips * cut
    padded = -(-lines // 128) * 128
    return call(
        stats_kernel,
        20 * lines * columns,
        14 * lines * columns,
        in_specs=[pl.BlockSpec(memory_space=pltpu.SMEM)] + in_vmem(2 * len(BATCHES) + 2),
        out_specs=in_vmem(2),
        out_shape=[
            jax.ShapeDtypeStruct((chips, cut, columns), F32),
            jax.ShapeDtypeStruct((members, 8, lines), F32),
        ],
        scratch_shapes=[pltpu.VMEM((padded, 128), F32)],
    )(z, *kept, *received, teacher, target)


def merged(table):
    max_s = jnp.max(table[:, 0], axis=0, keepdims=True)
    max_t = jnp.max(table[:, 3], axis=0, keepdims=True)
    scale_s = jnp.exp(table[:, 0] - max_s)
    scale_t = jnp.exp(table[:, 3] - max_t)

    def total(value):
        return jnp.sum(value, axis=0, keepdims=True)

    return [
        max_s,
        total(table[:, 1] * scale_s),
        total(table[:, 2] * scale_s),
        max_t,
        total(table[:, 4] * scale_t),
        total(table[:, 5]),
        total(table[:, 6]),
    ]


def merge_kernel(table_ref, out_ref):
    rows = merged(table_ref[...])
    table = jnp.concatenate(rows + [jnp.zeros_like(rows[0])], axis=0)
    out_ref[...] = jnp.broadcast_to(table[None], out_ref.shape)


def merge_of(table, members):
    lines = table.shape[2]
    return call(
        merge_kernel,
        16 * table.size,
        8 * table.size,
        out_shape=jax.ShapeDtypeStruct((members, 8, lines), F32),
    )(table)


def grad_kernel(place_ref, logits_ref, *refs):
    count = len(BATCHES)
    sent, received = refs[:count], refs[count : 2 * count]
    teacher_ref, table_ref, weight_ref, own_ref, partner_ref, rows_ref, columns_ref = refs[2 * count :]
    cut, columns = logits_ref.shape[1:]
    lines = cut * len(PLACE)
    padded = columns_ref.shape[1]
    members = table_ref.shape[0] // 2
    sec = place_ref[1]
    for i in range(2):
        which = sec if i == 0 else 1 - sec
        max_s, sum_s, cross, max_t, sum_t, pick_s, pick_t = merged(
            table_ref[pl.ds(which * members, members)]
        )
        student = max_s + jnp.log(sum_s)
        taught = max_t + jnp.log(sum_t)
        kl = cross / sum_s - student + taught
        gap = pick_s - student - (pick_t - taught)
        zero = jnp.zeros_like(kl)
        table = jnp.concatenate(
            [kl, gap, student, taught, weight_ref[i], zero, zero, zero], axis=0
        )
        rows_ref[which] = table
        table = jnp.concatenate([table, jnp.zeros((120, lines), F32)], axis=0)
        if padded > lines:
            table = jnp.concatenate([table, jnp.zeros((128, padded - lines), F32)], axis=1)
        columns_ref[i] = table.T

    def grad(logits, teacher, row):
        log_student = logits - row[:, 2:3]
        log_teacher = teacher - row[:, 3:4]
        return row[:, 4:5] * jnp.exp(log_student) * (log_student - log_teacher - row[:, 0:1])

    place = 0
    for b, batch in enumerate(BATCHES):
        for i, k in enumerate(batch):
            chip = lax.rem(place_ref[0] + k, len(PLACE))
            at = pl.ds(pl.multiple_of(chip * cut, 8), cut)
            teacher = teacher_ref[place].astype(F32)
            mine = grad(logits_ref[place], teacher[:cut], columns_ref[0, at, :])
            theirs = grad(sent[b][i] + received[b][i], teacher[cut:], columns_ref[1, at, :])
            both = jnp.concatenate([mine, theirs], axis=0).astype(BF16)
            own_ref[place] = both[:, : columns // 2]
            partner_ref[place] = both[:, columns // 2 :]
            place += 1


def grad_of(place, logits, sent, received, teacher, table, weight):
    chips, cut, columns = logits.shape
    lines = chips * cut
    padded = -(-lines // 128) * 128
    half = jax.ShapeDtypeStruct((chips, 2 * cut, columns // 2), BF16)
    return call(
        grad_kernel,
        20 * lines * columns,
        20 * lines * columns,
        in_specs=[pl.BlockSpec(memory_space=pltpu.SMEM)] + in_vmem(2 * len(BATCHES) + 4),
        out_specs=in_vmem(3),
        out_shape=[half, half, jax.ShapeDtypeStruct((2, 8, lines), F32)],
        scratch_shapes=[pltpu.VMEM((2, padded, 128), F32)],
    )(place, logits, *sent, *received, teacher, table, weight)


def terms_kernel(own_grad_ref, partner_grad_ref, own_ref, partner_ref, out_ref):
    members, width, _ = out_ref.shape
    group = members // 2
    for first in range(0, members, group):
        at = slice(first * width, (first + group) * width)
        terms = lax.dot_general(
            own_ref[at], own_grad_ref[...], NT, preferred_element_type=F32
        ) + lax.dot_general(
            partner_ref[at], partner_grad_ref[...], NT, preferred_element_type=F32
        )
        for i in range(group):
            out_ref[first + i] = terms[i * width : (i + 1) * width].astype(BF16)


def terms_of(own_grad, partner_grad, own, partner, members):
    chips, size, columns = own_grad.shape
    depth = own.shape[0]
    lines = chips * size
    return call(
        terms_kernel,
        4 * lines * columns * depth,
        4 * (lines + depth) * columns + 2 * lines * depth,
        in_specs=in_vmem(4),
        out_specs=in_vmem(1)[0],
        out_shape=jax.ShapeDtypeStruct((members, depth // members, lines), BF16),
    )(own_grad.reshape(lines, columns), partner_grad.reshape(lines, columns), own, partner)


def sum_kernel(place_ref, parts_ref, out_ref):
    size = out_ref.shape[1]
    total = None
    for member in range(parts_ref.shape[0]):
        term = parts_ref[member].astype(F32)
        total = term if total is None else total + term
    total = total.T.astype(BF16)
    for i, k in enumerate(PLACE):
        chip = lax.rem(place_ref[0] + k, len(PLACE))
        out_ref[chip] = total[i * size : (i + 1) * size]


def sum_of(place, parts):
    members, width, lines = parts.shape
    chips = len(PLACE)
    return call(
        sum_kernel,
        parts.size,
        2 * parts.size,
        in_specs=[pl.BlockSpec(memory_space=pltpu.SMEM)] + in_vmem(1),
        out_specs=in_vmem(1)[0],
        out_shape=jax.ShapeDtypeStruct((chips, lines // chips, width), BF16),
    )(place, parts)


def head_grad_kernel(a_rows_ref, b_rows_ref, a_grad_ref, b_grad_ref, out_ref):
    terms = lax.dot_general(a_rows_ref[...], a_grad_ref[...], TN, preferred_element_type=F32)
    terms += lax.dot_general(b_rows_ref[...], b_grad_ref[...], TN, preferred_element_type=F32)
    out_ref[...] = terms.astype(BF16)


def head_grad_of(a_rows, b_rows, a_grad, b_grad):
    lines, depth = a_rows.shape
    columns = a_grad.shape[-1]
    tile = min(256, depth)
    rows = pl.BlockSpec((lines, tile), lambda i: (0, i))
    return call(
        head_grad_kernel,
        4 * lines * depth * columns,
        4 * (lines * depth + lines * columns) + 2 * depth * columns,
        grid=(depth // tile,),
        in_specs=[rows, rows, whole((lines, columns)), whole((lines, columns))],
        out_specs=pl.BlockSpec((tile, columns), lambda i: (i, 0)),
        out_shape=jax.ShapeDtypeStruct((depth, columns), BF16),
    )(a_rows, b_rows, a_grad.reshape(lines, columns), b_grad.reshape(lines, columns))


def exchange(copies, axis, groups=None):
    return lax.all_to_all(
        copies, axis, split_axis=0, concat_axis=0, tiled=True, axis_index_groups=groups
    )


def on_device(hidden, head, teacher_logits, loss_mask, token_ids, row_order):
    dp_size = lax.axis_size("dp")
    vocab_size = lax.axis_size("vocab")
    z_size = dp_size // 2
    far = z_size // 2
    sec = lax.axis_index("sec")
    dp = lax.axis_index("dp")
    vocab = lax.axis_index("vocab")
    z, core = dp // 2, dp % 2
    block_width = head.shape[1]
    rows, width = hidden.shape
    cut = rows // 2
    lines = z_size * cut
    teacher_rows = teacher_logits.shape[0]
    swap_sec = [(0, 1), (1, 0)]
    swap_core = [(i, i ^ 1) for i in range(dp_size)]
    along = [[2 * i + c for i in range(z_size)] for c in range(2)]

    def shift(by):
        return [(i, (i + 2 * by) % dp_size) for i in range(dp_size)]

    def to_partner(value):
        return lax.ppermute(value, "dp", swap_core)

    head_partner = to_partner(head)
    arranged = jnp.where(sec == 0, hidden, jnp.concatenate([hidden[cut:], hidden[:cut]], axis=0))
    copies = jnp.broadcast_to(arranged[None], (vocab_size, rows, width))
    features = exchange(copies, "vocab").transpose(1, 0, 2).reshape(rows, vocab_size * width)

    tiles = teacher_logits.reshape(teacher_rows, 2, vocab_size, block_width)
    tiles = jnp.where(core == 0, tiles, jnp.concatenate([tiles[:, 1:], tiles[:, :1]], axis=1))
    tiles, features = lax.optimization_barrier((tiles, features))
    tiles = lax.all_to_all(tiles, "vocab", split_axis=2, concat_axis=1, tiled=True)
    tiles = tiles.reshape(teacher_rows, z_size, 2 * block_width)

    blocks = {0: [features]}
    kept, sent, received = [], [], []

    def take(batch):
        mine, theirs = logits_of([blocks[k] for k in batch], head, head_partner)
        kept.append(mine)
        sent.append(theirs)
        received.append(lax.ppermute(theirs, "sec", swap_sec))

    up, down = features, features
    middle = features.shape[1] // 2
    for step in range(1, far):
        up = lax.ppermute(up, "dp", shift(1))
        down = lax.ppermute(down, "dp", shift(-1))
        blocks[step], blocks[z_size - step] = [down], [up]
        if step == 2:
            up, down, kept[0] = lax.optimization_barrier((up, down, kept[0]))
        if step == 3:
            up, down, kept[1], received[0] = lax.optimization_barrier(
                (up, down, kept[1], received[0])
            )
        if step < far - 1:
            take(BATCHES[step - 1])
    blocks[far] = [
        lax.ppermute(up[:, :middle], "dp", shift(1)),
        lax.ppermute(down[:, middle:], "dp", shift(-1)),
    ]
    blocks[far], tiles, received[1] = lax.optimization_barrier((blocks[far], tiles, received[1]))
    teacher = lax.all_to_all(
        tiles, "dp", split_axis=1, concat_axis=0, tiled=True, axis_index_groups=along
    ).reshape(lines, 2 * block_width)
    take(BATCHES[2])
    teacher, received[2] = lax.optimization_barrier((teacher, received[2]))
    teacher_across = lax.ppermute(teacher, "sec", swap_sec)

    chips = (z + jnp.array(PLACE, jnp.int32)) % z_size
    line = jnp.arange(cut, dtype=jnp.int32)

    def tokens_at(chip, which):
        return (((chip * 2 + core) * rows + which * cut)[:, None] + line).astype(jnp.int32)

    token = jnp.concatenate([tokens_at(chips, sec), tokens_at(chips, 1 - sec)], axis=1)
    by_device = row_order.reshape(2, z_size, 2, teacher_rows)

    def order_of(section, parity):
        part = lax.dynamic_index_in_dim(by_device, section, 0, keepdims=False)
        return lax.dynamic_index_in_dim(part, parity, 1, keepdims=False).reshape(-1)

    order = jnp.concatenate(
        [order_of(a, c) for c in (core, 1 - core) for a in (sec, 1 - sec)]
    )
    taught = aligned(
        order[None, :],
        token.reshape(-1, 1),
        (teacher, teacher_across),
        (to_partner(teacher), to_partner(teacher_across)),
    ).reshape(z_size, rows, 2 * block_width)

    ids = jnp.take(token_ids, tokens_at(chips, sec))
    from_own = ids - ((2 * z + core) * vocab_size + vocab) * block_width
    from_partner = ids - ((2 * z + 1 - core) * vocab_size + vocab) * block_width

    def inside(value):
        return (value >= 0) & (value < block_width)

    target = jnp.where(
        inside(from_own), from_own, jnp.where(inside(from_partner), from_partner + block_width, -1)
    )
    place = jnp.stack([z, sec]).astype(jnp.int32)
    logits, table = stats_of(place, kept, received, taught, target[:, :, None], z_size)
    table = exchange(merge_of(exchange(table, "dp", along), 2 * vocab_size), ("sec", "vocab"))

    held, _ = lax.optimization_barrier((tuple(kept), teacher_across))
    returned = [lax.ppermute(part, "sec", swap_sec) for part in held]

    every = jnp.arange(z_size, dtype=jnp.int32)
    weight = jnp.stack(
        [jnp.take(loss_mask, tokens_at(every, a)).reshape(1, lines) for a in (sec, 1 - sec)]
    ).astype(F32)
    own_grad, partner_grad, per_row = grad_of(
        place, logits, sent, returned, taught, table, weight
    )

    terms = terms_of(own_grad, partner_grad, head, head_partner, vocab_size)
    by_chip = sum_of(place, exchange(terms, "vocab"))
    own_rows = jnp.concatenate([jnp.concatenate(blocks[k], axis=1) for k in PLACE], axis=0)
    head_grad = head_grad_of(
        own_rows, to_partner(own_rows), own_grad, to_partner(partner_grad)
    )

    by_chip, head_grad = lax.optimization_barrier((by_chip, head_grad))
    hidden_grad = jnp.sum(exchange(by_chip, "dp", along).astype(F32), axis=0)
    hidden_grad = jnp.where(
        sec == 0, hidden_grad, jnp.concatenate([hidden_grad[cut:], hidden_grad[:cut]], axis=0)
    )

    other_rows = to_partner(per_row)
    per_row = jnp.where(z % 2 == core, per_row, other_rows)
    per_row = lax.dynamic_index_in_dim(per_row, core, 0, keepdims=False)
    per_row = lax.dynamic_slice_in_dim(per_row, (sec * (z_size // 2) + z // 2) * cut, cut, 1)
    return (head_grad, hidden_grad, per_row[0], per_row[1])


def solution(mesh):
    in_specs = (
        P("dp", ("sec", "vocab")),
        P("sec", ("dp", "vocab")),
        P(("sec", "dp"), "vocab"),
        P(),
        P(),
        P(),
    )
    out_specs = (
        P("sec", ("dp", "vocab")),
        P("dp", ("sec", "vocab")),
        P(("sec", "dp")),
        P(("sec", "dp")),
    )
    return jax.shard_map(
        on_device, mesh=mesh, in_specs=in_specs, out_specs=out_specs, check_vma=False
    )
```

time: 1220 us -> 246 us (0.20)
  blocking collectives: 914 us -> 0 us
  waiting for transfers between devices: 218 us -> 77.6 us
  starting transfers between devices: 0.39 us -> 69.7 us
  Pallas kernels: 0 us -> 51.2 us
  matrix products: 32.9 us -> 0 us
  local copies, waits for them, and re-layouts: 23.7 us -> 40.8 us
  between operations: 13.9 us -> 1.12 us
    psum x1 -> x0, blocking collectives: 550 us -> none  [on_device(): lax.psum((jnp.sum(student_exp, axis=1), jnp.sum(teacher_exp, axis=1), jnp...]
    pmax x1 -> x0, blocking collectives: 279 us -> none  [on_device(): lax.pmax((local_student, local_teacher), ('dp', 'vocab'))]
    psum x1 -> x0, waiting for transfers between devices: 104 us -> none  [on_device(): logits = lax.psum(partial_value, 'sec')]
    reduce_scatter x1 -> x0, waiting for transfers between devices: 71 us -> none  [on_device(): lax.psum_scatter(lax.dot_general(logit_grad, head, (((1,), (1,)), ((), ()...]
    all_to_all x2 -> x0, blocking collectives: 56.9 us -> none  [the longest x1 41 us: on_device(): lax.all_to_all(lax.all_to_all(tiles, 'vocab', split_axis=2, concat_axis=1...]
    pallas_call x0 -> x10, Pallas kernels: none -> 51.2 us  [the longest x3 16.2 us: logits_of(): call(functools.partial(logits_kernel, tuple((len(block) for block in bloc...]
    ppermute x0 -> x21, waiting for transfers between devices: none -> 47.7 us  [the longest x3 17.4 us: take(): received.append(lax.ppermute(theirs, 'sec', swap_sec))]
    all_to_all x0 -> x7, starting transfers between devices: none -> 42.9 us  [the longest x5 31 us: exchange(): lax.all_to_all(copies, axis, split_axis=0, concat_axis=0, tiled=True, axi...]
  transfers between devices with their start and end apart: 5 -> 28, of which waited for: 5 -> 12; matrix products, arithmetic and copies ran while one was open for 4% -> 9% of each run, Pallas kernels for 0% -> 20%
where the time goes in v2:
time: 246 us; the launch traced here: 245 us
  waiting for transfers between devices  77.6 us (32%)
  starting transfers between devices  69.7 us (28%)
  Pallas kernels  51.2 us (21%)
  local copies, waits for them, and re-layouts  40.8 us (17%)
  other arithmetic  4.13 us (2%)
    all_to_all x5, starting transfers between devices, exchange(): lax.all_to_all(copies, axis, split_axis=0, concat_axis=0, tiled=True, axi...  31 us
    all_to_all x5, waiting for transfers between devices, exchange(): lax.all_to_all(copies, axis, split_axis=0, concat_axis=0, tiled=True, axi...  29.8 us
    unnamed x57, local copies, waits for them, and re-layouts  26.7 us
    ppermute x3, waiting for transfers between devices, take(): received.append(lax.ppermute(theirs, 'sec', swap_sec))  17.4 us
    pallas_call x3, Pallas kernels, logits_of(): call(functools.partial(logits_kernel, tuple((len(block) for block in bloc...  16.2 us
    ppermute x1, waiting for transfers between devices, on_device(): teacher_across = lax.ppermute(teacher, 'sec', swap_sec)  16.1 us
    pallas_call x1, Pallas kernels, head_grad_of(): call(head_grad_kernel, 4 * lines * depth * columns, 4 * (lines * depth +...  11.6 us
    ppermute x3, starting transfers between devices, on_device(): down = lax.ppermute(down, 'dp', shift(-1))  10.5 us
  transfers between devices with their start and end apart: 28, of which 12 were waited for; matrix products, arithmetic and copies ran while one was open for 9% of the time, Pallas kernels for 20%

profile of v2, /device:TPU:10, one launch (start us, length us, event | category | flops | bytes accessed | tf_op | source)
XLA Modules:
  0.0 244.6 jit_solution(15503358700966726703)
XLA Ops:
  3.1 5.8 %all-to-all-start = ((bf16[8,48,320]{2,1,0:T(8,128)(2,1)}), bf16[8,48,320]{2,1,0:T(8,128)(2,1)S(1)}, u32[]{:S(2)}, u32[]{:S(2)}) async-start(bf16[8,48,320]{2,1,0:T(8,128)(2,1)} %broadcast_in_dim.15), calls=%async_computation | async-start | bytes 589824 | tf_op jit(solution)/shard_map/all_to_all | solution.py:345
  11.5 3.6 %all-to-all-done = bf16[8,48,320]{2,1,0:T(8,128)(2,1)S(1)} async-done(((bf16[8,48,320]{2,1,0:T(8,128)(2,1)}), bf16[8,48,320]{2,1,0:T(8,128)(2,1)S(1)}, u32[]{:S(2)}, u32[]{:S(2)}) %all-to-all-start) | async-done | bytes 245792 | tf_op jit(solution)/shard_map/all_to_all | solution.py:345
  17.4 4.0 %collective-permute-start.2 = (bf16[48,2560]{1,0:T(8,128)(2,1)S(1)}, bf16[48,2560]{1,0:T(8,128)(2,1)S(1)}, u32[]{:S(2)}, u32[]{:S(2)}) collective-permute-start(bf16[48,2560]{1,0:T(8,128)(2,1)S(1)} %reshape.125.refs_0_), channel_id=1, source_target_pairs={{0,112},{8,120},{16,0},{24,8},{32,16},{40,24},{48,32},{56,40},{64,... | collective-permute-start | bytes 737288 | tf_op jit(solution)/shard_map/ppermute | solution.py:398
  22.7 4.1 %collective-permute-done.refs_2_ = bf16[48,2560]{1,0:T(8,128)(2,1)S(1)} collective-permute-done((bf16[48,2560]{1,0:T(8,128)(2,1)S(1)}, bf16[48,2560]{1,0:T(8,128)(2,1)S(1)}, u32[]{:S(2)}, u32[]{:S(2)}) %collective-permute-start) | collective-permute-done | bytes 245792 | tf_op jit(solution)/shard_map/ppermute | solution.py:397
  26.9 3.2 %collective-permute-start.3 = (bf16[48,2560]{1,0:T(8,128)(2,1)S(1)}, bf16[48,2560]{1,0:T(8,128)(2,1)S(1)}, u32[]{:S(2)}, u32[]{:S(2)}) collective-permute-start(bf16[48,2560]{1,0:T(8,128)(2,1)S(1)} %collective-permute-done.2.refs_1_), channel_id=1, source_target_pairs={{0,112},{8,120},{16,0},{24,8},{32,16},{40,24},{48,32},{56,40},{64,... | collective-permute-start | bytes 737288 | tf_op jit(solution)/shard_map/ppermute | solution.py:398
  30.1 2.7 %copy-done.1 = bf16[2560,1152]{1,0:T(8,128)(2,1)S(1)} copy-done((bf16[2560,1152]{1,0:T(8,128)(2,1)S(1)}, bf16[2560,1152]{1,0:T(8,128)(2,1)}, u32[]{:S(2)}) %copy-start.1) | copy-done | bytes 5898264
  32.8 4.9 %shard_map.102 = (f32[3,24,2304]{2,1,0:T(8,128)S(1)}, f32[3,24,2304]{2,1,0:T(8,128)S(1)}) custom-call(bf16[48,2560]{1,0:T(8,128)(2,1)S(1)} %reshape.125.refs_0_, bf16[48,2560]{1,0:T(8,128)(2,1)S(1)} %collective-permute-done.2.refs_1_, bf16[48,2560]{1,0:T(8,128)(2,1)S(1)} %collective-permute-done.refs_2_, bf16[2560,1152]{1,0:T(8,128)(2,1)S(1)} %copy-done.1, ...), custom_call_target="tpu_custom_call" | custom-call | flops 1698693120 | bytes 13123584 | tf_op jit(solution)/shard_map/pallas_call | solution.py:63
  39.3 2.8 %copy.22 = bf16[24,2,8,1152]{3,1,0,2:T(2,128)(2,1)} copy(bf16[24,2,8,1152]{3,2,1,0:T(8,128)(2,1)} %maximum_select_fusion) | data formatting | bytes 1769472 | tf_op jit(solution)/shard_map/optimization_barrier | solution.py:381
  42.0 6.7 %all-to-all-start.1 = ((bf16[24,2,8,1152]{3,1,0,2:T(2,128)(2,1)}), bf16[24,2,8,1152]{3,1,0,2:T(2,128)(2,1)}, u32[]{:S(2)}, u32[]{:S(2)}) async-start(bf16[24,2,8,1152]{3,1,0,2:T(2,128)(2,1)} %copy.22), calls=%async_computation.1 | async-start | bytes 1769472 | tf_op jit(solution)/shard_map/all_to_all | solution.py:382
  48.9 3.2 %collective-permute-start.6 = (bf16[48,2560]{1,0:T(8,128)(2,1)S(1)}, bf16[48,2560]{1,0:T(8,128)(2,1)S(1)}, u32[]{:S(2)}, u32[]{:S(2)}) collective-permute-start(bf16[48,2560]{1,0:T(8,128)(2,1)S(1)} %collective-permute-done.3.refs_0_), channel_id=1, source_target_pairs={{0,112},{8,120},{16,0},{24,8},{32,16},{40,24},{48,32},{56,40},{64,... | collective-permute-start | bytes 737288 | tf_op jit(solution)/shard_map/ppermute | solution.py:398
  54.8 5.7 %shard_map.103 = (f32[2,24,2304]{2,1,0:T(8,128)}, f32[2,24,2304]{2,1,0:T(8,128)}) custom-call(bf16[48,2560]{1,0:T(8,128)(2,1)S(1)} %collective-permute-done.3.refs_0_, bf16[48,2560]{1,0:T(8,128)(2,1)S(1)} %collective-permute-done.1.refs_1_, bf16[2560,1152]{1,0:T(8,128)(2,1)S(1)} %copy-done.2, ...), custom_call_target="tpu_custom_call" | custom-call | flops 1132462080 | bytes 12681216 | tf_op jit(solution)/shard_map/pallas_call | solution.py:63
  61.8 3.3 %collective-permute-start.9 = (bf16[48,1280]{1,0:T(8,128)(2,1)S(1)}, bf16[48,1280]{1,0:T(8,128)(2,1)S(1)}, u32[]{:S(2)}, u32[]{:S(2)}) collective-permute-start(bf16[48,1280]{1,0:T(8,128)(2,1)S(1)} %slice.37), channel_id=1, source_target_pairs={{0,112},{8,120},{16,0},{24,8},{32,16},{40,24},{48,32},{56,40},{64,... | collective-permute-start | bytes 368648 | tf_op jit(solution)/shard_map/ppermute | solution.py:410
  65.7 3.3 %reshape.126 = bf16[24,8,2304]{2,0,1:T(8,128)(2,1)} reshape(bf16[24,8,2,1,1152]{4,2,0,1,3:T(2,128)(2,1)} %bitcast.4) | data formatting | bytes 1769472 | tf_op jit(solution)/shard_map/reshape | solution.py:383
  69.1 4.3 %collective-permute-done.10.refs_4_ = f32[2,24,2304]{2,1,0:T(8,128)} collective-permute-done((f32[2,24,2304]{2,1,0:T(8,128)}, f32[2,24,2304]{2,1,0:T(8,128)}, u32[]{:S(2)}, u32[]{:S(2)}) %collective-permute-start.10) | collective-permute-done | bytes 442400 | tf_op jit(solution)/shard_map/ppermute | solution.py:392
  73.4 5.3 %all-to-all-start.2 = ((bf16[24,8,2304]{2,0,1:T(8,128)(2,1)}), bf16[24,8,2304]{2,0,1:T(8,128)(2,1)S(1)}, u32[]{:S(2)}, u32[]{:S(2)}) async-start(bf16[24,8,2304]{2,0,1:T(8,128)(2,1)} %reshape.126), calls=%async_computation.2 | async-start | bytes 1769472 | tf_op jit(solution)/shard_map/all_to_all | solution.py:413
  81.8 2.7 %copy-done.3 = bf16[2560,1152]{1,0:T(8,128)(2,1)S(1)} copy-done((bf16[2560,1152]{1,0:T(8,128)(2,1)S(1)}, bf16[2560,1152]{1,0:T(8,128)(2,1)}, u32[]{:S(2)}) %copy-start.3) | copy-done | bytes 5898264
  84.5 5.7 %shard_map.104 = (f32[3,24,2304]{2,1,0:T(8,128)}, f32[3,24,2304]{2,1,0:T(8,128)S(1)}) custom-call(bf16[48,2560]{1,0:T(8,128)(2,1)S(1)} %collective-permute-done.6.refs_0_, bf16[48,1280]{1,0:T(8,128)(2,1)S(1)} %collective-permute-done.8.refs_1_, bf16[48,1280]{1,0:T(8,128)(2,1)S(1)} %collective-permute-done.9.refs_2_, ...), custom_call_target="tpu_custom_call" | custom-call | flops 1698693120 | bytes 13123584 | tf_op jit(solution)/shard_map/pallas_call | solution.py:63
  92.9 13.0 %collective-permute-done.11.refs_5_ = f32[3,24,2304]{2,1,0:T(8,128)S(1)} collective-permute-done((f32[3,24,2304]{2,1,0:T(8,128)S(1)}, f32[3,24,2304]{2,1,0:T(8,128)S(1)}, u32[]{:S(2)}, u32[]{:S(2)}) %collective-permute-start.11) | collective-permute-done | bytes 663584 | tf_op jit(solution)/shard_map/ppermute | solution.py:392
  110.4 16.1 %collective-permute-done.12.b_ref = bf16[192,2304]{1,0:T(8,128)(2,1)S(1)} collective-permute-done((bf16[192,2304]{1,0:T(8,128)(2,1)S(1)}, bf16[192,2304]{1,0:T(8,128)(2,1)S(1)}, u32[]{:S(2)}, u32[]{:S(2)}) %collective-permute-start.12) | collective-permute-done | bytes 884768 | tf_op jit(solution)/shard_map/ppermute | solution.py:418
  134.0 4.5 %shard_map.105 = bf16[384,2304]{1,0:T(8,128)(2,1)S(1)} custom-call(s32[1,768]{1,0:T(1,128)S(1)} %broadcast_in_dim.17.order_ref, s32[384,1]{1,0:T(8,128)S(1)} %reshape.180.token_ref, bf16[192,2304]{1,0:T(8,128)(2,1)S(1)} %bitcast.30, bf16[192,2304]{1,0:T(8,128)(2,1)S(1)} %collective-permute-done.12.b_ref, ...), custom_call_target="tpu_custom_call" | custom-call | flops 1358954496 | bytes 5308416 | tf_op jit(solution)/shard_map/pallas_call | solution.py:95
  138.5 3.9 %shard_map.106 = (f32[8,24,2304]{2,1,0:T(8,128)S(1)}, f32[8,8,192]{2,1,0:T(8,128)}) custom-call(s32[2]{0:T(128)S(1)} %pad_add_fusion.2.z_ref.place_ref, f32[3,24,2304]{2,1,0:T(8,128)S(1)} %copy-done.11, f32[2,24,2304]{2,1,0:T(8,128)} %get-tuple-element.59.refs_1_, f32[3,24,2304]{2,1,0:T(8,128)} %get-tuple-element.60.refs_2_, f32[3,24,2304]{2,1,0:T(8,128)S(1)} %copy-done.13, ...), custom_call_target="tpu_custom_call" | custom-call | flops 8847360 | bytes 6193152 | tf_op jit(solution)/shard_map/pallas_call | solution.py:156
  143.6 6.6 %all-to-all-start.3 = ((f32[8,8,192]{2,1,0:T(8,128)}), f32[8,8,192]{2,1,0:T(8,128)S(1)}, u32[]{:S(2)}, u32[]{:S(2)}) async-start(f32[8,8,192]{2,1,0:T(8,128)} %get-tuple-element.61), calls=%async_computation.3 | async-start | bytes 131072 | tf_op jit(solution)/shard_map/all_to_all | solution.py:345
  150.5 8.1 %all-to-all-done.3.table_ref = f32[8,8,192]{2,1,0:T(8,128)S(1)} async-done(((f32[8,8,192]{2,1,0:T(8,128)}), f32[8,8,192]{2,1,0:T(8,128)S(1)}, u32[]{:S(2)}, u32[]{:S(2)}) %all-to-all-start.3) | async-done | bytes 49184 | tf_op jit(solution)/shard_map/all_to_all | solution.py:345
  159.3 5.4 %all-to-all-start.4 = ((f32[16,8,192]{2,1,0:T(8,128)}), f32[16,8,192]{2,1,0:T(8,128)S(1)}, u32[]{:S(2)}, u32[]{:S(2)}) async-start(f32[16,8,192]{2,1,0:T(8,128)} %shard_map.107), calls=%async_computation.4 | async-start | bytes 262144 | tf_op jit(solution)/shard_map/all_to_all | solution.py:345
  164.7 6.4 %collective-permute-done.16.refs_4_ = f32[2,24,2304]{2,1,0:T(8,128)} collective-permute-done((f32[2,24,2304]{2,1,0:T(8,128)}, f32[2,24,2304]{2,1,0:T(8,128)}, u32[]{:S(2)}, u32[]{:S(2)}) %collective-permute-start.16) | collective-permute-done | bytes 442400 | tf_op jit(solution)/shard_map/ppermute | solution.py:458
  174.4 3.3 %shard_map.108 = (bf16[8,48,1152]{2,1,0:T(8,128)(2,1)S(1)}, bf16[8,48,1152]{2,1,0:T(8,128)(2,1)S(1)}, f32[2,8,192]{2,1,0:T(8,128)S(1)}) custom-call(s32[2]{0:T(128)S(1)} %pad_add_fusion.2.z_ref.place_ref, f32[8,24,2304]{2,1,0:T(8,128)S(1)} %copy-done.7, f32[3,24,2304]{2,1,0:T(8,128)S(1)} %copy-done.9, f32[2,24,2304]{2,1,0:T(8,128)} %get-tuple-element.47.refs_1_, ...), custom_call_target="tpu_custom_call" | custom-call | flops 8847360 | bytes 8847360 | tf_op jit(solution)/shard_map/pallas_call | solution.py:258
  180.4 9.4 %shard_map.109 = bf16[8,320,384]{2,1,0:T(8,128)(2,1)S(1)} custom-call(bf16[384,1152]{1,0:T(8,128)(2,1)S(1)} %bitcast.31, bf16[384,1152]{1,0:T(8,128)(2,1)S(1)} %bitcast.33, bf16[2560,1152]{1,0:T(8,128)(2,1)S(1)} %copy-done.4, bf16[2560,1152]{1,0:T(8,128)(2,1)} %collective-permute-done.4.refs_4_.refs_3_.refs_5_.partner_ref), custom_call_target="tpu_custom_call" | custom-call | flops 4529848320 | bytes 15532032 | tf_op jit(solution)/shard_map/pallas_call | solution.py:287
  193.0 6.4 %all-to-all-start.5 = ((bf16[8,320,384]{2,1,0:T(8,128)(2,1)}), bf16[8,320,384]{2,1,0:T(8,128)(2,1)S(1)}, u32[]{:S(2)}, u32[]{:S(2)}) async-start(bf16[8,320,384]{2,1,0:T(8,128)(2,1)} %copy-done.5), calls=%async_computation.5 | async-start | bytes 3932160 | tf_op jit(solution)/shard_map/all_to_all | solution.py:345
  204.7 11.6 %shard_map.111 = bf16[2560,1152]{1,0:T(8,128)(2,1)} custom-call(bf16[384,2560]{1,0:T(8,128)(2,1)S(1)} %copy-done.18, bf16[384,2560]{1,0:T(8,128)(2,1)} %collective-permute-done.18.b_rows_ref, bf16[384,1152]{1,0:T(8,128)(2,1)S(1)} %bitcast.32, bf16[384,1152]{1,0:T(8,128)(2,1)S(1)} %bitcast.34), custom_call_target="tpu_custom_call" | custom-call | flops 4529848320 | bytes 11599872 | tf_op jit(solution)/shard_map/pallas_call | solution.py:333
  216.4 6.5 %all-to-all-done.5.parts_ref = bf16[8,320,384]{2,1,0:T(8,128)(2,1)S(1)} async-done(((bf16[8,320,384]{2,1,0:T(8,128)(2,1)}), bf16[8,320,384]{2,1,0:T(8,128)(2,1)S(1)}, u32[]{:S(2)}, u32[]{:S(2)}) %all-to-all-start.5) | async-done | bytes 1966112 | tf_op jit(solution)/shard_map/all_to_all | solution.py:345
  224.4 6.7 %all-to-all-start.6 = ((bf16[8,48,320]{2,1,0:T(8,128)(2,1)}), bf16[8,48,320]{2,1,0:T(8,128)(2,1)S(1)}, u32[]{:S(2)}, u32[]{:S(2)}) async-start(bf16[8,48,320]{2,1,0:T(8,128)(2,1)} %shard_map.110), calls=%async_computation.6 | async-start | bytes 589824 | tf_op jit(solution)/shard_map/all_to_all | solution.py:345
  232.9 11.0 %all-to-all-done.6 = bf16[8,48,320]{2,1,0:T(8,128)(2,1)S(1)} async-done(((bf16[8,48,320]{2,1,0:T(8,128)(2,1)}), bf16[8,48,320]{2,1,0:T(8,128)(2,1)S(1)}, u32[]{:S(2)}, u32[]{:S(2)}) %all-to-all-start.6) | async-done | bytes 245792 | tf_op jit(solution)/shard_map/all_to_all | solution.py:345
  (146 shorter events, 53.3 us)
Async XLA Ops:
  0.6 78.4 %copy-start = (s32[768]{0:T(1024)S(1)}, s32[768]{0:T(1024)}, u32[]{:S(2)}) copy-start(s32[768]{0:T(1024)} %param.12) | copy-start | bytes 9220
  0.7 29.4 %collective-permute-start.4 = (bf16[2560,1152]{1,0:T(8,128)(2,1)}, bf16[2560,1152]{1,0:T(8,128)(2,1)}, u32[]{:S(2)}, u32[]{:S(2)}) collective-permute-start(bf16[2560,1152]{1,0:T(8,128)(2,1)} %own_ref.1), channel_id=1, source_target_pairs={{0,8},{8,0},{16,24},{24,16},{32,40},{40,32},{48,56},{56,48},{64,72... | collective-permute-start | bytes 17694728 | tf_op jit(solution)/shard_map/ppermute | solution.py:372
  3.1 12.0 %all-to-all-start = ((bf16[8,48,320]{2,1,0:T(8,128)(2,1)}), bf16[8,48,320]{2,1,0:T(8,128)(2,1)S(1)}, u32[]{:S(2)}, u32[]{:S(2)}) async-start(bf16[8,48,320]{2,1,0:T(8,128)(2,1)} %broadcast_in_dim.15), calls=%async_computation | async-start | bytes 589824 | tf_op jit(solution)/shard_map/all_to_all | solution.py:345
  15.4 11.5 %collective-permute-start = (bf16[48,2560]{1,0:T(8,128)(2,1)S(1)}, bf16[48,2560]{1,0:T(8,128)(2,1)S(1)}, u32[]{:S(2)}, u32[]{:S(2)}) collective-permute-start(bf16[48,2560]{1,0:T(8,128)(2,1)S(1)} %reshape.125.refs_0_), channel_id=1, source_target_pairs={{0,16},{8,24},{16,32},{24,40},{32,48},{40,56},{48,64},{56,72},{64,... | collective-permute-start | bytes 737288 | tf_op jit(solution)/shard_map/ppermute | solution.py:397
  17.4 9.5 %collective-permute-start.2 = (bf16[48,2560]{1,0:T(8,128)(2,1)S(1)}, bf16[48,2560]{1,0:T(8,128)(2,1)S(1)}, u32[]{:S(2)}, u32[]{:S(2)}) collective-permute-start(bf16[48,2560]{1,0:T(8,128)(2,1)S(1)} %reshape.125.refs_0_), channel_id=1, source_target_pairs={{0,112},{8,120},{16,0},{24,8},{32,16},{40,24},{48,32},{56,40},{64,... | collective-permute-start | bytes 737288 | tf_op jit(solution)/shard_map/ppermute | solution.py:398
  26.9 21.9 %collective-permute-start.1 = (bf16[48,2560]{1,0:T(8,128)(2,1)S(1)}, bf16[48,2560]{1,0:T(8,128)(2,1)S(1)}, u32[]{:S(2)}, u32[]{:S(2)}) collective-permute-start(bf16[48,2560]{1,0:T(8,128)(2,1)S(1)} %collective-permute-done.refs_2_), channel_id=1, source_target_pairs={{0,16},{8,24},{16,32},{24,40},{32,48},{40,56},{48,64},{56,72},{64,... | collective-permute-start | bytes 737288 | tf_op jit(solution)/shard_map/ppermute | solution.py:397
  26.9 21.9 %collective-permute-start.3 = (bf16[48,2560]{1,0:T(8,128)(2,1)S(1)}, bf16[48,2560]{1,0:T(8,128)(2,1)S(1)}, u32[]{:S(2)}, u32[]{:S(2)}) collective-permute-start(bf16[48,2560]{1,0:T(8,128)(2,1)S(1)} %collective-permute-done.2.refs_1_), channel_id=1, source_target_pairs={{0,112},{8,120},{16,0},{24,8},{32,16},{40,24},{48,32},{56,40},{64,... | collective-permute-start | bytes 737288 | tf_op jit(solution)/shard_map/ppermute | solution.py:398
  37.6 22.8 %copy-start.8 = (f32[3,24,2304]{2,1,0:T(8,128)}, f32[3,24,2304]{2,1,0:T(8,128)S(1)}, u32[]{:S(2)}) copy-start(f32[3,24,2304]{2,1,0:T(8,128)S(1)} %get-tuple-element.42.refs_0_) | copy-start | bytes 1990660
  37.7 23.9 %collective-permute-start.7 = (f32[3,24,2304]{2,1,0:T(8,128)S(1)}, f32[3,24,2304]{2,1,0:T(8,128)S(1)}, u32[]{:S(2)}, u32[]{:S(2)}) collective-permute-start(f32[3,24,2304]{2,1,0:T(8,128)S(1)} %get-tuple-element.42.refs_0_), channel_id=1, source_target_pairs={{0,128},{128,0},{1,129},{129,1},{2,130},{130,2},{3,131},{131,3},{4... | collective-permute-start | bytes 1990664 | tf_op jit(solution)/shard_map/ppermute | solution.py:392
  42.0 23.7 %all-to-all-start.1 = ((bf16[24,2,8,1152]{3,1,0,2:T(2,128)(2,1)}), bf16[24,2,8,1152]{3,1,0,2:T(2,128)(2,1)}, u32[]{:S(2)}, u32[]{:S(2)}) async-start(bf16[24,2,8,1152]{3,1,0,2:T(2,128)(2,1)} %copy.22), calls=%async_computation.1 | async-start | bytes 1769472 | tf_op jit(solution)/shard_map/all_to_all | solution.py:382
  48.8 12.7 %collective-permute-start.5 = (bf16[48,2560]{1,0:T(8,128)(2,1)S(1)}, bf16[48,2560]{1,0:T(8,128)(2,1)S(1)}, u32[]{:S(2)}, u32[]{:S(2)}) collective-permute-start(bf16[48,2560]{1,0:T(8,128)(2,1)S(1)} %collective-permute-done.1.refs_1_), channel_id=1, source_target_pairs={{0,16},{8,24},{16,32},{24,40},{32,48},{40,56},{48,64},{56,72},{64,... | collective-permute-start | bytes 737288 | tf_op jit(solution)/shard_map/ppermute | solution.py:397
  48.9 12.6 %collective-permute-start.6 = (bf16[48,2560]{1,0:T(8,128)(2,1)S(1)}, bf16[48,2560]{1,0:T(8,128)(2,1)S(1)}, u32[]{:S(2)}, u32[]{:S(2)}) collective-permute-start(bf16[48,2560]{1,0:T(8,128)(2,1)S(1)} %collective-permute-done.3.refs_0_), channel_id=1, source_target_pairs={{0,112},{8,120},{16,0},{24,8},{32,16},{40,24},{48,32},{56,40},{64,... | collective-permute-start | bytes 737288 | tf_op jit(solution)/shard_map/ppermute | solution.py:398
  60.5 12.9 %collective-permute-start.10 = (f32[2,24,2304]{2,1,0:T(8,128)}, f32[2,24,2304]{2,1,0:T(8,128)}, u32[]{:S(2)}, u32[]{:S(2)}) collective-permute-start(f32[2,24,2304]{2,1,0:T(8,128)} %get-tuple-element.47.refs_1_), channel_id=1, source_target_pairs={{0,128},{128,0},{1,129},{129,1},{2,130},{130,2},{3,131},{131,3},{4... | collective-permute-start | bytes 1327112 | tf_op jit(solution)/shard_map/ppermute | solution.py:392
  61.5 11.9 %copy-start.12 = (f32[3,24,2304]{2,1,0:T(8,128)}, f32[3,24,2304]{2,1,0:T(8,128)S(1)}, u32[]{:S(2)}) copy-start(f32[3,24,2304]{2,1,0:T(8,128)S(1)} %collective-permute-done.7.refs_3_) | copy-start | bytes 1990660
  61.5 11.9 %collective-permute-start.8 = (bf16[48,1280]{1,0:T(8,128)(2,1)S(1)}, bf16[48,1280]{1,0:T(8,128)(2,1)S(1)}, u32[]{:S(2)}, u32[]{:S(2)}) collective-permute-start(bf16[48,1280]{1,0:T(8,128)(2,1)S(1)} %slice.36), channel_id=1, source_target_pairs={{0,16},{8,24},{16,32},{24,40},{32,48},{40,56},{48,64},{56,72},{64,... | collective-permute-start | bytes 368648 | tf_op jit(solution)/shard_map/ppermute | solution.py:409
  61.8 11.6 %collective-permute-start.9 = (bf16[48,1280]{1,0:T(8,128)(2,1)S(1)}, bf16[48,1280]{1,0:T(8,128)(2,1)S(1)}, u32[]{:S(2)}, u32[]{:S(2)}) collective-permute-start(bf16[48,1280]{1,0:T(8,128)(2,1)S(1)} %slice.37), channel_id=1, source_target_pairs={{0,112},{8,120},{16,0},{24,8},{32,16},{40,24},{48,32},{56,40},{64,... | collective-permute-start | bytes 368648 | tf_op jit(solution)/shard_map/ppermute | solution.py:410
  73.4 33.4 %all-to-all-start.2 = ((bf16[24,8,2304]{2,0,1:T(8,128)(2,1)}), bf16[24,8,2304]{2,0,1:T(8,128)(2,1)S(1)}, u32[]{:S(2)}, u32[]{:S(2)}) async-start(bf16[24,8,2304]{2,0,1:T(8,128)(2,1)} %reshape.126), calls=%async_computation.2 | async-start | bytes 1769472 | tf_op jit(solution)/shard_map/all_to_all | solution.py:413
  90.2 15.8 %collective-permute-start.11 = (f32[3,24,2304]{2,1,0:T(8,128)S(1)}, f32[3,24,2304]{2,1,0:T(8,128)S(1)}, u32[]{:S(2)}, u32[]{:S(2)}) collective-permute-start(f32[3,24,2304]{2,1,0:T(8,128)S(1)} %get-tuple-element.54.refs_2_), channel_id=1, source_target_pairs={{0,128},{128,0},{1,129},{129,1},{2,130},{130,2},{3,131},{131,3},{4... | collective-permute-start | bytes 1990664 | tf_op jit(solution)/shard_map/ppermute | solution.py:392
  106.8 19.6 %collective-permute-start.12 = (bf16[192,2304]{1,0:T(8,128)(2,1)S(1)}, bf16[192,2304]{1,0:T(8,128)(2,1)S(1)}, u32[]{:S(2)}, u32[]{:S(2)}) collective-permute-start(bf16[192,2304]{1,0:T(8,128)(2,1)S(1)} %bitcast.28), channel_id=1, source_target_pairs={{0,128},{128,0},{1,129},{129,1},{2,130},{130,2},{3,131},{131,3},{4... | collective-permute-start | bytes 2654216 | tf_op jit(solution)/shard_map/ppermute | solution.py:418
  110.4 21.7 %collective-permute-start.13 = (bf16[192,2304]{1,0:T(8,128)(2,1)S(1)}, bf16[192,2304]{1,0:T(8,128)(2,1)S(1)}, u32[]{:S(2)}, u32[]{:S(2)}) collective-permute-start(bf16[192,2304]{1,0:T(8,128)(2,1)S(1)} %bitcast.29), channel_id=1, source_target_pairs={{0,8},{8,0},{16,24},{24,16},{32,40},{40,32},{48,56},{56,48},{64,72... | collective-permute-start | bytes 2654216 | tf_op jit(solution)/shard_map/ppermute | solution.py:372
  126.5 7.5 %collective-permute-start.14 = (bf16[192,2304]{1,0:T(8,128)(2,1)S(1)}, bf16[192,2304]{1,0:T(8,128)(2,1)S(1)}, u32[]{:S(2)}, u32[]{:S(2)}) collective-permute-start(bf16[192,2304]{1,0:T(8,128)(2,1)S(1)} %collective-permute-done.12.b_ref), channel_id=1, source_target_pairs={{0,8},{8,0},{16,24},{24,16},{32,40},{40,32},{48,56},{56,48},{64,72... | collective-permute-start | bytes 2654216 | tf_op jit(solution)/shard_map/ppermute | solution.py:372
  127.9 43.3 %collective-permute-start.15 = (f32[3,24,2304]{2,1,0:T(8,128)}, f32[3,24,2304]{2,1,0:T(8,128)}, u32[]{:S(2)}, u32[]{:S(2)}) collective-permute-start(f32[3,24,2304]{2,1,0:T(8,128)} %copy-done.10), channel_id=1, source_target_pairs={{0,128},{128,0},{1,129},{129,1},{2,130},{130,2},{3,131},{131,3},{4... | collective-permute-start | bytes 1990664 | tf_op jit(solution)/shard_map/ppermute | solution.py:458
  129.4 41.8 %collective-permute-start.17 = (f32[3,24,2304]{2,1,0:T(8,128)}, f32[3,24,2304]{2,1,0:T(8,128)}, u32[]{:S(2)}, u32[]{:S(2)}) collective-permute-start(f32[3,24,2304]{2,1,0:T(8,128)} %get-tuple-element.60.refs_2_), channel_id=1, source_target_pairs={{0,128},{128,0},{1,129},{129,1},{2,130},{130,2},{3,131},{131,3},{4... | collective-permute-start | bytes 1990664 | tf_op jit(solution)/shard_map/ppermute | solution.py:458
  132.1 67.3 %collective-permute-start.18 = (bf16[384,2560]{1,0:T(8,128)(2,1)}, bf16[384,2560]{1,0:T(8,128)(2,1)}, u32[]{:S(2)}, u32[]{:S(2)}) collective-permute-start(bf16[384,2560]{1,0:T(8,128)(2,1)} %constant_dynamic-update-slice_fusion.a_rows_ref), channel_id=1, source_target_pairs={{0,8},{8,0},{16,24},{24,16},{32,40},{40,32},{48,56},{56,48},{64,72... | collective-permute-start | bytes 5898248 | tf_op jit(solution)/shard_map/ppermute | solution.py:372
  132.1 39.0 %collective-permute-start.16 = (f32[2,24,2304]{2,1,0:T(8,128)}, f32[2,24,2304]{2,1,0:T(8,128)}, u32[]{:S(2)}, u32[]{:S(2)}) collective-permute-start(f32[2,24,2304]{2,1,0:T(8,128)} %get-tuple-element.59.refs_1_), channel_id=1, source_target_pairs={{0,128},{128,0},{1,129},{129,1},{2,130},{130,2},{3,131},{131,3},{4... | collective-permute-start | bytes 1327112 | tf_op jit(solution)/shard_map/ppermute | solution.py:458
  138.5 33.4 %copy-start.9 = (f32[3,24,2304]{2,1,0:T(8,128)S(1)}, f32[3,24,2304]{2,1,0:T(8,128)}, u32[]{:S(2)}) copy-start(f32[3,24,2304]{2,1,0:T(8,128)} %copy-done.8) | copy-start | bytes 1990660
  143.6 15.0 %all-to-all-start.3 = ((f32[8,8,192]{2,1,0:T(8,128)}), f32[8,8,192]{2,1,0:T(8,128)S(1)}, u32[]{:S(2)}, u32[]{:S(2)}) async-start(f32[8,8,192]{2,1,0:T(8,128)} %get-tuple-element.61), calls=%async_computation.3 | async-start | bytes 131072 | tf_op jit(solution)/shard_map/all_to_all | solution.py:345
  159.3 12.5 %all-to-all-start.4 = ((f32[16,8,192]{2,1,0:T(8,128)}), f32[16,8,192]{2,1,0:T(8,128)S(1)}, u32[]{:S(2)}, u32[]{:S(2)}) async-start(f32[16,8,192]{2,1,0:T(8,128)} %shard_map.107), calls=%async_computation.4 | async-start | bytes 262144 | tf_op jit(solution)/shard_map/all_to_all | solution.py:345
  193.0 29.9 %all-to-all-start.5 = ((bf16[8,320,384]{2,1,0:T(8,128)(2,1)}), bf16[8,320,384]{2,1,0:T(8,128)(2,1)S(1)}, u32[]{:S(2)}, u32[]{:S(2)}) async-start(bf16[8,320,384]{2,1,0:T(8,128)(2,1)} %copy-done.5), calls=%async_computation.5 | async-start | bytes 3932160 | tf_op jit(solution)/shard_map/all_to_all | solution.py:345
  199.4 2.6 %collective-permute-start.19 = (bf16[8,48,1152]{2,1,0:T(8,128)(2,1)}, bf16[8,48,1152]{2,1,0:T(8,128)(2,1)S(1)}, u32[]{:S(2)}, u32[]{:S(2)}) collective-permute-start(bf16[8,48,1152]{2,1,0:T(8,128)(2,1)} %copy-done.21), channel_id=1, source_target_pairs={{0,8},{8,0},{16,24},{24,16},{32,40},{40,32},{48,56},{56,48},{64,72... | collective-permute-start | bytes 2654216 | tf_op jit(solution)/shard_map/ppermute | solution.py:372
  224.4 19.4 %all-to-all-start.6 = ((bf16[8,48,320]{2,1,0:T(8,128)(2,1)}), bf16[8,48,320]{2,1,0:T(8,128)(2,1)S(1)}, u32[]{:S(2)}, u32[]{:S(2)}) async-start(bf16[8,48,320]{2,1,0:T(8,128)(2,1)} %shard_map.110), calls=%async_computation.6 | async-start | bytes 589824 | tf_op jit(solution)/shard_map/all_to_all | solution.py:345
  231.1 1.2 collective-permute-start.20
  (21 other events, 85.2 us)

commit v3 on v2

--- a/solution.py
+++ b/solution.py
@@ -267,30 +267,27 @@
 
 
 def terms_kernel(own_grad_ref, partner_grad_ref, own_ref, partner_ref, out_ref):
-    members, width, _ = out_ref.shape
-    group = members // 2
-    for first in range(0, members, group):
-        at = slice(first * width, (first + group) * width)
-        terms = lax.dot_general(
-            own_ref[at], own_grad_ref[...], NT, preferred_element_type=F32
-        ) + lax.dot_general(
-            partner_ref[at], partner_grad_ref[...], NT, preferred_element_type=F32
-        )
-        for i in range(group):
-            out_ref[first + i] = terms[i * width : (i + 1) * width].astype(BF16)
+    terms = lax.dot_general(own_ref[...], own_grad_ref[...], NT, preferred_element_type=F32)
+    terms += lax.dot_general(
+        partner_ref[...], partner_grad_ref[...], NT, preferred_element_type=F32
+    )
+    out_ref[0] = terms.astype(BF16)
 
 
 def terms_of(own_grad, partner_grad, own, partner, members):
     chips, size, columns = own_grad.shape
     depth = own.shape[0]
     lines = chips * size
+    width = depth // members
+    weights = pl.BlockSpec((width, columns), lambda i: (i, 0))
     return call(
         terms_kernel,
         4 * lines * columns * depth,
         4 * (lines + depth) * columns + 2 * lines * depth,
-        in_specs=in_vmem(4),
-        out_specs=in_vmem(1)[0],
-        out_shape=jax.ShapeDtypeStruct((members, depth // members, lines), BF16),
+        grid=(members,),
+        in_specs=[whole((lines, columns))] * 2 + [weights] * 2,
+        out_specs=pl.BlockSpec((1, width, lines), lambda i: (i, 0, 0)),
+        out_shape=jax.ShapeDtypeStruct((members, width, lines), BF16),
     )(own_grad.reshape(lines, columns), partner_grad.reshape(lines, columns), own, partner)
 
 
@@ -385,10 +382,12 @@
     blocks = {0: [features]}
     kept, sent, received = [], [], []
 
-    def take(batch):
+    def take(batch, *before):
         mine, theirs = logits_of([blocks[k] for k in batch], head, head_partner)
         kept.append(mine)
         sent.append(theirs)
+        if before:
+            theirs = lax.optimization_barrier((theirs,) + before)[0]
         received.append(lax.ppermute(theirs, "sec", swap_sec))
 
     up, down = features, features
@@ -397,24 +396,23 @@
         up = lax.ppermute(up, "dp", shift(1))
         down = lax.ppermute(down, "dp", shift(-1))
         blocks[step], blocks[z_size - step] = [down], [up]
+        if step == 1:
+            up, down, tiles = lax.optimization_barrier((up, down, tiles))
         if step == 2:
             up, down, kept[0] = lax.optimization_barrier((up, down, kept[0]))
-        if step == 3:
-            up, down, kept[1], received[0] = lax.optimization_barrier(
-                (up, down, kept[1], received[0])
-            )
         if step < far - 1:
             take(BATCHES[step - 1])
     blocks[far] = [
         lax.ppermute(up[:, :middle], "dp", shift(1)),
         lax.ppermute(down[:, middle:], "dp", shift(-1)),
     ]
-    blocks[far], tiles, received[1] = lax.optimization_barrier((blocks[far], tiles, received[1]))
+    blocks[far], received[0] = lax.optimization_barrier((blocks[far], received[0]))
+    take(BATCHES[2])
+    tiles = lax.optimization_barrier((tiles, kept[2], received[1]))[0]
     teacher = lax.all_to_all(
         tiles, "dp", split_axis=1, concat_axis=0, tiled=True, axis_index_groups=along
     ).reshape(lines, 2 * block_width)
-    take(BATCHES[2])
-    teacher, received[2] = lax.optimization_barrier((teacher, received[2]))
+    teacher = lax.optimization_barrier((teacher, received[2]))[0]
     teacher_across = lax.ppermute(teacher, "sec", swap_sec)
 
     chips = (z + jnp.array(PLACE, jnp.int32)) % z_size
@@ -454,7 +452,7 @@
     logits, table = stats_of(place, kept, received, taught, target[:, :, None], z_size)
     table = exchange(merge_of(exchange(table, "dp", along), 2 * vocab_size), ("sec", "vocab"))
 
-    held, _ = lax.optimization_barrier((tuple(kept), teacher_across))
+    held = lax.optimization_barrier((tuple(kept), received[2], teacher_across))[0]
     returned = [lax.ppermute(part, "sec", swap_sec) for part in held]
 
     every = jnp.arange(z_size, dtype=jnp.int32)

time: 246 us -> 243 us (0.988)
  waiting for transfers between devices: 77.6 us -> 85.1 us
  starting transfers between devices: 69.7 us -> 65.4 us
  local copies, waits for them, and re-layouts: 40.8 us -> 37.7 us
    all_to_all x5, starting transfers between devices: 31 us -> 24.5 us  [exchange(): lax.all_to_all(copies, axis, split_axis=0, concat_axis=0, tiled=True, axi...]
    all_to_all x1, waiting for transfers between devices: 0.01 us -> 4.19 us  [on_device(): lax.all_to_all(tiles, 'vocab', split_axis=2, concat_axis=1, tiled=True)]
    ppermute x3, waiting for transfers between devices: 4.12 us -> 0.01 us  [on_device(): up = lax.ppermute(up, 'dp', shift(1))]
    ppermute x3, waiting for transfers between devices: 6.42 us -> 9.86 us  [on_device(): returned = [lax.ppermute(part, 'sec', swap_sec) for part in held]]
    ppermute x3, waiting for transfers between devices: 17.4 us -> 14.4 us  [take(): received.append(lax.ppermute(theirs, 'sec', swap_sec))]
    ppermute x1, waiting for transfers between devices: 0.01 us -> 2.69 us  [on_device(): lax.ppermute(up[:, :middle], 'dp', shift(1))]
    unnamed x57 -> x73, local copies, waits for them, and re-layouts: 26.7 us -> 26 us
  transfers between devices with their start and end apart: 28 -> 28, of which waited for: 12 -> 14; matrix products, arithmetic and copies ran while one was open for 9% -> 8% of each run, Pallas kernels for 20% -> 20%
where the time goes in v3:
time: 243 us; the launch traced here: 242 us
  waiting for transfers between devices  85.1 us (35%)
  starting transfers between devices  65.4 us (27%)
  Pallas kernels  48.8 us (20%)
  local copies, waits for them, and re-layouts  37.7 us (16%)
  other arithmetic  3.21 us (1%)
    all_to_all x5, waiting for transfers between devices, exchange(): lax.all_to_all(copies, axis, split_axis=0, concat_axis=0, tiled=True, axi...  31.2 us
    unnamed x73, local copies, waits for them, and re-layouts  26 us
    all_to_all x5, starting transfers between devices, exchange(): lax.all_to_all(copies, axis, split_axis=0, concat_axis=0, tiled=True, axi...  24.5 us
    ppermute x1, waiting for transfers between devices, on_device(): teacher_across = lax.ppermute(teacher, 'sec', swap_sec)  16.5 us
    pallas_call x3, Pallas kernels, logits_of(): call(functools.partial(logits_kernel, tuple((len(block) for block in bloc...  14.7 us
    ppermute x3, waiting for transfers between devices, take(): received.append(lax.ppermute(theirs, 'sec', swap_sec))  14.4 us
    pallas_call x1, Pallas kernels, head_grad_of(): call(head_grad_kernel, 4 * lines * depth * columns, 4 * (lines * depth +...  11.6 us
    ppermute x3, starting transfers between devices, on_device(): down = lax.ppermute(down, 'dp', shift(-1))  10.1 us
  transfers between devices with their start and end apart: 28, of which 14 were waited for; matrix products, arithmetic and copies ran while one was open for 8% of the time, Pallas kernels for 20%

profile of v3, /device:TPU:10, one launch (start us, length us, event | category | flops | bytes accessed | tf_op | source)
XLA Modules:
  0.0 241.5 jit_solution(4741167127377800337)
XLA Ops:
  3.0 5.8 %all-to-all-start = ((bf16[8,48,320]{2,1,0:T(8,128)(2,1)}), bf16[8,48,320]{2,1,0:T(8,128)(2,1)S(1)}, u32[]{:S(2)}, u32[]{:S(2)}) async-start(bf16[8,48,320]{2,1,0:T(8,128)(2,1)} %broadcast_in_dim.15), calls=%async_computation | async-start | bytes 589824 | tf_op jit(solution)/shard_map/all_to_all | solution.py:342
  10.8 4.2 %all-to-all-done = bf16[8,48,320]{2,1,0:T(8,128)(2,1)S(1)} async-done(((bf16[8,48,320]{2,1,0:T(8,128)(2,1)}), bf16[8,48,320]{2,1,0:T(8,128)(2,1)S(1)}, u32[]{:S(2)}, u32[]{:S(2)}) %all-to-all-start) | async-done | bytes 245792 | tf_op jit(solution)/shard_map/all_to_all | solution.py:342
  16.9 5.5 %all-to-all-start.1 = ((bf16[24,2,8,1152]{3,1,0,2:T(2,128)(2,1)}), bf16[24,2,8,1152]{3,1,0,2:T(2,128)(2,1)S(1)}, u32[]{:S(2)}, u32[]{:S(2)}) async-start(bf16[24,2,8,1152]{3,1,0,2:T(2,128)(2,1)} %copy.22), calls=%async_computation.1 | async-start | bytes 1769472 | tf_op jit(solution)/shard_map/all_to_all | solution.py:379
  24.6 4.0 %collective-permute-start.1 = (bf16[48,2560]{1,0:T(8,128)(2,1)S(1)}, bf16[48,2560]{1,0:T(8,128)(2,1)S(1)}, u32[]{:S(2)}, u32[]{:S(2)}) collective-permute-start(bf16[48,2560]{1,0:T(8,128)(2,1)S(1)} %reshape.125.refs_0_), channel_id=1, source_target_pairs={{0,112},{8,120},{16,0},{24,8},{32,16},{40,24},{48,32},{56,40},{64,... | collective-permute-start | bytes 737288 | tf_op jit(solution)/shard_map/ppermute | solution.py:397
  30.0 4.2 %all-to-all-done.1 = bf16[24,2,8,1152]{3,1,0,2:T(2,128)(2,1)S(1)} async-done(((bf16[24,2,8,1152]{3,1,0,2:T(2,128)(2,1)}), bf16[24,2,8,1152]{3,1,0,2:T(2,128)(2,1)S(1)}, u32[]{:S(2)}, u32[]{:S(2)}) %all-to-all-start.1) | async-done | bytes 884768 | tf_op jit(solution)/shard_map/all_to_all | solution.py:379
  37.6 4.0 %collective-permute-start.3 = (bf16[48,2560]{1,0:T(8,128)(2,1)S(1)}, bf16[48,2560]{1,0:T(8,128)(2,1)S(1)}, u32[]{:S(2)}, u32[]{:S(2)}) collective-permute-start(bf16[48,2560]{1,0:T(8,128)(2,1)S(1)} %collective-permute-done.1.refs_1_), channel_id=1, source_target_pairs={{0,112},{8,120},{16,0},{24,8},{32,16},{40,24},{48,32},{56,40},{64,... | collective-permute-start | bytes 737288 | tf_op jit(solution)/shard_map/ppermute | solution.py:397
  41.6 2.7 %copy-done.1 = bf16[2560,1152]{1,0:T(8,128)(2,1)S(1)} copy-done((bf16[2560,1152]{1,0:T(8,128)(2,1)S(1)}, bf16[2560,1152]{1,0:T(8,128)(2,1)}, u32[]{:S(2)}) %copy-start.1) | copy-done | bytes 5898264
  44.3 4.9 %shard_map.102 = (f32[3,24,2304]{2,1,0:T(8,128)S(1)}, f32[3,24,2304]{2,1,0:T(8,128)S(1)}) custom-call(bf16[48,2560]{1,0:T(8,128)(2,1)S(1)} %reshape.125.refs_0_, bf16[48,2560]{1,0:T(8,128)(2,1)S(1)} %collective-permute-done.1.refs_1_, bf16[48,2560]{1,0:T(8,128)(2,1)S(1)} %collective-permute-done.refs_2_, bf16[2560,1152]{1,0:T(8,128)(2,1)S(1)} %copy-done.1, ...), custom_call_target="tpu_custom_call" | custom-call | flops 1698693120 | bytes 13123584 | tf_op jit(solution)/shard_map/pallas_call | solution.py:63
  53.4 2.7 %copy-done.2 = bf16[2560,1152]{1,0:T(8,128)(2,1)S(1)} copy-done((bf16[2560,1152]{1,0:T(8,128)(2,1)S(1)}, bf16[2560,1152]{1,0:T(8,128)(2,1)}, u32[]{:S(2)}) %copy-start.2) | copy-done | bytes 5898264
  56.1 4.8 %shard_map.103 = (f32[2,24,2304]{2,1,0:T(8,128)S(1)}, f32[2,24,2304]{2,1,0:T(8,128)S(1)}) custom-call(bf16[48,2560]{1,0:T(8,128)(2,1)S(1)} %collective-permute-done.3.refs_0_, bf16[48,2560]{1,0:T(8,128)(2,1)S(1)} %collective-permute-done.2.refs_1_, bf16[2560,1152]{1,0:T(8,128)(2,1)S(1)} %copy-done.2, ...), custom_call_target="tpu_custom_call" | custom-call | flops 1132462080 | bytes 12681216 | tf_op jit(solution)/shard_map/pallas_call | solution.py:63
  64.0 3.3 %collective-permute-start.8 = (bf16[48,1280]{1,0:T(8,128)(2,1)S(1)}, bf16[48,1280]{1,0:T(8,128)(2,1)S(1)}, u32[]{:S(2)}, u32[]{:S(2)}) collective-permute-start(bf16[48,1280]{1,0:T(8,128)(2,1)S(1)} %slice.51), channel_id=1, source_target_pairs={{0,112},{8,120},{16,0},{24,8},{32,16},{40,24},{48,32},{56,40},{64,... | collective-permute-start | bytes 368648 | tf_op jit(solution)/shard_map/ppermute | solution.py:407
  67.3 2.7 %collective-permute-done.7.refs_1_ = bf16[48,1280]{1,0:T(8,128)(2,1)S(1)} collective-permute-done((bf16[48,1280]{1,0:T(8,128)(2,1)S(1)}, bf16[48,1280]{1,0:T(8,128)(2,1)S(1)}, u32[]{:S(2)}, u32[]{:S(2)}) %collective-permute-start.7) | collective-permute-done | bytes 122912 | tf_op jit(solution)/shard_map/ppermute | solution.py:406
  70.0 5.1 %shard_map.104 = (f32[3,24,2304]{2,1,0:T(8,128)S(1)}, f32[3,24,2304]{2,1,0:T(8,128)S(1)}) custom-call(bf16[48,2560]{1,0:T(8,128)(2,1)S(1)} %collective-permute-done.5.refs_0_, bf16[48,1280]{1,0:T(8,128)(2,1)S(1)} %collective-permute-done.7.refs_1_, bf16[48,1280]{1,0:T(8,128)(2,1)S(1)} %collective-permute-done.8.refs_2_, ...), custom_call_target="tpu_custom_call" | custom-call | flops 1698693120 | bytes 13123584 | tf_op jit(solution)/shard_map/pallas_call | solution.py:63
  77.2 6.0 %all-to-all-start.2 = ((bf16[24,8,2304]{2,0,1:T(8,128)(2,1)}), bf16[24,8,2304]{2,0,1:T(8,128)(2,1)S(1)}, u32[]{:S(2)}, u32[]{:S(2)}) async-start(bf16[24,8,2304]{2,0,1:T(8,128)(2,1)} %reshape.126), calls=%async_computation.2 | async-start | bytes 1769472 | tf_op jit(solution)/shard_map/all_to_all | solution.py:412
  89.8 13.1 %collective-permute-done.11.refs_5_ = f32[3,24,2304]{2,1,0:T(8,128)S(1)} collective-permute-done((f32[3,24,2304]{2,1,0:T(8,128)}, f32[3,24,2304]{2,1,0:T(8,128)S(1)}, u32[]{:S(2)}, u32[]{:S(2)}) %collective-permute-start.11) | collective-permute-done | bytes 663584 | tf_op jit(solution)/shard_map/ppermute | solution.py:391
  103.8 2.4 %all-to-all-done.2 = bf16[24,8,2304]{2,0,1:T(8,128)(2,1)S(1)} async-done(((bf16[24,8,2304]{2,0,1:T(8,128)(2,1)}), bf16[24,8,2304]{2,0,1:T(8,128)(2,1)S(1)}, u32[]{:S(2)}, u32[]{:S(2)}) %all-to-all-start.2) | async-done | bytes 884768 | tf_op jit(solution)/shard_map/all_to_all | solution.py:412
  109.9 16.5 %collective-permute-done.12.b_ref = bf16[192,2304]{1,0:T(8,128)(2,1)S(1)} collective-permute-done((bf16[192,2304]{1,0:T(8,128)(2,1)S(1)}, bf16[192,2304]{1,0:T(8,128)(2,1)S(1)}, u32[]{:S(2)}, u32[]{:S(2)}) %collective-permute-start.12) | collective-permute-done | bytes 884768 | tf_op jit(solution)/shard_map/ppermute | solution.py:416
  134.0 4.5 %shard_map.105 = bf16[384,2304]{1,0:T(8,128)(2,1)S(1)} custom-call(s32[1,768]{1,0:T(1,128)S(1)} %broadcast_in_dim.17.order_ref, s32[384,1]{1,0:T(8,128)S(1)} %reshape.180.token_ref, bf16[192,2304]{1,0:T(8,128)(2,1)S(1)} %bitcast.30, bf16[192,2304]{1,0:T(8,128)(2,1)S(1)} %collective-permute-done.12.b_ref, ...), custom_call_target="tpu_custom_call" | custom-call | flops 1358954496 | bytes 5308416 | tf_op jit(solution)/shard_map/pallas_call | solution.py:95
  138.6 3.0 %shard_map.106 = (f32[8,24,2304]{2,1,0:T(8,128)S(1)}, f32[8,8,192]{2,1,0:T(8,128)}) custom-call(s32[2]{0:T(128)S(1)} %pad_add_fusion.2.z_ref.place_ref, f32[3,24,2304]{2,1,0:T(8,128)S(1)} %copy-done.10, f32[2,24,2304]{2,1,0:T(8,128)S(1)} %copy-done.22, f32[3,24,2304]{2,1,0:T(8,128)S(1)} %copy-done.16, f32[3,24,2304]{2,1,0:T(8,128)S(1)} %copy-done.12, ...), custom_call_target="tpu_custom_call" | custom-call | flops 8847360 | bytes 6193152 | tf_op jit(solution)/shard_map/pallas_call | solution.py:156
  142.8 3.6 %all-to-all-start.3 = ((f32[8,8,192]{2,1,0:T(8,128)}), f32[8,8,192]{2,1,0:T(8,128)S(1)}, u32[]{:S(2)}, u32[]{:S(2)}) async-start(f32[8,8,192]{2,1,0:T(8,128)} %get-tuple-element.57), calls=%async_computation.3 | async-start | bytes 131072 | tf_op jit(solution)/shard_map/all_to_all | solution.py:342
  146.6 8.1 %all-to-all-done.3.table_ref = f32[8,8,192]{2,1,0:T(8,128)S(1)} async-done(((f32[8,8,192]{2,1,0:T(8,128)}), f32[8,8,192]{2,1,0:T(8,128)S(1)}, u32[]{:S(2)}, u32[]{:S(2)}) %all-to-all-start.3) | async-done | bytes 49184 | tf_op jit(solution)/shard_map/all_to_all | solution.py:342
  155.5 5.8 %all-to-all-start.4 = ((f32[16,8,192]{2,1,0:T(8,128)}), f32[16,8,192]{2,1,0:T(8,128)S(1)}, u32[]{:S(2)}, u32[]{:S(2)}) async-start(f32[16,8,192]{2,1,0:T(8,128)} %shard_map.107), calls=%async_computation.4 | async-start | bytes 262144 | tf_op jit(solution)/shard_map/all_to_all | solution.py:342
  161.3 9.9 %collective-permute-done.16.refs_4_ = f32[2,24,2304]{2,1,0:T(8,128)} collective-permute-done((f32[2,24,2304]{2,1,0:T(8,128)}, f32[2,24,2304]{2,1,0:T(8,128)}, u32[]{:S(2)}, u32[]{:S(2)}) %collective-permute-start.16) | collective-permute-done | bytes 442400 | tf_op jit(solution)/shard_map/ppermute | solution.py:456
  175.1 3.2 %shard_map.108 = (bf16[8,48,1152]{2,1,0:T(8,128)(2,1)S(1)}, bf16[8,48,1152]{2,1,0:T(8,128)(2,1)S(1)}, f32[2,8,192]{2,1,0:T(8,128)S(1)}) custom-call(s32[2]{0:T(128)S(1)} %pad_add_fusion.2.z_ref.place_ref, f32[8,24,2304]{2,1,0:T(8,128)S(1)} %copy-done.6, f32[3,24,2304]{2,1,0:T(8,128)S(1)} %copy-done.8, f32[2,24,2304]{2,1,0:T(8,128)S(1)} %copy-done.20, ...), custom_call_target="tpu_custom_call" | custom-call | flops 8847360 | bytes 8847360 | tf_op jit(solution)/shard_map/pallas_call | solution.py:258
  178.3 2.7 %copy-done.3 = bf16[2560,1152]{1,0:T(8,128)(2,1)S(1)} copy-done((bf16[2560,1152]{1,0:T(8,128)(2,1)S(1)}, bf16[2560,1152]{1,0:T(8,128)(2,1)}, u32[]{:S(2)}) %copy-start.3) | copy-done | bytes 5898264
  180.9 9.5 %shard_map.109 = bf16[8,320,384]{2,1,0:T(8,128)(2,1)S(1)} custom-call(bf16[384,1152]{1,0:T(8,128)(2,1)S(1)} %bitcast.31, bf16[384,1152]{1,0:T(8,128)(2,1)S(1)} %bitcast.33, bf16[2560,1152]{1,0:T(8,128)(2,1)S(1)} %copy-done.3, bf16[2560,1152]{1,0:T(8,128)(2,1)} %collective-permute-done.4.refs_4_.refs_3_.refs_5_.partner_ref), custom_call_target="tpu_custom_call" | custom-call | flops 4529848320 | bytes 15532032 | tf_op jit(solution)/shard_map/pallas_call | solution.py:283
  193.6 5.8 %all-to-all-start.5 = ((bf16[8,320,384]{2,1,0:T(8,128)(2,1)}), bf16[8,320,384]{2,1,0:T(8,128)(2,1)S(1)}, u32[]{:S(2)}, u32[]{:S(2)}) async-start(bf16[8,320,384]{2,1,0:T(8,128)(2,1)} %copy-done.4), calls=%async_computation.5 | async-start | bytes 3932160 | tf_op jit(solution)/shard_map/all_to_all | solution.py:342
  199.4 2.6 %collective-permute-done.19 = bf16[8,48,1152]{2,1,0:T(8,128)(2,1)S(1)} collective-permute-done((bf16[8,48,1152]{2,1,0:T(8,128)(2,1)}, bf16[8,48,1152]{2,1,0:T(8,128)(2,1)S(1)}, u32[]{:S(2)}, u32[]{:S(2)}) %collective-permute-start.19) | collective-permute-done | bytes 884768 | tf_op jit(solution)/shard_map/ppermute | solution.py:369
  204.7 11.6 %shard_map.111 = bf16[2560,1152]{1,0:T(8,128)(2,1)} custom-call(bf16[384,2560]{1,0:T(8,128)(2,1)S(1)} %copy-done.26, bf16[384,2560]{1,0:T(8,128)(2,1)} %collective-permute-done.18.b_rows_ref, bf16[384,1152]{1,0:T(8,128)(2,1)S(1)} %bitcast.32, bf16[384,1152]{1,0:T(8,128)(2,1)S(1)} %bitcast.34), custom_call_target="tpu_custom_call" | custom-call | flops 4529848320 | bytes 11599872 | tf_op jit(solution)/shard_map/pallas_call | solution.py:330
  216.4 6.5 %all-to-all-done.5.parts_ref = bf16[8,320,384]{2,1,0:T(8,128)(2,1)S(1)} async-done(((bf16[8,320,384]{2,1,0:T(8,128)(2,1)}), bf16[8,320,384]{2,1,0:T(8,128)(2,1)S(1)}, u32[]{:S(2)}, u32[]{:S(2)}) %all-to-all-start.5) | async-done | bytes 1966112 | tf_op jit(solution)/shard_map/all_to_all | solution.py:342
  224.4 3.6 %all-to-all-start.6 = ((bf16[8,48,320]{2,1,0:T(8,128)(2,1)}), bf16[8,48,320]{2,1,0:T(8,128)(2,1)S(1)}, u32[]{:S(2)}, u32[]{:S(2)}) async-start(bf16[8,48,320]{2,1,0:T(8,128)(2,1)} %shard_map.110), calls=%async_computation.6 | async-start | bytes 589824 | tf_op jit(solution)/shard_map/all_to_all | solution.py:342
  229.8 11.0 %all-to-all-done.6 = bf16[8,48,320]{2,1,0:T(8,128)(2,1)S(1)} async-done(((bf16[8,48,320]{2,1,0:T(8,128)(2,1)}), bf16[8,48,320]{2,1,0:T(8,128)(2,1)S(1)}, u32[]{:S(2)}, u32[]{:S(2)}) %all-to-all-start.6) | async-done | bytes 245792 | tf_op jit(solution)/shard_map/all_to_all | solution.py:342
  (162 shorter events, 57.1 us)
Async XLA Ops:
  0.6 83.6 %copy-start = (s32[768]{0:T(1024)S(1)}, s32[768]{0:T(1024)}, u32[]{:S(2)}) copy-start(s32[768]{0:T(1024)} %param.12) | copy-start | bytes 9220
  0.6 41.0 %collective-permute-start.4 = (bf16[2560,1152]{1,0:T(8,128)(2,1)}, bf16[2560,1152]{1,0:T(8,128)(2,1)}, u32[]{:S(2)}, u32[]{:S(2)}) collective-permute-start(bf16[2560,1152]{1,0:T(8,128)(2,1)} %own_ref.1), channel_id=1, source_target_pairs={{0,8},{8,0},{16,24},{24,16},{32,40},{40,32},{48,56},{56,48},{64,72... | collective-permute-start | bytes 17694728 | tf_op jit(solution)/shard_map/ppermute | solution.py:369
  3.0 12.0 %all-to-all-start = ((bf16[8,48,320]{2,1,0:T(8,128)(2,1)}), bf16[8,48,320]{2,1,0:T(8,128)(2,1)S(1)}, u32[]{:S(2)}, u32[]{:S(2)}) async-start(bf16[8,48,320]{2,1,0:T(8,128)(2,1)} %broadcast_in_dim.15), calls=%async_computation | async-start | bytes 589824 | tf_op jit(solution)/shard_map/all_to_all | solution.py:342
  16.9 17.3 %all-to-all-start.1 = ((bf16[24,2,8,1152]{3,1,0,2:T(2,128)(2,1)}), bf16[24,2,8,1152]{3,1,0,2:T(2,128)(2,1)S(1)}, u32[]{:S(2)}, u32[]{:S(2)}) async-start(bf16[24,2,8,1152]{3,1,0,2:T(2,128)(2,1)} %copy.22), calls=%async_computation.1 | async-start | bytes 1769472 | tf_op jit(solution)/shard_map/all_to_all | solution.py:379
  22.6 13.0 %collective-permute-start = (bf16[48,2560]{1,0:T(8,128)(2,1)S(1)}, bf16[48,2560]{1,0:T(8,128)(2,1)S(1)}, u32[]{:S(2)}, u32[]{:S(2)}) collective-permute-start(bf16[48,2560]{1,0:T(8,128)(2,1)S(1)} %reshape.125.refs_0_), channel_id=1, source_target_pairs={{0,16},{8,24},{16,32},{24,40},{32,48},{40,56},{48,64},{56,72},{64,... | collective-permute-start | bytes 737288 | tf_op jit(solution)/shard_map/ppermute | solution.py:396
  24.6 11.0 %collective-permute-start.1 = (bf16[48,2560]{1,0:T(8,128)(2,1)S(1)}, bf16[48,2560]{1,0:T(8,128)(2,1)S(1)}, u32[]{:S(2)}, u32[]{:S(2)}) collective-permute-start(bf16[48,2560]{1,0:T(8,128)(2,1)S(1)} %reshape.125.refs_0_), channel_id=1, source_target_pairs={{0,112},{8,120},{16,0},{24,8},{32,16},{40,24},{48,32},{56,40},{64,... | collective-permute-start | bytes 737288 | tf_op jit(solution)/shard_map/ppermute | solution.py:397
  34.2 16.5 %copy-start.31 = (s32[768]{0:T(1024)S(1)}, s32[768]{0:T(1024)}, u32[]{:S(2)}) copy-start(s32[768]{0:T(1024)} %param.14) | copy-start | bytes 9220
  35.7 15.5 %collective-permute-start.2 = (bf16[48,2560]{1,0:T(8,128)(2,1)S(1)}, bf16[48,2560]{1,0:T(8,128)(2,1)S(1)}, u32[]{:S(2)}, u32[]{:S(2)}) collective-permute-start(bf16[48,2560]{1,0:T(8,128)(2,1)S(1)} %collective-permute-done.refs_2_), channel_id=1, source_target_pairs={{0,16},{8,24},{16,32},{24,40},{32,48},{40,56},{48,64},{56,72},{64,... | collective-permute-start | bytes 737288 | tf_op jit(solution)/shard_map/ppermute | solution.py:396
  37.6 13.6 %collective-permute-start.3 = (bf16[48,2560]{1,0:T(8,128)(2,1)S(1)}, bf16[48,2560]{1,0:T(8,128)(2,1)S(1)}, u32[]{:S(2)}, u32[]{:S(2)}) collective-permute-start(bf16[48,2560]{1,0:T(8,128)(2,1)S(1)} %collective-permute-done.1.refs_1_), channel_id=1, source_target_pairs={{0,112},{8,120},{16,0},{24,8},{32,16},{40,24},{48,32},{56,40},{64,... | collective-permute-start | bytes 737288 | tf_op jit(solution)/shard_map/ppermute | solution.py:397
  49.2 20.8 %collective-permute-start.9 = (f32[3,24,2304]{2,1,0:T(8,128)S(1)}, f32[3,24,2304]{2,1,0:T(8,128)S(1)}, u32[]{:S(2)}, u32[]{:S(2)}) collective-permute-start(f32[3,24,2304]{2,1,0:T(8,128)S(1)} %get-tuple-element.43.refs_0_), channel_id=1, source_target_pairs={{0,128},{128,0},{1,129},{129,1},{2,130},{130,2},{3,131},{131,3},{4... | collective-permute-start | bytes 1990664 | tf_op jit(solution)/shard_map/ppermute | solution.py:391
  51.3 12.7 %collective-permute-start.5 = (bf16[48,2560]{1,0:T(8,128)(2,1)S(1)}, bf16[48,2560]{1,0:T(8,128)(2,1)S(1)}, u32[]{:S(2)}, u32[]{:S(2)}) collective-permute-start(bf16[48,2560]{1,0:T(8,128)(2,1)S(1)} %collective-permute-done.3.refs_0_), channel_id=1, source_target_pairs={{0,112},{8,120},{16,0},{24,8},{32,16},{40,24},{48,32},{56,40},{64,... | collective-permute-start | bytes 737288 | tf_op jit(solution)/shard_map/ppermute | solution.py:397
  53.3 10.6 %collective-permute-start.6 = (bf16[48,2560]{1,0:T(8,128)(2,1)S(1)}, bf16[48,2560]{1,0:T(8,128)(2,1)S(1)}, u32[]{:S(2)}, u32[]{:S(2)}) collective-permute-start(bf16[48,2560]{1,0:T(8,128)(2,1)S(1)} %collective-permute-done.2.refs_1_), channel_id=1, source_target_pairs={{0,16},{8,24},{16,32},{24,40},{32,48},{40,56},{48,64},{56,72},{64,... | collective-permute-start | bytes 737288 | tf_op jit(solution)/shard_map/ppermute | solution.py:396
  61.6 14.8 %collective-permute-start.10 = (f32[2,24,2304]{2,1,0:T(8,128)S(1)}, f32[2,24,2304]{2,1,0:T(8,128)S(1)}, u32[]{:S(2)}, u32[]{:S(2)}) collective-permute-start(f32[2,24,2304]{2,1,0:T(8,128)S(1)} %get-tuple-element.48.refs_1_), channel_id=1, source_target_pairs={{0,128},{128,0},{1,129},{129,1},{2,130},{130,2},{3,131},{131,3},{4... | collective-permute-start | bytes 1327112 | tf_op jit(solution)/shard_map/ppermute | solution.py:391
  63.8 6.2 %collective-permute-start.7 = (bf16[48,1280]{1,0:T(8,128)(2,1)S(1)}, bf16[48,1280]{1,0:T(8,128)(2,1)S(1)}, u32[]{:S(2)}, u32[]{:S(2)}) collective-permute-start(bf16[48,1280]{1,0:T(8,128)(2,1)S(1)} %slice.50), channel_id=1, source_target_pairs={{0,16},{8,24},{16,32},{24,40},{32,48},{40,56},{48,64},{56,72},{64,... | collective-permute-start | bytes 368648 | tf_op jit(solution)/shard_map/ppermute | solution.py:406
  64.0 6.1 %collective-permute-start.8 = (bf16[48,1280]{1,0:T(8,128)(2,1)S(1)}, bf16[48,1280]{1,0:T(8,128)(2,1)S(1)}, u32[]{:S(2)}, u32[]{:S(2)}) collective-permute-start(bf16[48,1280]{1,0:T(8,128)(2,1)S(1)} %slice.51), channel_id=1, source_target_pairs={{0,112},{8,120},{16,0},{24,8},{32,16},{40,24},{48,32},{56,40},{64,... | collective-permute-start | bytes 368648 | tf_op jit(solution)/shard_map/ppermute | solution.py:407
  77.2 29.1 %all-to-all-start.2 = ((bf16[24,8,2304]{2,0,1:T(8,128)(2,1)}), bf16[24,8,2304]{2,0,1:T(8,128)(2,1)S(1)}, u32[]{:S(2)}, u32[]{:S(2)}) async-start(bf16[24,8,2304]{2,0,1:T(8,128)(2,1)} %reshape.126), calls=%async_computation.2 | async-start | bytes 1769472 | tf_op jit(solution)/shard_map/all_to_all | solution.py:412
  87.0 15.9 %collective-permute-start.11 = (f32[3,24,2304]{2,1,0:T(8,128)}, f32[3,24,2304]{2,1,0:T(8,128)S(1)}, u32[]{:S(2)}, u32[]{:S(2)}) collective-permute-start(f32[3,24,2304]{2,1,0:T(8,128)} %copy-done.13), channel_id=1, source_target_pairs={{0,128},{128,0},{1,129},{129,1},{2,130},{130,2},{3,131},{131,3},{4... | collective-permute-start | bytes 1990664 | tf_op jit(solution)/shard_map/ppermute | solution.py:391
  106.2 20.2 %collective-permute-start.12 = (bf16[192,2304]{1,0:T(8,128)(2,1)S(1)}, bf16[192,2304]{1,0:T(8,128)(2,1)S(1)}, u32[]{:S(2)}, u32[]{:S(2)}) collective-permute-start(bf16[192,2304]{1,0:T(8,128)(2,1)S(1)} %bitcast.28), channel_id=1, source_target_pairs={{0,128},{128,0},{1,129},{129,1},{2,130},{130,2},{3,131},{131,3},{4... | collective-permute-start | bytes 2654216 | tf_op jit(solution)/shard_map/ppermute | solution.py:416
  109.9 22.3 %collective-permute-start.13 = (bf16[192,2304]{1,0:T(8,128)(2,1)S(1)}, bf16[192,2304]{1,0:T(8,128)(2,1)S(1)}, u32[]{:S(2)}, u32[]{:S(2)}) collective-permute-start(bf16[192,2304]{1,0:T(8,128)(2,1)S(1)} %bitcast.29), channel_id=1, source_target_pairs={{0,8},{8,0},{16,24},{24,16},{32,40},{40,32},{48,56},{56,48},{64,72... | collective-permute-start | bytes 2654216 | tf_op jit(solution)/shard_map/ppermute | solution.py:369
  126.4 7.6 %collective-permute-start.14 = (bf16[192,2304]{1,0:T(8,128)(2,1)S(1)}, bf16[192,2304]{1,0:T(8,128)(2,1)S(1)}, u32[]{:S(2)}, u32[]{:S(2)}) collective-permute-start(bf16[192,2304]{1,0:T(8,128)(2,1)S(1)} %collective-permute-done.12.b_ref), channel_id=1, source_target_pairs={{0,8},{8,0},{16,24},{24,16},{32,40},{40,32},{48,56},{56,48},{64,72... | collective-permute-start | bytes 2654216 | tf_op jit(solution)/shard_map/ppermute | solution.py:369
  127.8 43.3 %collective-permute-start.15 = (f32[3,24,2304]{2,1,0:T(8,128)}, f32[3,24,2304]{2,1,0:T(8,128)}, u32[]{:S(2)}, u32[]{:S(2)}) collective-permute-start(f32[3,24,2304]{2,1,0:T(8,128)} %copy-done.9), channel_id=1, source_target_pairs={{0,128},{128,0},{1,129},{129,1},{2,130},{130,2},{3,131},{131,3},{4... | collective-permute-start | bytes 1990664 | tf_op jit(solution)/shard_map/ppermute | solution.py:456
  129.5 41.6 %collective-permute-start.17 = (f32[3,24,2304]{2,1,0:T(8,128)}, f32[3,24,2304]{2,1,0:T(8,128)}, u32[]{:S(2)}, u32[]{:S(2)}) collective-permute-start(f32[3,24,2304]{2,1,0:T(8,128)} %copy-done.15), channel_id=1, source_target_pairs={{0,128},{128,0},{1,129},{129,1},{2,130},{130,2},{3,131},{131,3},{4... | collective-permute-start | bytes 1990664 | tf_op jit(solution)/shard_map/ppermute | solution.py:456
  132.1 67.3 %collective-permute-start.18 = (bf16[384,2560]{1,0:T(8,128)(2,1)}, bf16[384,2560]{1,0:T(8,128)(2,1)}, u32[]{:S(2)}, u32[]{:S(2)}) collective-permute-start(bf16[384,2560]{1,0:T(8,128)(2,1)} %constant_dynamic-update-slice_fusion.a_rows_ref), channel_id=1, source_target_pairs={{0,8},{8,0},{16,24},{24,16},{32,40},{40,32},{48,56},{56,48},{64,72... | collective-permute-start | bytes 5898248 | tf_op jit(solution)/shard_map/ppermute | solution.py:369
  132.2 38.9 %collective-permute-start.16 = (f32[2,24,2304]{2,1,0:T(8,128)}, f32[2,24,2304]{2,1,0:T(8,128)}, u32[]{:S(2)}, u32[]{:S(2)}) collective-permute-start(f32[2,24,2304]{2,1,0:T(8,128)} %copy-done.21), channel_id=1, source_target_pairs={{0,128},{128,0},{1,129},{129,1},{2,130},{130,2},{3,131},{131,3},{4... | collective-permute-start | bytes 1327112 | tf_op jit(solution)/shard_map/ppermute | solution.py:456
  138.6 33.9 %copy-start.8 = (f32[3,24,2304]{2,1,0:T(8,128)S(1)}, f32[3,24,2304]{2,1,0:T(8,128)}, u32[]{:S(2)}) copy-start(f32[3,24,2304]{2,1,0:T(8,128)} %copy-done.7) | copy-start | bytes 1990660
  138.6 33.9 %copy-start.20 = (f32[2,24,2304]{2,1,0:T(8,128)S(1)}, f32[2,24,2304]{2,1,0:T(8,128)}, u32[]{:S(2)}) copy-start(f32[2,24,2304]{2,1,0:T(8,128)} %copy-done.19) | copy-start | bytes 1327108
  142.8 11.9 %all-to-all-start.3 = ((f32[8,8,192]{2,1,0:T(8,128)}), f32[8,8,192]{2,1,0:T(8,128)S(1)}, u32[]{:S(2)}, u32[]{:S(2)}) async-start(f32[8,8,192]{2,1,0:T(8,128)} %get-tuple-element.57), calls=%async_computation.3 | async-start | bytes 131072 | tf_op jit(solution)/shard_map/all_to_all | solution.py:342
  155.5 17.0 %all-to-all-start.4 = ((f32[16,8,192]{2,1,0:T(8,128)}), f32[16,8,192]{2,1,0:T(8,128)S(1)}, u32[]{:S(2)}, u32[]{:S(2)}) async-start(f32[16,8,192]{2,1,0:T(8,128)} %shard_map.107), calls=%async_computation.4 | async-start | bytes 262144 | tf_op jit(solution)/shard_map/all_to_all | solution.py:342
  193.6 29.2 %all-to-all-start.5 = ((bf16[8,320,384]{2,1,0:T(8,128)(2,1)}), bf16[8,320,384]{2,1,0:T(8,128)(2,1)S(1)}, u32[]{:S(2)}, u32[]{:S(2)}) async-start(bf16[8,320,384]{2,1,0:T(8,128)(2,1)} %copy-done.4), calls=%async_computation.5 | async-start | bytes 3932160 | tf_op jit(solution)/shard_map/all_to_all | solution.py:342
  199.4 2.6 %collective-permute-start.19 = (bf16[8,48,1152]{2,1,0:T(8,128)(2,1)}, bf16[8,48,1152]{2,1,0:T(8,128)(2,1)S(1)}, u32[]{:S(2)}, u32[]{:S(2)}) collective-permute-start(bf16[8,48,1152]{2,1,0:T(8,128)(2,1)} %copy-done.29), channel_id=1, source_target_pairs={{0,8},{8,0},{16,24},{24,16},{32,40},{40,32},{48,56},{56,48},{64,72... | collective-permute-start | bytes 2654216 | tf_op jit(solution)/shard_map/ppermute | solution.py:369
  224.4 16.4 %all-to-all-start.6 = ((bf16[8,48,320]{2,1,0:T(8,128)(2,1)}), bf16[8,48,320]{2,1,0:T(8,128)(2,1)S(1)}, u32[]{:S(2)}, u32[]{:S(2)}) async-start(bf16[8,48,320]{2,1,0:T(8,128)(2,1)} %shard_map.110), calls=%async_computation.6 | async-start | bytes 589824 | tf_op jit(solution)/shard_map/all_to_all | solution.py:342
  228.0 1.2 collective-permute-start.20
  (29 other events, 115.0 us)

commit v4 on v3

--- a/solution.py
+++ b/solution.py
@@ -205,8 +205,8 @@
 
 def grad_kernel(place_ref, logits_ref, *refs):
     count = len(BATCHES)
-    sent, received = refs[:count], refs[count : 2 * count]
-    teacher_ref, table_ref, weight_ref, own_ref, partner_ref, rows_ref, columns_ref = refs[2 * count :]
+    sent, received_ref = refs[:count], refs[count]
+    teacher_ref, table_ref, weight_ref, own_ref, partner_ref, rows_ref, columns_ref = refs[count + 1 :]
     cut, columns = logits_ref.shape[1:]
     lines = cut * len(PLACE)
     padded = columns_ref.shape[1]
@@ -243,7 +243,7 @@
             at = pl.ds(pl.multiple_of(chip * cut, 8), cut)
             teacher = teacher_ref[place].astype(F32)
             mine = grad(logits_ref[place], teacher[:cut], columns_ref[0, at, :])
-            theirs = grad(sent[b][i] + received[b][i], teacher[cut:], columns_ref[1, at, :])
+            theirs = grad(sent[b][i] + received_ref[place], teacher[cut:], columns_ref[1, at, :])
             both = jnp.concatenate([mine, theirs], axis=0).astype(BF16)
             own_ref[place] = both[:, : columns // 2]
             partner_ref[place] = both[:, columns // 2 :]
@@ -259,11 +259,11 @@
         grad_kernel,
         20 * lines * columns,
         20 * lines * columns,
-        in_specs=[pl.BlockSpec(memory_space=pltpu.SMEM)] + in_vmem(2 * len(BATCHES) + 4),
+        in_specs=[pl.BlockSpec(memory_space=pltpu.SMEM)] + in_vmem(len(BATCHES) + 5),
         out_specs=in_vmem(3),
         out_shape=[half, half, jax.ShapeDtypeStruct((2, 8, lines), F32)],
         scratch_shapes=[pltpu.VMEM((2, padded, 128), F32)],
-    )(place, logits, *sent, *received, teacher, table, weight)
+    )(place, logits, *sent, received, teacher, table, weight)
 
 
 def terms_kernel(own_grad_ref, partner_grad_ref, own_ref, partner_ref, out_ref):
@@ -452,8 +452,9 @@
     logits, table = stats_of(place, kept, received, taught, target[:, :, None], z_size)
     table = exchange(merge_of(exchange(table, "dp", along), 2 * vocab_size), ("sec", "vocab"))
 
-    held = lax.optimization_barrier((tuple(kept), received[2], teacher_across))[0]
-    returned = [lax.ppermute(part, "sec", swap_sec) for part in held]
+    held = lax.optimization_barrier(jnp.concatenate(kept, axis=0))
+    held = lax.optimization_barrier((held, received[2], teacher_across))[0]
+    returned = lax.ppermute(held, "sec", swap_sec)
 
     every = jnp.arange(z_size, dtype=jnp.int32)
     weight = jnp.stack(

time: 243 us -> 238 us (0.979)
  waiting for transfers between devices: 85.1 us -> 78.4 us
    ppermute x3 -> x1, waiting for transfers between devices: 9.86 us -> 0.01 us  [on_device(): returned = lax.ppermute(held, 'sec', swap_sec)]
    all_to_all x5, waiting for transfers between devices: 31.2 us -> 35.8 us  [exchange(): lax.all_to_all(copies, axis, split_axis=0, concat_axis=0, tiled=True, axi...]
    ppermute x3 -> x1, starting transfers between devices: 5.29 us -> 1.32 us  [on_device(): returned = lax.ppermute(held, 'sec', swap_sec)]
    unnamed x73 -> x77, local copies, waits for them, and re-layouts: 26 us -> 25.4 us
  transfers between devices with their start and end apart: 28 -> 26, of which waited for: 14 -> 14; matrix products, arithmetic and copies ran while one was open for 8% -> 10% of each run, Pallas kernels for 20% -> 21%
where the time goes in v4:
time: 238 us; the launch traced here: 236 us
  waiting for transfers between devices  78.4 us (33%)
  starting transfers between devices  63.8 us (27%)
  Pallas kernels  50.9 us (21%)
  local copies, waits for them, and re-layouts  37.1 us (16%)
  other arithmetic  4.6 us (2%)
    all_to_all x5, waiting for transfers between devices, exchange(): lax.all_to_all(copies, axis, split_axis=0, concat_axis=0, tiled=True, axi...  35.8 us
    all_to_all x5, starting transfers between devices, exchange(): lax.all_to_all(copies, axis, split_axis=0, concat_axis=0, tiled=True, axi...  26.8 us
    unnamed x77, local copies, waits for them, and re-layouts  25.4 us
    pallas_call x3, Pallas kernels, logits_of(): call(functools.partial(logits_kernel, tuple((len(block) for block in bloc...  15.5 us
    ppermute x1, waiting for transfers between devices, on_device(): teacher_across = lax.ppermute(teacher, 'sec', swap_sec)  14.8 us
    ppermute x3, waiting for transfers between devices, take(): received.append(lax.ppermute(theirs, 'sec', swap_sec))  13.8 us
    pallas_call x1, Pallas kernels, head_grad_of(): call(head_grad_kernel, 4 * lines * depth * columns, 4 * (lines * depth +...  12.1 us
    ppermute x3, starting transfers between devices, on_device(): down = lax.ppermute(down, 'dp', shift(-1))  10.1 us
  transfers between devices with their start and end apart: 26, of which 14 were waited for; matrix products, arithmetic and copies ran while one was open for 10% of the time, Pallas kernels for 21%

profile of v4, /device:TPU:10, one launch (start us, length us, event | category | flops | bytes accessed | tf_op | source)
XLA Modules:
  0.0 236.1 jit_solution(6885425365964818333)
XLA Ops:
  3.0 5.8 %all-to-all-start = ((bf16[8,48,320]{2,1,0:T(8,128)(2,1)}), bf16[8,48,320]{2,1,0:T(8,128)(2,1)S(1)}, u32[]{:S(2)}, u32[]{:S(2)}) async-start(bf16[8,48,320]{2,1,0:T(8,128)(2,1)} %broadcast_in_dim.15), calls=%async_computation | async-start | bytes 589824 | tf_op jit(solution)/shard_map/all_to_all | solution.py:342
  10.8 4.2 %all-to-all-done = bf16[8,48,320]{2,1,0:T(8,128)(2,1)S(1)} async-done(((bf16[8,48,320]{2,1,0:T(8,128)(2,1)}), bf16[8,48,320]{2,1,0:T(8,128)(2,1)S(1)}, u32[]{:S(2)}, u32[]{:S(2)}) %all-to-all-start) | async-done | bytes 245792 | tf_op jit(solution)/shard_map/all_to_all | solution.py:342
  16.9 5.5 %all-to-all-start.1 = ((bf16[24,2,8,1152]{3,1,0,2:T(2,128)(2,1)}), bf16[24,2,8,1152]{3,1,0,2:T(2,128)(2,1)S(1)}, u32[]{:S(2)}, u32[]{:S(2)}) async-start(bf16[24,2,8,1152]{3,1,0,2:T(2,128)(2,1)} %copy.22), calls=%async_computation.1 | async-start | bytes 1769472 | tf_op jit(solution)/shard_map/all_to_all | solution.py:379
  24.6 4.0 %collective-permute-start.1 = (bf16[48,2560]{1,0:T(8,128)(2,1)S(1)}, bf16[48,2560]{1,0:T(8,128)(2,1)S(1)}, u32[]{:S(2)}, u32[]{:S(2)}) collective-permute-start(bf16[48,2560]{1,0:T(8,128)(2,1)S(1)} %reshape.125.refs_0_), channel_id=1, source_target_pairs={{0,112},{8,120},{16,0},{24,8},{32,16},{40,24},{48,32},{56,40},{64,... | collective-permute-start | bytes 737288 | tf_op jit(solution)/shard_map/ppermute | solution.py:397
  30.0 4.2 %all-to-all-done.1 = bf16[24,2,8,1152]{3,1,0,2:T(2,128)(2,1)S(1)} async-done(((bf16[24,2,8,1152]{3,1,0,2:T(2,128)(2,1)}), bf16[24,2,8,1152]{3,1,0,2:T(2,128)(2,1)S(1)}, u32[]{:S(2)}, u32[]{:S(2)}) %all-to-all-start.1) | async-done | bytes 884768 | tf_op jit(solution)/shard_map/all_to_all | solution.py:379
  37.7 4.0 %collective-permute-start.3 = (bf16[48,2560]{1,0:T(8,128)(2,1)S(1)}, bf16[48,2560]{1,0:T(8,128)(2,1)S(1)}, u32[]{:S(2)}, u32[]{:S(2)}) collective-permute-start(bf16[48,2560]{1,0:T(8,128)(2,1)S(1)} %collective-permute-done.1.refs_1_), channel_id=1, source_target_pairs={{0,112},{8,120},{16,0},{24,8},{32,16},{40,24},{48,32},{56,40},{64,... | collective-permute-start | bytes 737288 | tf_op jit(solution)/shard_map/ppermute | solution.py:397
  41.7 2.7 %copy-done.1 = bf16[2560,1152]{1,0:T(8,128)(2,1)S(1)} copy-done((bf16[2560,1152]{1,0:T(8,128)(2,1)S(1)}, bf16[2560,1152]{1,0:T(8,128)(2,1)}, u32[]{:S(2)}) %copy-start.1) | copy-done | bytes 5898264
  44.4 5.8 %shard_map.102 = (f32[3,24,2304]{2,1,0:T(8,128)S(1)}, f32[3,24,2304]{2,1,0:T(8,128)}) custom-call(bf16[48,2560]{1,0:T(8,128)(2,1)S(1)} %reshape.125.refs_0_, bf16[48,2560]{1,0:T(8,128)(2,1)S(1)} %collective-permute-done.1.refs_1_, bf16[48,2560]{1,0:T(8,128)(2,1)S(1)} %collective-permute-done.refs_2_, bf16[2560,1152]{1,0:T(8,128)(2,1)S(1)} %copy-done.1, ...), custom_call_target="tpu_custom_call" | custom-call | flops 1698693120 | bytes 13123584 | tf_op jit(solution)/shard_map/pallas_call | solution.py:63
  54.3 2.7 %copy-done.2 = bf16[2560,1152]{1,0:T(8,128)(2,1)S(1)} copy-done((bf16[2560,1152]{1,0:T(8,128)(2,1)S(1)}, bf16[2560,1152]{1,0:T(8,128)(2,1)}, u32[]{:S(2)}) %copy-start.2) | copy-done | bytes 5898264
  57.0 4.8 %shard_map.103 = (f32[2,24,2304]{2,1,0:T(8,128)S(1)}, f32[2,24,2304]{2,1,0:T(8,128)S(1)}) custom-call(bf16[48,2560]{1,0:T(8,128)(2,1)S(1)} %collective-permute-done.3.refs_0_, bf16[48,2560]{1,0:T(8,128)(2,1)S(1)} %collective-permute-done.2.refs_1_, bf16[2560,1152]{1,0:T(8,128)(2,1)S(1)} %copy-done.2, ...), custom_call_target="tpu_custom_call" | custom-call | flops 1132462080 | bytes 12681216 | tf_op jit(solution)/shard_map/pallas_call | solution.py:63
  61.9 2.4 %collective-permute-start.10 = (f32[2,24,2304]{2,1,0:T(8,128)S(1)}, f32[2,24,2304]{2,1,0:T(8,128)S(1)}, u32[]{:S(2)}, u32[]{:S(2)}) collective-permute-start(f32[2,24,2304]{2,1,0:T(8,128)S(1)} %get-tuple-element.46.refs_1_), channel_id=1, source_target_pairs={{0,128},{128,0},{1,129},{129,1},{2,130},{130,2},{3,131},{131,3},{4... | collective-permute-start | bytes 1327112 | tf_op jit(solution)/shard_map/ppermute | solution.py:391
  64.4 3.3 %collective-permute-start.8 = (bf16[48,1280]{1,0:T(8,128)(2,1)S(1)}, bf16[48,1280]{1,0:T(8,128)(2,1)S(1)}, u32[]{:S(2)}, u32[]{:S(2)}) collective-permute-start(bf16[48,1280]{1,0:T(8,128)(2,1)S(1)} %slice.51), channel_id=1, source_target_pairs={{0,112},{8,120},{16,0},{24,8},{32,16},{40,24},{48,32},{56,40},{64,... | collective-permute-start | bytes 368648 | tf_op jit(solution)/shard_map/ppermute | solution.py:407
  67.8 2.7 %collective-permute-done.7.refs_1_ = bf16[48,1280]{1,0:T(8,128)(2,1)S(1)} collective-permute-done((bf16[48,1280]{1,0:T(8,128)(2,1)S(1)}, bf16[48,1280]{1,0:T(8,128)(2,1)S(1)}, u32[]{:S(2)}, u32[]{:S(2)}) %collective-permute-start.7) | collective-permute-done | bytes 122912 | tf_op jit(solution)/shard_map/ppermute | solution.py:406
  70.5 4.9 %shard_map.104 = (f32[3,24,2304]{2,1,0:T(8,128)S(1)}, f32[3,24,2304]{2,1,0:T(8,128)S(1)}) custom-call(bf16[48,2560]{1,0:T(8,128)(2,1)S(1)} %collective-permute-done.5.refs_0_, bf16[48,1280]{1,0:T(8,128)(2,1)S(1)} %collective-permute-done.7.refs_1_, bf16[48,1280]{1,0:T(8,128)(2,1)S(1)} %collective-permute-done.8.refs_2_, ...), custom_call_target="tpu_custom_call" | custom-call | flops 1698693120 | bytes 13123584 | tf_op jit(solution)/shard_map/pallas_call | solution.py:63
  78.3 5.5 %all-to-all-start.2 = ((bf16[24,8,2304]{2,0,1:T(8,128)(2,1)}), bf16[24,8,2304]{2,0,1:T(8,128)(2,1)S(1)}, u32[]{:S(2)}, u32[]{:S(2)}) async-start(bf16[24,8,2304]{2,0,1:T(8,128)(2,1)} %reshape.126), calls=%async_computation.2 | async-start | bytes 1769472 | tf_op jit(solution)/shard_map/all_to_all | solution.py:412
  91.4 12.6 %collective-permute-done.11.refs_5_ = f32[3,24,2304]{2,1,0:T(8,128)S(1)} collective-permute-done((f32[3,24,2304]{2,1,0:T(8,128)}, f32[3,24,2304]{2,1,0:T(8,128)S(1)}, u32[]{:S(2)}, u32[]{:S(2)}) %collective-permute-start.11) | collective-permute-done | bytes 663584 | tf_op jit(solution)/shard_map/ppermute | solution.py:391
  113.4 14.8 %collective-permute-done.12.b_ref = bf16[192,2304]{1,0:T(8,128)(2,1)S(1)} collective-permute-done((bf16[192,2304]{1,0:T(8,128)(2,1)S(1)}, bf16[192,2304]{1,0:T(8,128)(2,1)S(1)}, u32[]{:S(2)}, u32[]{:S(2)}) %collective-permute-start.12) | collective-permute-done | bytes 884768 | tf_op jit(solution)/shard_map/ppermute | solution.py:416
  134.0 4.5 %shard_map.105 = bf16[384,2304]{1,0:T(8,128)(2,1)S(1)} custom-call(s32[1,768]{1,0:T(1,128)S(1)} %broadcast_in_dim.17.order_ref, s32[384,1]{1,0:T(8,128)S(1)} %reshape.180.token_ref, bf16[192,2304]{1,0:T(8,128)(2,1)S(1)} %bitcast.30, bf16[192,2304]{1,0:T(8,128)(2,1)S(1)} %collective-permute-done.12.b_ref, ...), custom_call_target="tpu_custom_call" | custom-call | flops 1358954496 | bytes 5308416 | tf_op jit(solution)/shard_map/pallas_call | solution.py:95
  138.5 3.7 %shard_map.106 = (f32[8,24,2304]{2,1,0:T(8,128)S(1)}, f32[8,8,192]{2,1,0:T(8,128)}) custom-call(s32[2]{0:T(128)S(1)} %pad_add_fusion.2.z_ref.place_ref, f32[3,24,2304]{2,1,0:T(8,128)S(1)} %get-tuple-element.37.refs_0_, f32[2,24,2304]{2,1,0:T(8,128)S(1)} %copy-done.10, f32[3,24,2304]{2,1,0:T(8,128)S(1)} %copy-done.5, ...), custom_call_target="tpu_custom_call" | custom-call | flops 8847360 | bytes 6193152 | tf_op jit(solution)/shard_map/pallas_call | solution.py:156
  143.4 3.4 %all-to-all-start.3 = ((f32[8,8,192]{2,1,0:T(8,128)}), f32[8,8,192]{2,1,0:T(8,128)S(1)}, u32[]{:S(2)}, u32[]{:S(2)}) async-start(f32[8,8,192]{2,1,0:T(8,128)} %get-tuple-element.53), calls=%async_computation.3 | async-start | bytes 131072 | tf_op jit(solution)/shard_map/all_to_all | solution.py:342
  147.0 8.1 %all-to-all-done.3.table_ref = f32[8,8,192]{2,1,0:T(8,128)S(1)} async-done(((f32[8,8,192]{2,1,0:T(8,128)}), f32[8,8,192]{2,1,0:T(8,128)S(1)}, u32[]{:S(2)}, u32[]{:S(2)}) %all-to-all-start.3) | async-done | bytes 49184 | tf_op jit(solution)/shard_map/all_to_all | solution.py:342
  155.8 6.1 %all-to-all-start.4 = ((f32[16,8,192]{2,1,0:T(8,128)}), f32[16,8,192]{2,1,0:T(8,128)S(1)}, u32[]{:S(2)}, u32[]{:S(2)}) async-start(f32[16,8,192]{2,1,0:T(8,128)} %shard_map.107), calls=%async_computation.4 | async-start | bytes 262144 | tf_op jit(solution)/shard_map/all_to_all | solution.py:342
  162.0 7.4 %all-to-all-done.4.refs_5_ = f32[16,8,192]{2,1,0:T(8,128)S(1)} async-done(((f32[16,8,192]{2,1,0:T(8,128)}), f32[16,8,192]{2,1,0:T(8,128)S(1)}, u32[]{:S(2)}, u32[]{:S(2)}) %all-to-all-start.4) | async-done | bytes 98336 | tf_op jit(solution)/shard_map/all_to_all | solution.py:342
  171.9 3.4 %shard_map.108 = (bf16[8,48,1152]{2,1,0:T(8,128)(2,1)S(1)}, bf16[8,48,1152]{2,1,0:T(8,128)(2,1)S(1)}, f32[2,8,192]{2,1,0:T(8,128)S(1)}) custom-call(s32[2]{0:T(128)S(1)} %pad_add_fusion.2.z_ref.place_ref, f32[8,24,2304]{2,1,0:T(8,128)S(1)} %copy-done.8, f32[3,24,2304]{2,1,0:T(8,128)} %get-tuple-element.41.refs_0_, f32[2,24,2304]{2,1,0:T(8,128)S(1)} %copy-done.27, ...), custom_call_target="tpu_custom_call" | custom-call | flops 8847360 | bytes 8847360 | tf_op jit(solution)/shard_map/pallas_call | solution.py:258
  175.3 2.7 %copy-done.3 = bf16[2560,1152]{1,0:T(8,128)(2,1)S(1)} copy-done((bf16[2560,1152]{1,0:T(8,128)(2,1)S(1)}, bf16[2560,1152]{1,0:T(8,128)(2,1)}, u32[]{:S(2)}) %copy-start.3) | copy-done | bytes 5898264
  178.0 9.5 %shard_map.109 = bf16[8,320,384]{2,1,0:T(8,128)(2,1)S(1)} custom-call(bf16[384,1152]{1,0:T(8,128)(2,1)S(1)} %bitcast.31, bf16[384,1152]{1,0:T(8,128)(2,1)S(1)} %bitcast.33, bf16[2560,1152]{1,0:T(8,128)(2,1)S(1)} %copy-done.3, bf16[2560,1152]{1,0:T(8,128)(2,1)} %collective-permute-done.4.refs_4_.refs_3_.refs_5_.partner_ref), custom_call_target="tpu_custom_call" | custom-call | flops 4529848320 | bytes 15532032 | tf_op jit(solution)/shard_map/pallas_call | solution.py:283
  189.7 5.7 %all-to-all-start.5 = ((bf16[8,320,384]{2,1,0:T(8,128)(2,1)}), bf16[8,320,384]{2,1,0:T(8,128)(2,1)S(1)}, u32[]{:S(2)}, u32[]{:S(2)}) async-start(bf16[8,320,384]{2,1,0:T(8,128)(2,1)} %copy-done.6), calls=%async_computation.5 | async-start | bytes 3932160 | tf_op jit(solution)/shard_map/all_to_all | solution.py:342
  195.4 2.6 %collective-permute-done.17 = bf16[8,48,1152]{2,1,0:T(8,128)(2,1)S(1)} collective-permute-done((bf16[8,48,1152]{2,1,0:T(8,128)(2,1)}, bf16[8,48,1152]{2,1,0:T(8,128)(2,1)S(1)}, u32[]{:S(2)}, u32[]{:S(2)}) %collective-permute-start.17) | collective-permute-done | bytes 884768 | tf_op jit(solution)/shard_map/ppermute | solution.py:369
  198.1 12.1 %shard_map.111 = bf16[2560,1152]{1,0:T(8,128)(2,1)} custom-call(bf16[384,2560]{1,0:T(8,128)(2,1)} %constant_dynamic-update-slice_fusion.a_rows_ref, bf16[384,2560]{1,0:T(8,128)(2,1)} %collective-permute-done.16.b_rows_ref, bf16[384,1152]{1,0:T(8,128)(2,1)S(1)} %bitcast.32, bf16[384,1152]{1,0:T(8,128)(2,1)S(1)} %bitcast.34), custom_call_target="tpu_custom_call" | custom-call | flops 4529848320 | bytes 11599872 | tf_op jit(solution)/shard_map/pallas_call | solution.py:330
  210.2 5.0 %all-to-all-done.5.parts_ref = bf16[8,320,384]{2,1,0:T(8,128)(2,1)S(1)} async-done(((bf16[8,320,384]{2,1,0:T(8,128)(2,1)}), bf16[8,320,384]{2,1,0:T(8,128)(2,1)S(1)}, u32[]{:S(2)}, u32[]{:S(2)}) %all-to-all-start.5) | async-done | bytes 1966112 | tf_op jit(solution)/shard_map/all_to_all | solution.py:342
  216.8 5.8 %all-to-all-start.6 = ((bf16[8,48,320]{2,1,0:T(8,128)(2,1)}), bf16[8,48,320]{2,1,0:T(8,128)(2,1)S(1)}, u32[]{:S(2)}, u32[]{:S(2)}) async-start(bf16[8,48,320]{2,1,0:T(8,128)(2,1)} %shard_map.110), calls=%async_computation.6 | async-start | bytes 589824 | tf_op jit(solution)/shard_map/all_to_all | solution.py:342
  224.4 11.0 %all-to-all-done.6 = bf16[8,48,320]{2,1,0:T(8,128)(2,1)S(1)} async-done(((bf16[8,48,320]{2,1,0:T(8,128)(2,1)}), bf16[8,48,320]{2,1,0:T(8,128)(2,1)S(1)}, u32[]{:S(2)}, u32[]{:S(2)}) %all-to-all-start.6) | async-done | bytes 245792 | tf_op jit(solution)/shard_map/all_to_all | solution.py:342
  (163 shorter events, 53.8 us)
Async XLA Ops:
  0.6 84.2 %copy-start = (s32[768]{0:T(1024)S(1)}, s32[768]{0:T(1024)}, u32[]{:S(2)}) copy-start(s32[768]{0:T(1024)} %param.12) | copy-start | bytes 9220
  0.6 41.1 %collective-permute-start.4 = (bf16[2560,1152]{1,0:T(8,128)(2,1)}, bf16[2560,1152]{1,0:T(8,128)(2,1)}, u32[]{:S(2)}, u32[]{:S(2)}) collective-permute-start(bf16[2560,1152]{1,0:T(8,128)(2,1)} %own_ref.1), channel_id=1, source_target_pairs={{0,8},{8,0},{16,24},{24,16},{32,40},{40,32},{48,56},{56,48},{64,72... | collective-permute-start | bytes 17694728 | tf_op jit(solution)/shard_map/ppermute | solution.py:369
  3.0 12.0 %all-to-all-start = ((bf16[8,48,320]{2,1,0:T(8,128)(2,1)}), bf16[8,48,320]{2,1,0:T(8,128)(2,1)S(1)}, u32[]{:S(2)}, u32[]{:S(2)}) async-start(bf16[8,48,320]{2,1,0:T(8,128)(2,1)} %broadcast_in_dim.15), calls=%async_computation | async-start | bytes 589824 | tf_op jit(solution)/shard_map/all_to_all | solution.py:342
  16.9 17.3 %all-to-all-start.1 = ((bf16[24,2,8,1152]{3,1,0,2:T(2,128)(2,1)}), bf16[24,2,8,1152]{3,1,0,2:T(2,128)(2,1)S(1)}, u32[]{:S(2)}, u32[]{:S(2)}) async-start(bf16[24,2,8,1152]{3,1,0,2:T(2,128)(2,1)} %copy.22), calls=%async_computation.1 | async-start | bytes 1769472 | tf_op jit(solution)/shard_map/all_to_all | solution.py:379
  22.6 13.0 %collective-permute-start = (bf16[48,2560]{1,0:T(8,128)(2,1)S(1)}, bf16[48,2560]{1,0:T(8,128)(2,1)S(1)}, u32[]{:S(2)}, u32[]{:S(2)}) collective-permute-start(bf16[48,2560]{1,0:T(8,128)(2,1)S(1)} %reshape.125.refs_0_), channel_id=1, source_target_pairs={{0,16},{8,24},{16,32},{24,40},{32,48},{40,56},{48,64},{56,72},{64,... | collective-permute-start | bytes 737288 | tf_op jit(solution)/shard_map/ppermute | solution.py:396
  24.6 11.0 %collective-permute-start.1 = (bf16[48,2560]{1,0:T(8,128)(2,1)S(1)}, bf16[48,2560]{1,0:T(8,128)(2,1)S(1)}, u32[]{:S(2)}, u32[]{:S(2)}) collective-permute-start(bf16[48,2560]{1,0:T(8,128)(2,1)S(1)} %reshape.125.refs_0_), channel_id=1, source_target_pairs={{0,112},{8,120},{16,0},{24,8},{32,16},{40,24},{48,32},{56,40},{64,... | collective-permute-start | bytes 737288 | tf_op jit(solution)/shard_map/ppermute | solution.py:397
  35.7 16.4 %collective-permute-start.2 = (bf16[48,2560]{1,0:T(8,128)(2,1)S(1)}, bf16[48,2560]{1,0:T(8,128)(2,1)S(1)}, u32[]{:S(2)}, u32[]{:S(2)}) collective-permute-start(bf16[48,2560]{1,0:T(8,128)(2,1)S(1)} %collective-permute-done.refs_2_), channel_id=1, source_target_pairs={{0,16},{8,24},{16,32},{24,40},{32,48},{40,56},{48,64},{56,72},{64,... | collective-permute-start | bytes 737288 | tf_op jit(solution)/shard_map/ppermute | solution.py:396
  37.7 14.4 %collective-permute-start.3 = (bf16[48,2560]{1,0:T(8,128)(2,1)S(1)}, bf16[48,2560]{1,0:T(8,128)(2,1)S(1)}, u32[]{:S(2)}, u32[]{:S(2)}) collective-permute-start(bf16[48,2560]{1,0:T(8,128)(2,1)S(1)} %collective-permute-done.1.refs_1_), channel_id=1, source_target_pairs={{0,112},{8,120},{16,0},{24,8},{32,16},{40,24},{48,32},{56,40},{64,... | collective-permute-start | bytes 737288 | tf_op jit(solution)/shard_map/ppermute | solution.py:397
  50.2 20.3 %collective-permute-start.9 = (f32[3,24,2304]{2,1,0:T(8,128)}, f32[3,24,2304]{2,1,0:T(8,128)}, u32[]{:S(2)}, u32[]{:S(2)}) collective-permute-start(f32[3,24,2304]{2,1,0:T(8,128)} %get-tuple-element.41.refs_0_), channel_id=1, source_target_pairs={{0,128},{128,0},{1,129},{129,1},{2,130},{130,2},{3,131},{131,3},{4... | collective-permute-start | bytes 1990664 | tf_op jit(solution)/shard_map/ppermute | solution.py:391
  52.1 12.3 %collective-permute-start.5 = (bf16[48,2560]{1,0:T(8,128)(2,1)S(1)}, bf16[48,2560]{1,0:T(8,128)(2,1)S(1)}, u32[]{:S(2)}, u32[]{:S(2)}) collective-permute-start(bf16[48,2560]{1,0:T(8,128)(2,1)S(1)} %collective-permute-done.3.refs_0_), channel_id=1, source_target_pairs={{0,112},{8,120},{16,0},{24,8},{32,16},{40,24},{48,32},{56,40},{64,... | collective-permute-start | bytes 737288 | tf_op jit(solution)/shard_map/ppermute | solution.py:397
  54.2 10.1 %collective-permute-start.6 = (bf16[48,2560]{1,0:T(8,128)(2,1)S(1)}, bf16[48,2560]{1,0:T(8,128)(2,1)S(1)}, u32[]{:S(2)}, u32[]{:S(2)}) collective-permute-start(bf16[48,2560]{1,0:T(8,128)(2,1)S(1)} %collective-permute-done.2.refs_1_), channel_id=1, source_target_pairs={{0,16},{8,24},{16,32},{24,40},{32,48},{40,56},{48,64},{56,72},{64,... | collective-permute-start | bytes 737288 | tf_op jit(solution)/shard_map/ppermute | solution.py:396
  61.9 50.2 %copy-start.9 = (f32[2,24,2304]{2,1,0:T(8,128)}, f32[2,24,2304]{2,1,0:T(8,128)S(1)}, u32[]{:S(2)}) copy-start(f32[2,24,2304]{2,1,0:T(8,128)S(1)} %get-tuple-element.38.refs_1_) | copy-start | bytes 1327108
  61.9 15.7 %collective-permute-start.10 = (f32[2,24,2304]{2,1,0:T(8,128)S(1)}, f32[2,24,2304]{2,1,0:T(8,128)S(1)}, u32[]{:S(2)}, u32[]{:S(2)}) collective-permute-start(f32[2,24,2304]{2,1,0:T(8,128)S(1)} %get-tuple-element.46.refs_1_), channel_id=1, source_target_pairs={{0,128},{128,0},{1,129},{129,1},{2,130},{130,2},{3,131},{131,3},{4... | collective-permute-start | bytes 1327112 | tf_op jit(solution)/shard_map/ppermute | solution.py:391
  64.3 6.2 %collective-permute-start.7 = (bf16[48,1280]{1,0:T(8,128)(2,1)S(1)}, bf16[48,1280]{1,0:T(8,128)(2,1)S(1)}, u32[]{:S(2)}, u32[]{:S(2)}) collective-permute-start(bf16[48,1280]{1,0:T(8,128)(2,1)S(1)} %slice.50), channel_id=1, source_target_pairs={{0,16},{8,24},{16,32},{24,40},{32,48},{40,56},{48,64},{56,72},{64,... | collective-permute-start | bytes 368648 | tf_op jit(solution)/shard_map/ppermute | solution.py:406
  64.4 6.0 %collective-permute-start.8 = (bf16[48,1280]{1,0:T(8,128)(2,1)S(1)}, bf16[48,1280]{1,0:T(8,128)(2,1)S(1)}, u32[]{:S(2)}, u32[]{:S(2)}) collective-permute-start(bf16[48,1280]{1,0:T(8,128)(2,1)S(1)} %slice.51), channel_id=1, source_target_pairs={{0,112},{8,120},{16,0},{24,8},{32,16},{40,24},{48,32},{56,40},{64,... | collective-permute-start | bytes 368648 | tf_op jit(solution)/shard_map/ppermute | solution.py:407
  76.3 35.7 %copy-start.4 = (f32[3,24,2304]{2,1,0:T(8,128)}, f32[3,24,2304]{2,1,0:T(8,128)S(1)}, u32[]{:S(2)}) copy-start(f32[3,24,2304]{2,1,0:T(8,128)S(1)} %get-tuple-element.44.refs_2_) | copy-start | bytes 1990660
  78.3 29.0 %all-to-all-start.2 = ((bf16[24,8,2304]{2,0,1:T(8,128)(2,1)}), bf16[24,8,2304]{2,0,1:T(8,128)(2,1)S(1)}, u32[]{:S(2)}, u32[]{:S(2)}) async-start(bf16[24,8,2304]{2,0,1:T(8,128)(2,1)} %reshape.126), calls=%async_computation.2 | async-start | bytes 1769472 | tf_op jit(solution)/shard_map/all_to_all | solution.py:412
  87.7 16.4 %collective-permute-start.11 = (f32[3,24,2304]{2,1,0:T(8,128)}, f32[3,24,2304]{2,1,0:T(8,128)S(1)}, u32[]{:S(2)}, u32[]{:S(2)}) collective-permute-start(f32[3,24,2304]{2,1,0:T(8,128)} %copy-done.18), channel_id=1, source_target_pairs={{0,128},{128,0},{1,129},{129,1},{2,130},{130,2},{3,131},{131,3},{4... | collective-permute-start | bytes 1990664 | tf_op jit(solution)/shard_map/ppermute | solution.py:391
  107.3 20.9 %collective-permute-start.12 = (bf16[192,2304]{1,0:T(8,128)(2,1)S(1)}, bf16[192,2304]{1,0:T(8,128)(2,1)S(1)}, u32[]{:S(2)}, u32[]{:S(2)}) collective-permute-start(bf16[192,2304]{1,0:T(8,128)(2,1)S(1)} %bitcast.28), channel_id=1, source_target_pairs={{0,128},{128,0},{1,129},{129,1},{2,130},{130,2},{3,131},{131,3},{4... | collective-permute-start | bytes 2654216 | tf_op jit(solution)/shard_map/ppermute | solution.py:416
  112.1 19.5 %copy-start.23 = (bf16[48,1280]{1,0:T(8,128)(2,1)S(1)}, bf16[48,1280]{1,0:T(8,128)(2,1)}, u32[]{:S(2)}) copy-start(bf16[48,1280]{1,0:T(8,128)(2,1)} %copy-done.22) | copy-start | bytes 368644
  112.1 19.5 %copy-start.25 = (bf16[48,1280]{1,0:T(8,128)(2,1)S(1)}, bf16[48,1280]{1,0:T(8,128)(2,1)}, u32[]{:S(2)}) copy-start(bf16[48,1280]{1,0:T(8,128)(2,1)} %copy-done.24) | copy-start | bytes 368644
  128.3 41.2 %collective-permute-start.15 = (f32[8,24,2304]{2,1,0:T(8,128)}, f32[8,24,2304]{2,1,0:T(8,128)}, u32[]{:S(2)}, u32[]{:S(2)}) collective-permute-start(f32[8,24,2304]{2,1,0:T(8,128)} %pad_maximum_fusion), channel_id=1, source_target_pairs={{0,128},{128,0},{1,129},{129,1},{2,130},{130,2},{3,131},{131,3},{4... | collective-permute-start | bytes 5308424 | tf_op jit(solution)/shard_map/ppermute | solution.py:457
  130.3 2.8 %collective-permute-start.13 = (bf16[192,2304]{1,0:T(8,128)(2,1)S(1)}, bf16[192,2304]{1,0:T(8,128)(2,1)S(1)}, u32[]{:S(2)}, u32[]{:S(2)}) collective-permute-start(bf16[192,2304]{1,0:T(8,128)(2,1)S(1)} %bitcast.29), channel_id=1, source_target_pairs={{0,8},{8,0},{16,24},{24,16},{32,40},{40,32},{48,56},{56,48},{64,72... | collective-permute-start | bytes 2654216 | tf_op jit(solution)/shard_map/ppermute | solution.py:369
  130.3 3.7 %collective-permute-start.14 = (bf16[192,2304]{1,0:T(8,128)(2,1)S(1)}, bf16[192,2304]{1,0:T(8,128)(2,1)S(1)}, u32[]{:S(2)}, u32[]{:S(2)}) collective-permute-start(bf16[192,2304]{1,0:T(8,128)(2,1)S(1)} %collective-permute-done.12.b_ref), channel_id=1, source_target_pairs={{0,8},{8,0},{16,24},{24,16},{32,40},{40,32},{48,56},{56,48},{64,72... | collective-permute-start | bytes 2654216 | tf_op jit(solution)/shard_map/ppermute | solution.py:369
  133.0 62.4 %collective-permute-start.16 = (bf16[384,2560]{1,0:T(8,128)(2,1)}, bf16[384,2560]{1,0:T(8,128)(2,1)}, u32[]{:S(2)}, u32[]{:S(2)}) collective-permute-start(bf16[384,2560]{1,0:T(8,128)(2,1)} %constant_dynamic-update-slice_fusion.a_rows_ref), channel_id=1, source_target_pairs={{0,8},{8,0},{16,24},{24,16},{32,40},{40,32},{48,56},{56,48},{64,72... | collective-permute-start | bytes 5898248 | tf_op jit(solution)/shard_map/ppermute | solution.py:369
  138.5 30.9 %copy-start.19 = (f32[3,24,2304]{2,1,0:T(8,128)S(1)}, f32[3,24,2304]{2,1,0:T(8,128)}, u32[]{:S(2)}) copy-start(f32[3,24,2304]{2,1,0:T(8,128)} %copy-done.18) | copy-start | bytes 1990660
  143.4 11.7 %all-to-all-start.3 = ((f32[8,8,192]{2,1,0:T(8,128)}), f32[8,8,192]{2,1,0:T(8,128)S(1)}, u32[]{:S(2)}, u32[]{:S(2)}) async-start(f32[8,8,192]{2,1,0:T(8,128)} %get-tuple-element.53), calls=%async_computation.3 | async-start | bytes 131072 | tf_op jit(solution)/shard_map/all_to_all | solution.py:342
  155.8 13.6 %all-to-all-start.4 = ((f32[16,8,192]{2,1,0:T(8,128)}), f32[16,8,192]{2,1,0:T(8,128)S(1)}, u32[]{:S(2)}, u32[]{:S(2)}) async-start(f32[16,8,192]{2,1,0:T(8,128)} %shard_map.107), calls=%async_computation.4 | async-start | bytes 262144 | tf_op jit(solution)/shard_map/all_to_all | solution.py:342
  189.7 25.5 %all-to-all-start.5 = ((bf16[8,320,384]{2,1,0:T(8,128)(2,1)}), bf16[8,320,384]{2,1,0:T(8,128)(2,1)S(1)}, u32[]{:S(2)}, u32[]{:S(2)}) async-start(bf16[8,320,384]{2,1,0:T(8,128)(2,1)} %copy-done.6), calls=%async_computation.5 | async-start | bytes 3932160 | tf_op jit(solution)/shard_map/all_to_all | solution.py:342
  195.4 2.6 %collective-permute-start.17 = (bf16[8,48,1152]{2,1,0:T(8,128)(2,1)}, bf16[8,48,1152]{2,1,0:T(8,128)(2,1)S(1)}, u32[]{:S(2)}, u32[]{:S(2)}) collective-permute-start(bf16[8,48,1152]{2,1,0:T(8,128)(2,1)} %copy-done.31), channel_id=1, source_target_pairs={{0,8},{8,0},{16,24},{24,16},{32,40},{40,32},{48,56},{56,48},{64,72... | collective-permute-start | bytes 2654216 | tf_op jit(solution)/shard_map/ppermute | solution.py:369
  216.8 18.5 %all-to-all-start.6 = ((bf16[8,48,320]{2,1,0:T(8,128)(2,1)}), bf16[8,48,320]{2,1,0:T(8,128)(2,1)S(1)}, u32[]{:S(2)}, u32[]{:S(2)}) async-start(bf16[8,48,320]{2,1,0:T(8,128)(2,1)} %shard_map.110), calls=%async_computation.6 | async-start | bytes 589824 | tf_op jit(solution)/shard_map/all_to_all | solution.py:342
  222.6 1.2 collective-permute-start.18
  (29 other events, 196.5 us)

commit v5 on v4

--- a/solution.py
+++ b/solution.py
@@ -87,7 +87,7 @@
 
 def aligned(order, token, own, swapped):
     lines, columns = own[0].shape
-    tiles = 6 if columns % 768 == 0 else 2
+    tiles = 2
     tile = columns // tiles
     here = pl.BlockSpec((lines, tile), lambda i: (0, i))
     there = pl.BlockSpec((lines, tile), lambda i: (0, lax.rem(i + tiles // 2, tiles)))
@@ -271,7 +271,9 @@
     terms += lax.dot_general(
         partner_ref[...], partner_grad_ref[...], NT, preferred_element_type=F32
     )
-    out_ref[0] = terms.astype(BF16)
+    width = out_ref.shape[1]
+    for i in range(out_ref.shape[0]):
+        out_ref[i] = terms[i * width : (i + 1) * width].astype(BF16)
 
 
 def terms_of(own_grad, partner_grad, own, partner, members):
@@ -279,14 +281,15 @@
     depth = own.shape[0]
     lines = chips * size
     width = depth // members
-    weights = pl.BlockSpec((width, columns), lambda i: (i, 0))
+    group = 2
+    weights = pl.BlockSpec((group * width, columns), lambda i: (i, 0))
     return call(
         terms_kernel,
         4 * lines * columns * depth,
         4 * (lines + depth) * columns + 2 * lines * depth,
-        grid=(members,),
+        grid=(members // group,),
         in_specs=[whole((lines, columns))] * 2 + [weights] * 2,
-        out_specs=pl.BlockSpec((1, width, lines), lambda i: (i, 0, 0)),
+        out_specs=pl.BlockSpec((group, width, lines), lambda i: (i, 0, 0)),
         out_shape=jax.ShapeDtypeStruct((members, width, lines), BF16),
     )(own_grad.reshape(lines, columns), partner_grad.reshape(lines, columns), own, partner)
 

time: 238 us -> 238 us (level)
  waiting for transfers between devices: 78.4 us -> 83.6 us
    all_to_all x5, waiting for transfers between devices: 35.8 us -> 41 us  [exchange(): lax.all_to_all(copies, axis, split_axis=0, concat_axis=0, tiled=True, axi...]
  transfers between devices with their start and end apart: 26 -> 26, of which waited for: 14 -> 14; matrix products, arithmetic and copies ran while one was open for 10% -> 10% of each run, Pallas kernels for 21% -> 20%
where the time goes in v5:
time: 238 us; the launch traced here: 237 us
  waiting for transfers between devices  83.6 us (35%)
  starting transfers between devices  61.5 us (26%)
  Pallas kernels  48.6 us (20%)
  local copies, waits for them, and re-layouts  37.1 us (16%)
  other arithmetic  4.6 us (2%)
    all_to_all x5, waiting for transfers between devices, exchange(): lax.all_to_all(copies, axis, split_axis=0, concat_axis=0, tiled=True, axi...  41 us
    unnamed x77, local copies, waits for them, and re-layouts  25.4 us
    all_to_all x5, starting transfers between devices, exchange(): lax.all_to_all(copies, axis, split_axis=0, concat_axis=0, tiled=True, axi...  24.4 us
    pallas_call x3, Pallas kernels, logits_of(): call(functools.partial(logits_kernel, tuple((len(block) for block in bloc...  15.5 us
    ppermute x1, waiting for transfers between devices, on_device(): teacher_across = lax.ppermute(teacher, 'sec', swap_sec)  14.8 us
    ppermute x3, waiting for transfers between devices, take(): received.append(lax.ppermute(theirs, 'sec', swap_sec))  13.8 us
    pallas_call x1, Pallas kernels, head_grad_of(): call(head_grad_kernel, 4 * lines * depth * columns, 4 * (lines * depth +...  12.1 us
    ppermute x3, starting transfers between devices, on_device(): down = lax.ppermute(down, 'dp', shift(-1))  10.1 us
  transfers between devices with their start and end apart: 26, of which 14 were waited for; matrix products, arithmetic and copies ran while one was open for 10% of the time, Pallas kernels for 20%

profile of v5, /device:TPU:10, one launch (start us, length us, event | category | flops | bytes accessed | tf_op | source)
XLA Modules:
  0.0 236.7 jit_solution(6502699764923304499)
XLA Ops:
  3.0 5.8 %all-to-all-start = ((bf16[8,48,320]{2,1,0:T(8,128)(2,1)}), bf16[8,48,320]{2,1,0:T(8,128)(2,1)S(1)}, u32[]{:S(2)}, u32[]{:S(2)}) async-start(bf16[8,48,320]{2,1,0:T(8,128)(2,1)} %broadcast_in_dim.15), calls=%async_computation | async-start | bytes 589824 | tf_op jit(solution)/shard_map/all_to_all | solution.py:345
  10.8 4.2 %all-to-all-done = bf16[8,48,320]{2,1,0:T(8,128)(2,1)S(1)} async-done(((bf16[8,48,320]{2,1,0:T(8,128)(2,1)}), bf16[8,48,320]{2,1,0:T(8,128)(2,1)S(1)}, u32[]{:S(2)}, u32[]{:S(2)}) %all-to-all-start) | async-done | bytes 245792 | tf_op jit(solution)/shard_map/all_to_all | solution.py:345
  16.9 5.5 %all-to-all-start.1 = ((bf16[24,2,8,1152]{3,1,0,2:T(2,128)(2,1)}), bf16[24,2,8,1152]{3,1,0,2:T(2,128)(2,1)S(1)}, u32[]{:S(2)}, u32[]{:S(2)}) async-start(bf16[24,2,8,1152]{3,1,0,2:T(2,128)(2,1)} %copy.22), calls=%async_computation.1 | async-start | bytes 1769472 | tf_op jit(solution)/shard_map/all_to_all | solution.py:382
  24.6 4.0 %collective-permute-start.1 = (bf16[48,2560]{1,0:T(8,128)(2,1)S(1)}, bf16[48,2560]{1,0:T(8,128)(2,1)S(1)}, u32[]{:S(2)}, u32[]{:S(2)}) collective-permute-start(bf16[48,2560]{1,0:T(8,128)(2,1)S(1)} %reshape.125.refs_0_), channel_id=1, source_target_pairs={{0,112},{8,120},{16,0},{24,8},{32,16},{40,24},{48,32},{56,40},{64,... | collective-permute-start | bytes 737288 | tf_op jit(solution)/shard_map/ppermute | solution.py:400
  30.0 4.2 %all-to-all-done.1 = bf16[24,2,8,1152]{3,1,0,2:T(2,128)(2,1)S(1)} async-done(((bf16[24,2,8,1152]{3,1,0,2:T(2,128)(2,1)}), bf16[24,2,8,1152]{3,1,0,2:T(2,128)(2,1)S(1)}, u32[]{:S(2)}, u32[]{:S(2)}) %all-to-all-start.1) | async-done | bytes 884768 | tf_op jit(solution)/shard_map/all_to_all | solution.py:382
  37.7 4.0 %collective-permute-start.3 = (bf16[48,2560]{1,0:T(8,128)(2,1)S(1)}, bf16[48,2560]{1,0:T(8,128)(2,1)S(1)}, u32[]{:S(2)}, u32[]{:S(2)}) collective-permute-start(bf16[48,2560]{1,0:T(8,128)(2,1)S(1)} %collective-permute-done.1.refs_1_), channel_id=1, source_target_pairs={{0,112},{8,120},{16,0},{24,8},{32,16},{40,24},{48,32},{56,40},{64,... | collective-permute-start | bytes 737288 | tf_op jit(solution)/shard_map/ppermute | solution.py:400
  41.7 2.7 %copy-done.1 = bf16[2560,1152]{1,0:T(8,128)(2,1)S(1)} copy-done((bf16[2560,1152]{1,0:T(8,128)(2,1)S(1)}, bf16[2560,1152]{1,0:T(8,128)(2,1)}, u32[]{:S(2)}) %copy-start.1) | copy-done | bytes 5898264
  44.4 5.8 %shard_map.102 = (f32[3,24,2304]{2,1,0:T(8,128)S(1)}, f32[3,24,2304]{2,1,0:T(8,128)}) custom-call(bf16[48,2560]{1,0:T(8,128)(2,1)S(1)} %reshape.125.refs_0_, bf16[48,2560]{1,0:T(8,128)(2,1)S(1)} %collective-permute-done.1.refs_1_, bf16[48,2560]{1,0:T(8,128)(2,1)S(1)} %collective-permute-done.refs_2_, bf16[2560,1152]{1,0:T(8,128)(2,1)S(1)} %copy-done.1, ...), custom_call_target="tpu_custom_call" | custom-call | flops 1698693120 | bytes 13123584 | tf_op jit(solution)/shard_map/pallas_call | solution.py:63
  54.3 2.7 %copy-done.2 = bf16[2560,1152]{1,0:T(8,128)(2,1)S(1)} copy-done((bf16[2560,1152]{1,0:T(8,128)(2,1)S(1)}, bf16[2560,1152]{1,0:T(8,128)(2,1)}, u32[]{:S(2)}) %copy-start.2) | copy-done | bytes 5898264
  57.0 4.8 %shard_map.103 = (f32[2,24,2304]{2,1,0:T(8,128)S(1)}, f32[2,24,2304]{2,1,0:T(8,128)S(1)}) custom-call(bf16[48,2560]{1,0:T(8,128)(2,1)S(1)} %collective-permute-done.3.refs_0_, bf16[48,2560]{1,0:T(8,128)(2,1)S(1)} %collective-permute-done.2.refs_1_, bf16[2560,1152]{1,0:T(8,128)(2,1)S(1)} %copy-done.2, ...), custom_call_target="tpu_custom_call" | custom-call | flops 1132462080 | bytes 12681216 | tf_op jit(solution)/shard_map/pallas_call | solution.py:63
  61.9 2.4 %collective-permute-start.10 = (f32[2,24,2304]{2,1,0:T(8,128)S(1)}, f32[2,24,2304]{2,1,0:T(8,128)S(1)}, u32[]{:S(2)}, u32[]{:S(2)}) collective-permute-start(f32[2,24,2304]{2,1,0:T(8,128)S(1)} %get-tuple-element.46.refs_1_), channel_id=1, source_target_pairs={{0,128},{128,0},{1,129},{129,1},{2,130},{130,2},{3,131},{131,3},{4... | collective-permute-start | bytes 1327112 | tf_op jit(solution)/shard_map/ppermute | solution.py:394
  64.4 3.3 %collective-permute-start.8 = (bf16[48,1280]{1,0:T(8,128)(2,1)S(1)}, bf16[48,1280]{1,0:T(8,128)(2,1)S(1)}, u32[]{:S(2)}, u32[]{:S(2)}) collective-permute-start(bf16[48,1280]{1,0:T(8,128)(2,1)S(1)} %slice.51), channel_id=1, source_target_pairs={{0,112},{8,120},{16,0},{24,8},{32,16},{40,24},{48,32},{56,40},{64,... | collective-permute-start | bytes 368648 | tf_op jit(solution)/shard_map/ppermute | solution.py:410
  67.8 2.7 %collective-permute-done.7.refs_1_ = bf16[48,1280]{1,0:T(8,128)(2,1)S(1)} collective-permute-done((bf16[48,1280]{1,0:T(8,128)(2,1)S(1)}, bf16[48,1280]{1,0:T(8,128)(2,1)S(1)}, u32[]{:S(2)}, u32[]{:S(2)}) %collective-permute-start.7) | collective-permute-done | bytes 122912 | tf_op jit(solution)/shard_map/ppermute | solution.py:409
  70.5 4.9 %shard_map.104 = (f32[3,24,2304]{2,1,0:T(8,128)S(1)}, f32[3,24,2304]{2,1,0:T(8,128)S(1)}) custom-call(bf16[48,2560]{1,0:T(8,128)(2,1)S(1)} %collective-permute-done.5.refs_0_, bf16[48,1280]{1,0:T(8,128)(2,1)S(1)} %collective-permute-done.7.refs_1_, bf16[48,1280]{1,0:T(8,128)(2,1)S(1)} %collective-permute-done.8.refs_2_, ...), custom_call_target="tpu_custom_call" | custom-call | flops 1698693120 | bytes 13123584 | tf_op jit(solution)/shard_map/pallas_call | solution.py:63
  78.3 5.5 %all-to-all-start.2 = ((bf16[24,8,2304]{2,0,1:T(8,128)(2,1)}), bf16[24,8,2304]{2,0,1:T(8,128)(2,1)S(1)}, u32[]{:S(2)}, u32[]{:S(2)}) async-start(bf16[24,8,2304]{2,0,1:T(8,128)(2,1)} %reshape.126), calls=%async_computation.2 | async-start | bytes 1769472 | tf_op jit(solution)/shard_map/all_to_all | solution.py:415
  91.4 12.6 %collective-permute-done.11.refs_5_ = f32[3,24,2304]{2,1,0:T(8,128)S(1)} collective-permute-done((f32[3,24,2304]{2,1,0:T(8,128)}, f32[3,24,2304]{2,1,0:T(8,128)S(1)}, u32[]{:S(2)}, u32[]{:S(2)}) %collective-permute-start.11) | collective-permute-done | bytes 663584 | tf_op jit(solution)/shard_map/ppermute | solution.py:394
  113.4 14.8 %collective-permute-done.12.b_ref = bf16[192,2304]{1,0:T(8,128)(2,1)S(1)} collective-permute-done((bf16[192,2304]{1,0:T(8,128)(2,1)S(1)}, bf16[192,2304]{1,0:T(8,128)(2,1)S(1)}, u32[]{:S(2)}, u32[]{:S(2)}) %collective-permute-start.12) | collective-permute-done | bytes 884768 | tf_op jit(solution)/shard_map/ppermute | solution.py:419
  134.0 3.1 %shard_map.105 = bf16[384,2304]{1,0:T(8,128)(2,1)S(1)} custom-call(s32[1,768]{1,0:T(1,128)S(1)} %broadcast_in_dim.17.order_ref, s32[384,1]{1,0:T(8,128)S(1)} %reshape.180.token_ref, bf16[192,2304]{1,0:T(8,128)(2,1)S(1)} %bitcast.30, bf16[192,2304]{1,0:T(8,128)(2,1)S(1)} %collective-permute-done.12.b_ref, ...), custom_call_target="tpu_custom_call" | custom-call | flops 1358954496 | bytes 5308416 | tf_op jit(solution)/shard_map/pallas_call | solution.py:95
  137.1 3.7 %shard_map.106 = (f32[8,24,2304]{2,1,0:T(8,128)S(1)}, f32[8,8,192]{2,1,0:T(8,128)}) custom-call(s32[2]{0:T(128)S(1)} %pad_add_fusion.2.z_ref.place_ref, f32[3,24,2304]{2,1,0:T(8,128)S(1)} %get-tuple-element.37.refs_0_, f32[2,24,2304]{2,1,0:T(8,128)S(1)} %copy-done.10, f32[3,24,2304]{2,1,0:T(8,128)S(1)} %copy-done.5, ...), custom_call_target="tpu_custom_call" | custom-call | flops 8847360 | bytes 6193152 | tf_op jit(solution)/shard_map/pallas_call | solution.py:156
  142.0 3.4 %all-to-all-start.3 = ((f32[8,8,192]{2,1,0:T(8,128)}), f32[8,8,192]{2,1,0:T(8,128)S(1)}, u32[]{:S(2)}, u32[]{:S(2)}) async-start(f32[8,8,192]{2,1,0:T(8,128)} %get-tuple-element.53), calls=%async_computation.3 | async-start | bytes 131072 | tf_op jit(solution)/shard_map/all_to_all | solution.py:345
  145.6 8.1 %all-to-all-done.3.table_ref = f32[8,8,192]{2,1,0:T(8,128)S(1)} async-done(((f32[8,8,192]{2,1,0:T(8,128)}), f32[8,8,192]{2,1,0:T(8,128)S(1)}, u32[]{:S(2)}, u32[]{:S(2)}) %all-to-all-start.3) | async-done | bytes 49184 | tf_op jit(solution)/shard_map/all_to_all | solution.py:345
  154.4 6.1 %all-to-all-start.4 = ((f32[16,8,192]{2,1,0:T(8,128)}), f32[16,8,192]{2,1,0:T(8,128)S(1)}, u32[]{:S(2)}, u32[]{:S(2)}) async-start(f32[16,8,192]{2,1,0:T(8,128)} %shard_map.107), calls=%async_computation.4 | async-start | bytes 262144 | tf_op jit(solution)/shard_map/all_to_all | solution.py:345
  160.5 8.9 %all-to-all-done.4.refs_5_ = f32[16,8,192]{2,1,0:T(8,128)S(1)} async-done(((f32[16,8,192]{2,1,0:T(8,128)}), f32[16,8,192]{2,1,0:T(8,128)S(1)}, u32[]{:S(2)}, u32[]{:S(2)}) %all-to-all-start.4) | async-done | bytes 98336 | tf_op jit(solution)/shard_map/all_to_all | solution.py:345
  171.9 3.4 %shard_map.108 = (bf16[8,48,1152]{2,1,0:T(8,128)(2,1)S(1)}, bf16[8,48,1152]{2,1,0:T(8,128)(2,1)S(1)}, f32[2,8,192]{2,1,0:T(8,128)S(1)}) custom-call(s32[2]{0:T(128)S(1)} %pad_add_fusion.2.z_ref.place_ref, f32[8,24,2304]{2,1,0:T(8,128)S(1)} %copy-done.8, f32[3,24,2304]{2,1,0:T(8,128)} %get-tuple-element.41.refs_0_, f32[2,24,2304]{2,1,0:T(8,128)S(1)} %copy-done.27, ...), custom_call_target="tpu_custom_call" | custom-call | flops 8847360 | bytes 8847360 | tf_op jit(solution)/shard_map/pallas_call | solution.py:258
  175.3 2.7 %copy-done.3 = bf16[2560,1152]{1,0:T(8,128)(2,1)S(1)} copy-done((bf16[2560,1152]{1,0:T(8,128)(2,1)S(1)}, bf16[2560,1152]{1,0:T(8,128)(2,1)}, u32[]{:S(2)}) %copy-start.3) | copy-done | bytes 5898264
  178.0 8.6 %shard_map.109 = bf16[8,320,384]{2,1,0:T(8,128)(2,1)S(1)} custom-call(bf16[384,1152]{1,0:T(8,128)(2,1)S(1)} %bitcast.31, bf16[384,1152]{1,0:T(8,128)(2,1)S(1)} %bitcast.33, bf16[2560,1152]{1,0:T(8,128)(2,1)S(1)} %copy-done.3, bf16[2560,1152]{1,0:T(8,128)(2,1)} %collective-permute-done.4.refs_4_.refs_3_.refs_5_.partner_ref), custom_call_target="tpu_custom_call" | custom-call | flops 4529848320 | bytes 15532032 | tf_op jit(solution)/shard_map/pallas_call | solution.py:286
  188.8 5.7 %all-to-all-start.5 = ((bf16[8,320,384]{2,1,0:T(8,128)(2,1)}), bf16[8,320,384]{2,1,0:T(8,128)(2,1)S(1)}, u32[]{:S(2)}, u32[]{:S(2)}) async-start(bf16[8,320,384]{2,1,0:T(8,128)(2,1)} %copy-done.6), calls=%async_computation.5 | async-start | bytes 3932160 | tf_op jit(solution)/shard_map/all_to_all | solution.py:345
  194.5 2.6 %collective-permute-done.17 = bf16[8,48,1152]{2,1,0:T(8,128)(2,1)S(1)} collective-permute-done((bf16[8,48,1152]{2,1,0:T(8,128)(2,1)}, bf16[8,48,1152]{2,1,0:T(8,128)(2,1)S(1)}, u32[]{:S(2)}, u32[]{:S(2)}) %collective-permute-start.17) | collective-permute-done | bytes 884768 | tf_op jit(solution)/shard_map/ppermute | solution.py:372
  197.2 12.1 %shard_map.111 = bf16[2560,1152]{1,0:T(8,128)(2,1)} custom-call(bf16[384,2560]{1,0:T(8,128)(2,1)} %constant_dynamic-update-slice_fusion.a_rows_ref, bf16[384,2560]{1,0:T(8,128)(2,1)} %collective-permute-done.16.b_rows_ref, bf16[384,1152]{1,0:T(8,128)(2,1)S(1)} %bitcast.32, bf16[384,1152]{1,0:T(8,128)(2,1)S(1)} %bitcast.34), custom_call_target="tpu_custom_call" | custom-call | flops 4529848320 | bytes 11599872 | tf_op jit(solution)/shard_map/pallas_call | solution.py:333
  209.3 8.7 %all-to-all-done.5.parts_ref = bf16[8,320,384]{2,1,0:T(8,128)(2,1)S(1)} async-done(((bf16[8,320,384]{2,1,0:T(8,128)(2,1)}), bf16[8,320,384]{2,1,0:T(8,128)(2,1)S(1)}, u32[]{:S(2)}, u32[]{:S(2)}) %all-to-all-start.5) | async-done | bytes 1966112 | tf_op jit(solution)/shard_map/all_to_all | solution.py:345
  219.6 3.4 %all-to-all-start.6 = ((bf16[8,48,320]{2,1,0:T(8,128)(2,1)}), bf16[8,48,320]{2,1,0:T(8,128)(2,1)S(1)}, u32[]{:S(2)}, u32[]{:S(2)}) async-start(bf16[8,48,320]{2,1,0:T(8,128)(2,1)} %shard_map.110), calls=%async_computation.6 | async-start | bytes 589824 | tf_op jit(solution)/shard_map/all_to_all | solution.py:345
  224.9 11.1 %all-to-all-done.6 = bf16[8,48,320]{2,1,0:T(8,128)(2,1)S(1)} async-done(((bf16[8,48,320]{2,1,0:T(8,128)(2,1)}), bf16[8,48,320]{2,1,0:T(8,128)(2,1)S(1)}, u32[]{:S(2)}, u32[]{:S(2)}) %all-to-all-start.6) | async-done | bytes 245792 | tf_op jit(solution)/shard_map/all_to_all | solution.py:345
  (163 shorter events, 53.9 us)
Async XLA Ops:
  0.6 84.2 %copy-start = (s32[768]{0:T(1024)S(1)}, s32[768]{0:T(1024)}, u32[]{:S(2)}) copy-start(s32[768]{0:T(1024)} %param.12) | copy-start | bytes 9220
  0.6 41.1 %collective-permute-start.4 = (bf16[2560,1152]{1,0:T(8,128)(2,1)}, bf16[2560,1152]{1,0:T(8,128)(2,1)}, u32[]{:S(2)}, u32[]{:S(2)}) collective-permute-start(bf16[2560,1152]{1,0:T(8,128)(2,1)} %own_ref.1), channel_id=1, source_target_pairs={{0,8},{8,0},{16,24},{24,16},{32,40},{40,32},{48,56},{56,48},{64,72... | collective-permute-start | bytes 17694728 | tf_op jit(solution)/shard_map/ppermute | solution.py:372
  3.0 12.0 %all-to-all-start = ((bf16[8,48,320]{2,1,0:T(8,128)(2,1)}), bf16[8,48,320]{2,1,0:T(8,128)(2,1)S(1)}, u32[]{:S(2)}, u32[]{:S(2)}) async-start(bf16[8,48,320]{2,1,0:T(8,128)(2,1)} %broadcast_in_dim.15), calls=%async_computation | async-start | bytes 589824 | tf_op jit(solution)/shard_map/all_to_all | solution.py:345
  16.9 17.3 %all-to-all-start.1 = ((bf16[24,2,8,1152]{3,1,0,2:T(2,128)(2,1)}), bf16[24,2,8,1152]{3,1,0,2:T(2,128)(2,1)S(1)}, u32[]{:S(2)}, u32[]{:S(2)}) async-start(bf16[24,2,8,1152]{3,1,0,2:T(2,128)(2,1)} %copy.22), calls=%async_computation.1 | async-start | bytes 1769472 | tf_op jit(solution)/shard_map/all_to_all | solution.py:382
  22.6 13.0 %collective-permute-start = (bf16[48,2560]{1,0:T(8,128)(2,1)S(1)}, bf16[48,2560]{1,0:T(8,128)(2,1)S(1)}, u32[]{:S(2)}, u32[]{:S(2)}) collective-permute-start(bf16[48,2560]{1,0:T(8,128)(2,1)S(1)} %reshape.125.refs_0_), channel_id=1, source_target_pairs={{0,16},{8,24},{16,32},{24,40},{32,48},{40,56},{48,64},{56,72},{64,... | collective-permute-start | bytes 737288 | tf_op jit(solution)/shard_map/ppermute | solution.py:399
  24.6 11.0 %collective-permute-start.1 = (bf16[48,2560]{1,0:T(8,128)(2,1)S(1)}, bf16[48,2560]{1,0:T(8,128)(2,1)S(1)}, u32[]{:S(2)}, u32[]{:S(2)}) collective-permute-start(bf16[48,2560]{1,0:T(8,128)(2,1)S(1)} %reshape.125.refs_0_), channel_id=1, source_target_pairs={{0,112},{8,120},{16,0},{24,8},{32,16},{40,24},{48,32},{56,40},{64,... | collective-permute-start | bytes 737288 | tf_op jit(solution)/shard_map/ppermute | solution.py:400
  35.7 16.4 %collective-permute-start.2 = (bf16[48,2560]{1,0:T(8,128)(2,1)S(1)}, bf16[48,2560]{1,0:T(8,128)(2,1)S(1)}, u32[]{:S(2)}, u32[]{:S(2)}) collective-permute-start(bf16[48,2560]{1,0:T(8,128)(2,1)S(1)} %collective-permute-done.refs_2_), channel_id=1, source_target_pairs={{0,16},{8,24},{16,32},{24,40},{32,48},{40,56},{48,64},{56,72},{64,... | collective-permute-start | bytes 737288 | tf_op jit(solution)/shard_map/ppermute | solution.py:399
  37.7 14.4 %collective-permute-start.3 = (bf16[48,2560]{1,0:T(8,128)(2,1)S(1)}, bf16[48,2560]{1,0:T(8,128)(2,1)S(1)}, u32[]{:S(2)}, u32[]{:S(2)}) collective-permute-start(bf16[48,2560]{1,0:T(8,128)(2,1)S(1)} %collective-permute-done.1.refs_1_), channel_id=1, source_target_pairs={{0,112},{8,120},{16,0},{24,8},{32,16},{40,24},{48,32},{56,40},{64,... | collective-permute-start | bytes 737288 | tf_op jit(solution)/shard_map/ppermute | solution.py:400
  50.2 20.3 %collective-permute-start.9 = (f32[3,24,2304]{2,1,0:T(8,128)}, f32[3,24,2304]{2,1,0:T(8,128)}, u32[]{:S(2)}, u32[]{:S(2)}) collective-permute-start(f32[3,24,2304]{2,1,0:T(8,128)} %get-tuple-element.41.refs_0_), channel_id=1, source_target_pairs={{0,128},{128,0},{1,129},{129,1},{2,130},{130,2},{3,131},{131,3},{4... | collective-permute-start | bytes 1990664 | tf_op jit(solution)/shard_map/ppermute | solution.py:394
  52.1 12.3 %collective-permute-start.5 = (bf16[48,2560]{1,0:T(8,128)(2,1)S(1)}, bf16[48,2560]{1,0:T(8,128)(2,1)S(1)}, u32[]{:S(2)}, u32[]{:S(2)}) collective-permute-start(bf16[48,2560]{1,0:T(8,128)(2,1)S(1)} %collective-permute-done.3.refs_0_), channel_id=1, source_target_pairs={{0,112},{8,120},{16,0},{24,8},{32,16},{40,24},{48,32},{56,40},{64,... | collective-permute-start | bytes 737288 | tf_op jit(solution)/shard_map/ppermute | solution.py:400
  54.2 10.1 %collective-permute-start.6 = (bf16[48,2560]{1,0:T(8,128)(2,1)S(1)}, bf16[48,2560]{1,0:T(8,128)(2,1)S(1)}, u32[]{:S(2)}, u32[]{:S(2)}) collective-permute-start(bf16[48,2560]{1,0:T(8,128)(2,1)S(1)} %collective-permute-done.2.refs_1_), channel_id=1, source_target_pairs={{0,16},{8,24},{16,32},{24,40},{32,48},{40,56},{48,64},{56,72},{64,... | collective-permute-start | bytes 737288 | tf_op jit(solution)/shard_map/ppermute | solution.py:399
  61.9 50.2 %copy-start.9 = (f32[2,24,2304]{2,1,0:T(8,128)}, f32[2,24,2304]{2,1,0:T(8,128)S(1)}, u32[]{:S(2)}) copy-start(f32[2,24,2304]{2,1,0:T(8,128)S(1)} %get-tuple-element.38.refs_1_) | copy-start | bytes 1327108
  61.9 15.7 %collective-permute-start.10 = (f32[2,24,2304]{2,1,0:T(8,128)S(1)}, f32[2,24,2304]{2,1,0:T(8,128)S(1)}, u32[]{:S(2)}, u32[]{:S(2)}) collective-permute-start(f32[2,24,2304]{2,1,0:T(8,128)S(1)} %get-tuple-element.46.refs_1_), channel_id=1, source_target_pairs={{0,128},{128,0},{1,129},{129,1},{2,130},{130,2},{3,131},{131,3},{4... | collective-permute-start | bytes 1327112 | tf_op jit(solution)/shard_map/ppermute | solution.py:394
  64.3 6.2 %collective-permute-start.7 = (bf16[48,1280]{1,0:T(8,128)(2,1)S(1)}, bf16[48,1280]{1,0:T(8,128)(2,1)S(1)}, u32[]{:S(2)}, u32[]{:S(2)}) collective-permute-start(bf16[48,1280]{1,0:T(8,128)(2,1)S(1)} %slice.50), channel_id=1, source_target_pairs={{0,16},{8,24},{16,32},{24,40},{32,48},{40,56},{48,64},{56,72},{64,... | collective-permute-start | bytes 368648 | tf_op jit(solution)/shard_map/ppermute | solution.py:409
  64.4 6.0 %collective-permute-start.8 = (bf16[48,1280]{1,0:T(8,128)(2,1)S(1)}, bf16[48,1280]{1,0:T(8,128)(2,1)S(1)}, u32[]{:S(2)}, u32[]{:S(2)}) collective-permute-start(bf16[48,1280]{1,0:T(8,128)(2,1)S(1)} %slice.51), channel_id=1, source_target_pairs={{0,112},{8,120},{16,0},{24,8},{32,16},{40,24},{48,32},{56,40},{64,... | collective-permute-start | bytes 368648 | tf_op jit(solution)/shard_map/ppermute | solution.py:410
  76.3 35.7 %copy-start.4 = (f32[3,24,2304]{2,1,0:T(8,128)}, f32[3,24,2304]{2,1,0:T(8,128)S(1)}, u32[]{:S(2)}) copy-start(f32[3,24,2304]{2,1,0:T(8,128)S(1)} %get-tuple-element.44.refs_2_) | copy-start | bytes 1990660
  78.3 29.0 %all-to-all-start.2 = ((bf16[24,8,2304]{2,0,1:T(8,128)(2,1)}), bf16[24,8,2304]{2,0,1:T(8,128)(2,1)S(1)}, u32[]{:S(2)}, u32[]{:S(2)}) async-start(bf16[24,8,2304]{2,0,1:T(8,128)(2,1)} %reshape.126), calls=%async_computation.2 | async-start | bytes 1769472 | tf_op jit(solution)/shard_map/all_to_all | solution.py:415
  87.7 16.4 %collective-permute-start.11 = (f32[3,24,2304]{2,1,0:T(8,128)}, f32[3,24,2304]{2,1,0:T(8,128)S(1)}, u32[]{:S(2)}, u32[]{:S(2)}) collective-permute-start(f32[3,24,2304]{2,1,0:T(8,128)} %copy-done.18), channel_id=1, source_target_pairs={{0,128},{128,0},{1,129},{129,1},{2,130},{130,2},{3,131},{131,3},{4... | collective-permute-start | bytes 1990664 | tf_op jit(solution)/shard_map/ppermute | solution.py:394
  107.3 20.9 %collective-permute-start.12 = (bf16[192,2304]{1,0:T(8,128)(2,1)S(1)}, bf16[192,2304]{1,0:T(8,128)(2,1)S(1)}, u32[]{:S(2)}, u32[]{:S(2)}) collective-permute-start(bf16[192,2304]{1,0:T(8,128)(2,1)S(1)} %bitcast.28), channel_id=1, source_target_pairs={{0,128},{128,0},{1,129},{129,1},{2,130},{130,2},{3,131},{131,3},{4... | collective-permute-start | bytes 2654216 | tf_op jit(solution)/shard_map/ppermute | solution.py:419
  112.1 19.5 %copy-start.23 = (bf16[48,1280]{1,0:T(8,128)(2,1)S(1)}, bf16[48,1280]{1,0:T(8,128)(2,1)}, u32[]{:S(2)}) copy-start(bf16[48,1280]{1,0:T(8,128)(2,1)} %copy-done.22) | copy-start | bytes 368644
  112.1 19.5 %copy-start.25 = (bf16[48,1280]{1,0:T(8,128)(2,1)S(1)}, bf16[48,1280]{1,0:T(8,128)(2,1)}, u32[]{:S(2)}) copy-start(bf16[48,1280]{1,0:T(8,128)(2,1)} %copy-done.24) | copy-start | bytes 368644
  128.3 41.2 %collective-permute-start.15 = (f32[8,24,2304]{2,1,0:T(8,128)}, f32[8,24,2304]{2,1,0:T(8,128)}, u32[]{:S(2)}, u32[]{:S(2)}) collective-permute-start(f32[8,24,2304]{2,1,0:T(8,128)} %pad_maximum_fusion), channel_id=1, source_target_pairs={{0,128},{128,0},{1,129},{129,1},{2,130},{130,2},{3,131},{131,3},{4... | collective-permute-start | bytes 5308424 | tf_op jit(solution)/shard_map/ppermute | solution.py:460
  130.3 2.8 %collective-permute-start.13 = (bf16[192,2304]{1,0:T(8,128)(2,1)S(1)}, bf16[192,2304]{1,0:T(8,128)(2,1)S(1)}, u32[]{:S(2)}, u32[]{:S(2)}) collective-permute-start(bf16[192,2304]{1,0:T(8,128)(2,1)S(1)} %bitcast.29), channel_id=1, source_target_pairs={{0,8},{8,0},{16,24},{24,16},{32,40},{40,32},{48,56},{56,48},{64,72... | collective-permute-start | bytes 2654216 | tf_op jit(solution)/shard_map/ppermute | solution.py:372
  130.3 3.7 %collective-permute-start.14 = (bf16[192,2304]{1,0:T(8,128)(2,1)S(1)}, bf16[192,2304]{1,0:T(8,128)(2,1)S(1)}, u32[]{:S(2)}, u32[]{:S(2)}) collective-permute-start(bf16[192,2304]{1,0:T(8,128)(2,1)S(1)} %collective-permute-done.12.b_ref), channel_id=1, source_target_pairs={{0,8},{8,0},{16,24},{24,16},{32,40},{40,32},{48,56},{56,48},{64,72... | collective-permute-start | bytes 2654216 | tf_op jit(solution)/shard_map/ppermute | solution.py:372
  133.0 61.5 %collective-permute-start.16 = (bf16[384,2560]{1,0:T(8,128)(2,1)}, bf16[384,2560]{1,0:T(8,128)(2,1)}, u32[]{:S(2)}, u32[]{:S(2)}) collective-permute-start(bf16[384,2560]{1,0:T(8,128)(2,1)} %constant_dynamic-update-slice_fusion.a_rows_ref), channel_id=1, source_target_pairs={{0,8},{8,0},{16,24},{24,16},{32,40},{40,32},{48,56},{56,48},{64,72... | collective-permute-start | bytes 5898248 | tf_op jit(solution)/shard_map/ppermute | solution.py:372
  137.1 32.3 %copy-start.19 = (f32[3,24,2304]{2,1,0:T(8,128)S(1)}, f32[3,24,2304]{2,1,0:T(8,128)}, u32[]{:S(2)}) copy-start(f32[3,24,2304]{2,1,0:T(8,128)} %copy-done.18) | copy-start | bytes 1990660
  142.0 11.7 %all-to-all-start.3 = ((f32[8,8,192]{2,1,0:T(8,128)}), f32[8,8,192]{2,1,0:T(8,128)S(1)}, u32[]{:S(2)}, u32[]{:S(2)}) async-start(f32[8,8,192]{2,1,0:T(8,128)} %get-tuple-element.53), calls=%async_computation.3 | async-start | bytes 131072 | tf_op jit(solution)/shard_map/all_to_all | solution.py:345
  154.4 15.0 %all-to-all-start.4 = ((f32[16,8,192]{2,1,0:T(8,128)}), f32[16,8,192]{2,1,0:T(8,128)S(1)}, u32[]{:S(2)}, u32[]{:S(2)}) async-start(f32[16,8,192]{2,1,0:T(8,128)} %shard_map.107), calls=%async_computation.4 | async-start | bytes 262144 | tf_op jit(solution)/shard_map/all_to_all | solution.py:345
  188.8 29.2 %all-to-all-start.5 = ((bf16[8,320,384]{2,1,0:T(8,128)(2,1)}), bf16[8,320,384]{2,1,0:T(8,128)(2,1)S(1)}, u32[]{:S(2)}, u32[]{:S(2)}) async-start(bf16[8,320,384]{2,1,0:T(8,128)(2,1)} %copy-done.6), calls=%async_computation.5 | async-start | bytes 3932160 | tf_op jit(solution)/shard_map/all_to_all | solution.py:345
  194.5 2.6 %collective-permute-start.17 = (bf16[8,48,1152]{2,1,0:T(8,128)(2,1)}, bf16[8,48,1152]{2,1,0:T(8,128)(2,1)S(1)}, u32[]{:S(2)}, u32[]{:S(2)}) collective-permute-start(bf16[8,48,1152]{2,1,0:T(8,128)(2,1)} %copy-done.31), channel_id=1, source_target_pairs={{0,8},{8,0},{16,24},{24,16},{32,40},{40,32},{48,56},{56,48},{64,72... | collective-permute-start | bytes 2654216 | tf_op jit(solution)/shard_map/ppermute | solution.py:372
  219.6 16.4 %all-to-all-start.6 = ((bf16[8,48,320]{2,1,0:T(8,128)(2,1)}), bf16[8,48,320]{2,1,0:T(8,128)(2,1)S(1)}, u32[]{:S(2)}, u32[]{:S(2)}) async-start(bf16[8,48,320]{2,1,0:T(8,128)(2,1)} %shard_map.110), calls=%async_computation.6 | async-start | bytes 589824 | tf_op jit(solution)/shard_map/all_to_all | solution.py:345
  223.0 1.3 collective-permute-start.18
  (29 other events, 189.4 us)
